TPU v7x, 256 devices: a whole 4x4x8 slice. The times are simulated.
256 devices in a mesh: section: 2 (over z_lo), shard: 64 (over y, x, z_hi), rep: 2 (over core).
Axes of the slice: x: 4, y: 4, z: 8 (z_hi: 4, z_lo: 2; z = z_hi * 2 + z_lo), core: 2. Of those that a mesh axis runs over, the one named last changes fastest.
Arguments:
- acts: bfloat16 [2, 2, 1536, 4608], P('section', 'rep', 'shard'), may hold values from -6 to 6
- logit_grad: bfloat16 [2, 1536, 24576], P('rep', None, 'shard'), may hold values from -0.109375 to 0.109375
- token_ids: int32 [2, 1536], P('rep'), may hold values from 0 to 255999
- table: float32 [24576, 4608], P(('shard', 'section', 'rep')), may hold values from -4 to 4
- moment_one: float32 [24576, 4608], P(('shard', 'section', 'rep')), may hold values from -3 to 3
- moment_two: float32 [24576, 4608], P(('shard', 'section', 'rep')), may hold values from 0.05 to 2
Outputs:
- new_table: float32 [24576, 4608], P(('shard', 'section', 'rep'))
- new_moment_one: float32 [24576, 4608], P(('shard', 'section', 'rep'))
- new_moment_two: float32 [24576, 4608], P(('shard', 'section', 'rep'))
All inputs are finite; a program needn't handle non-finite values.
Results may differ from a plain program's by a relative error of at most 0.0003.
Values may be sent and summed in bfloat16 or wider, within the bound.
No kernel may reach another device: no remote copies, remote signals or barrier semaphores. Data moves between devices by JAX's collectives and lax.ppermute only.
A program may use at most 128 MiB of HBM per device.

v0:
```python
import jax
import jax.numpy as jnp
from jax import lax
from jax.sharding import PartitionSpec as P

corr_first = 1.0 - 0.9**10
corr_second = 1.0 - 0.95**10


def adamw_rows(gradient, table, moment_one, moment_two):
    new_one = 0.9 * moment_one + 0.1 * gradient
    new_two = 0.95 * moment_two + 0.05 * gradient * gradient
    update = new_one / corr_first / (jnp.sqrt(new_two / corr_second) + 1e-08)
    new_table = table - 0.01 * (update + 0.1 * table)
    return (new_table, new_one, new_two)


def local(acts, logit_grad, token_ids, table, moment_one, moment_two):
    section_idx = lax.axis_index("section")
    shard_idx = lax.axis_index("shard")
    reps = lax.axis_size("rep")
    sections = lax.axis_size("section")
    local_acts = acts[0, 0]
    grad_rows = logit_grad[0]
    id_rows = token_ids[0]
    voc_shard = grad_rows.shape[1]
    quarter = voc_shard // (sections * reps)
    vocab_cols = shard_idx * voc_shard + lax.broadcasted_iota(jnp.int32, (1, voc_shard), 1)
    one_hot = (id_rows[:, None] == vocab_cols).astype(jnp.bfloat16)
    coefficient = jnp.where(section_idx == 0, one_hot, grad_rows)
    fold_input = (local_acts,)
    folded = lax.dot_general(
        coefficient,
        (lax.all_gather(fold_input[0], "shard", axis=0, tiled=True),)[0],
        (((0,), (0,)), ((), ())),
        preferred_element_type=jnp.float32,
    )
    summed = lax.psum(folded, "rep")
    half_sum = lax.psum_scatter(summed, "section", scatter_dimension=0, tiled=True)
    gradient = lax.dynamic_slice_in_dim(half_sum, lax.axis_index("rep") * quarter, quarter, 0)
    return adamw_rows(gradient, table, moment_one, moment_two)


def solution(mesh):
    placed = (
        P("section", "rep", "shard", None),
        P("rep", None, "shard"),
        P("rep", None),
        P(("shard", "section", "rep"), None),
        P(("shard", "section", "rep"), None),
        P(("shard", "section", "rep"), None),
    )
    return jax.shard_map(
        local,
        mesh=mesh,
        in_specs=placed,
        out_specs=(
            P(("shard", "section", "rep"), None),
            P(("shard", "section", "rep"), None),
            P(("shard", "section", "rep"), None),
        ),
        check_vma=False,
    )
```

profile of v0, /device:TPU:1, one launch (start us, length us, event | category | flops | bytes accessed | tf_op | source)
XLA Modules:
  0.0 317.9 jit_solution(1310148859726157315)
XLA Ops:
  7.2 0.0 all-gather.3.cloned.1.call-start
  7.2 0.7 all-gather.3.cloned.1.call-update
  7.9 0.0 reduce-scatter.2.cloned.1.call-start
  8.0 0.7 reduce
  8.7 146.5 %all-gather.3.cloned.1.call-done = bf16[1,1,1536,4608]{3,2,1,0:T(8,128)(2,1)} async-done(((bf16[1,1,24,4608]{3,2,1,0:T(8,128)(2,1)}), bf16[1,1,1536,4608]{3,2,1,0:T(8,128)(2,1)}) %all-gather.3.cloned.1.call-update) | async-done | bytes 14155792 | tf_op jit(solution)/shard_map/all_gather | solution.py:34
  155.2 11.3 %fusion = f32[384,4608]{1,0:T(8,128)} fusion(bf16[1,1,1536,4608]{3,2,1,0:T(8,128)(2,1)} %all-gather.3.cloned.1.call-done, bf16[1,1536,384]{2,1,0:T(8,128)(2,1)} %param.7, s32[384]{0:T(512)S(1)} %iota_add_fusion, s32[1536]{0:T(1024)S(1)} %reduce, pred[]{:T(512)S(6)} %eq.18), kind=kOutput, calls=%fused_computation | convolution fusion | flops 5437587456 | bytes 22420992 | tf_op jit(solution)/shard_map/dot_general | solution.py:32
  166.4 0.0 reduce-scatter.2.cloned.1.call-update
  166.5 0.0 all-reduce.2.cloned.1.call-start
  166.5 100.9 %reduce-scatter.2.cloned.1.call-done = f32[192,4608]{1,0:T(8,128)} async-done(((f32[384,4608]{1,0:T(8,128)}), f32[192,4608]{1,0:T(8,128)}) %reduce-scatter.2.cloned.1.call-update) | async-done | bytes 3538960 | tf_op jit(solution)/shard_map/reduce_scatter | solution.py:39
  267.4 0.0 copy-start
  267.4 0.0 copy-start.1
  267.4 0.0 all-reduce.2.cloned.1.call-update
  267.4 38.7 %all-reduce.2.cloned.1.call-done = f32[192,4608]{1,0:T(8,128)} async-done(((f32[192,4608]{1,0:T(8,128)}), f32[192,4608]{1,0:T(8,128)}) %all-reduce.2.cloned.1.call-update) | async-done | bytes 3538960 | tf_op jit(solution)/shard_map/psum | solution.py:38
  306.1 0.0 copy-done
  306.1 0.0 copy-done.1
  306.1 5.3 %multiply_subtract_fusion = (f32[96,4608]{1,0:T(8,128)}, f32[96,4608]{1,0:T(8,128)}, f32[96,4608]{1,0:T(8,128)}) fusion(f32[96,4608]{1,0:T(8,128)S(1)} %copy-done, f32[192,4608]{1,0:T(8,128)} %all-reduce.2.cloned.1.call-done, s32[]{:T(128)S(6)} %select_n.13, f32[96,4608]{1,0:T(8,128)S(1)} %copy-done.1, f32[96,4608]{1,0:T(8,128)} %param.11), kind=kLoop, calls=%fused_computation.5 | loop fusion | flops 6635520 | bytes 12386308 | tf_op jit(solution)/shard_map/sub | solution.py:14
  (1 shorter events, 0.0 us)
Async XLA Ops:
  7.2 148.0 %all-gather.3.cloned.1.call-start = ((), (), s32[]{:S(2)}) async-start(), calls=%async_computation.1 | async-start | bytes 14376960 | tf_op jit(solution)/shard_map/all_gather | solution.py:34
  7.9 259.5 %reduce-scatter.2.cloned.1.call-start = ((), (), s32[]{:S(2)}) async-start(), calls=%async_computation.2 | async-start | bytes 10616832 | tf_op jit(solution)/shard_map/reduce_scatter | solution.py:39
  166.5 139.6 %all-reduce.2.cloned.1.call-start = ((), (), s32[]{:S(2)}) async-start(), calls=%async_computation.3 | async-start | bytes 7077888 | tf_op jit(solution)/shard_map/psum | solution.py:38
  267.4 38.7 %copy-start = (f32[96,4608]{1,0:T(8,128)S(1)}, f32[96,4608]{1,0:T(8,128)}, u32[]{:S(2)}) copy-start(f32[96,4608]{1,0:T(8,128)} %param.9) | copy-start | bytes 5308420
  267.4 38.7 %copy-start.1 = (f32[96,4608]{1,0:T(8,128)S(1)}, f32[96,4608]{1,0:T(8,128)}, u32[]{:S(2)}) copy-start(f32[96,4608]{1,0:T(8,128)} %param.10) | copy-start | bytes 5308420
Sparse Core Ops, SparseCore 0:
  11.3 143.8 all-gather.2
  166.6 100.7 reduce-scatter.1
  270.2 35.8 all-reduce.1
where the time goes:
time: 318 us
  waiting for transfers between devices  287 us (90%)
  between operations  13.8 us (4%)
  matrix products  11.3 us (4%)
  other arithmetic  5.99 us (2%)
    all_gather x1, waiting for transfers between devices, local(): lax.all_gather(fold_input[0], 'shard', axis=0, tiled=True)  146 us
    reduce_scatter x1, waiting for transfers between devices, local(): lax.psum_scatter(summed, 'section', scatter_dimension=0, tiled=True)  101 us
    psum x1, waiting for transfers between devices, local(): summed = lax.psum(folded, 'rep')  38.7 us
    dot_general x1, matrix products, local(): lax.dot_general(coefficient, (lax.all_gather(fold_input[0], 'shard', axis...  11.3 us
  transfers between devices with their start and end apart: 3, of which 3 were waited for; matrix products, arithmetic and copies ran while one was open for 0% of the time, Pallas kernels for 0%

commit v1 on v0

v1 whole, which is shorter than its diff:
```python
import functools

import jax
import jax.numpy as jnp
from jax import lax
from jax.experimental import pallas as pl
from jax.experimental.pallas import tpu as pltpu
from jax.sharding import PartitionSpec as P

corr_first = 1.0 - 0.9**10
corr_second = 1.0 - 0.95**10

AXES = ("section", "shard", "rep")
RING = 4
CAP_CHUNK = 16
CAP_ROUTE = 16
SUBS = ((0, 9),)
LANE = 128


def index_of(section, y, x, z_hi, rep):
    return (section * 64 + (y * RING + x) * RING + z_hi) * 2 + rep


def pairs(move):
    out = []
    for section in range(2):
        for y in range(RING):
            for x in range(RING):
                for z_hi in range(RING):
                    for rep in range(2):
                        out.append((index_of(section, y, x, z_hi, rep), index_of(*move(section, y, x, z_hi, rep))))
    return out


def quad_pairs(a, b):
    return pairs(lambda s, y, x, z, r: (s ^ a, y, x, z, r ^ b))


def depth_pairs(step):
    return pairs(lambda s, y, x, z, r: (s, y, x, (z + step) % RING, r))


def second_pairs(step):
    return pairs(lambda s, y, x, z, r: (s, (y + step * r) % RING, (x + step * (1 - r)) % RING, z, r))


def last_pairs(step):
    return pairs(lambda s, y, x, z, r: (s, (y + step * (1 - r)) % RING, (x + step * r) % RING, z, r))


def send(array, table):
    return lax.ppermute(array, AXES, table)


def pick(mask, first, second):
    return jnp.where(mask, first, second)


def roll_to(array, shift, axis):
    size = array.shape[axis]
    head = lax.slice_in_dim(array, 0, size - 1, axis=axis)
    return lax.dynamic_slice_in_dim(jnp.concatenate([array, head], axis), shift, size, axis)


def slots_of(mask, cap):
    size = mask.shape[-1]
    upto = lax.broadcasted_iota(jnp.int32, (size, size), 0) <= lax.broadcasted_iota(jnp.int32, (size, size), 1)
    counts = mask.astype(jnp.int32)
    rank = jnp.sum(counts[..., :, None] * upto.astype(jnp.int32), axis=-2) - 1
    places = lax.broadcasted_iota(jnp.int32, (cap, 1), 0)
    return jnp.logical_and(rank[..., None, :] == places, mask[..., None, :])


def adamw_kernel(where_ref, g_ref, t_ref, m_ref, v_ref, *rest):
    t_out, m_out, v_out = rest[-3:]
    g = g_ref[...]
    new_one = 0.9 * m_ref[...] + 0.1 * g
    new_two = 0.95 * v_ref[...] + 0.05 * g * g
    update = new_one / corr_first / (jnp.sqrt(new_two / corr_second) + 1e-08)
    t = t_ref[...]
    t_out[...] = t - 0.01 * (update + 0.1 * t)
    m_out[...] = new_one
    v_out[...] = new_two


def adamw_part(where, g, table, one, two, previous, step):
    rows, width = g.shape
    wide = pl.BlockSpec((rows, step), lambda i, where_ref: (0, where_ref[0] + i))
    specs = [pl.BlockSpec((rows, step), lambda i, where_ref: (0, i)), wide, wide, wide]
    args = [g, table, one, two]
    aliases = {}
    if previous is not None:
        specs += [pl.BlockSpec(memory_space=pl.ANY)] * 3
        args += list(previous)
        aliases = {5: 0, 6: 1, 7: 2}
    return pl.pallas_call(
        adamw_kernel,
        grid_spec=pltpu.PrefetchScalarGridSpec(
            num_scalar_prefetch=1, grid=(width // step,), in_specs=specs, out_specs=[wide] * 3
        ),
        out_shape=[jax.ShapeDtypeStruct(table.shape, jnp.float32)] * 3,
        input_output_aliases=aliases,
        cost_estimate=pl.CostEstimate(flops=16 * rows * width, bytes_accessed=28 * rows * width, transcendentals=rows * width),
        compiler_params=pltpu.CompilerParams(vmem_limit_bytes=16 * 1024 * 1024),
    )(where, *args)


def dot_rows(weights, rows):
    return lax.dot_general(weights, rows, (((0,), (0,)), ((), ())), preferred_element_type=jnp.float32)


def full_embedding(acts, own_ids, section, shard, quarter, voc, width):
    tokens = acts.shape[0]
    step = pairs(lambda s, y, x, z, r: (s, (y + (x + (z + 1) // RING) // RING) % RING, (x + (z + 1) // RING) % RING, (z + 1) % RING, r))
    rows = shard * voc + lax.broadcasted_iota(jnp.int32, (1, voc), 1)

    def body(i, state):
        current, total = state
        source = lax.rem(shard - i + 64, 64)
        ids = lax.dynamic_slice_in_dim(own_ids, source * tokens, tokens, 0)
        hot = jnp.logical_and(ids[:, None] == rows, section == 0).astype(jnp.bfloat16)
        return send(current, step), total + dot_rows(hot, current)

    total = lax.fori_loop(0, 64, body, (acts, jnp.zeros((voc, acts.shape[1]), jnp.float32)))[1]
    total = total + send(total, quad_pairs(0, 1))
    total = total + send(total, quad_pairs(1, 0))
    return lax.dynamic_slice_in_dim(total, quarter * width, width, 1)


def local(acts, logit_grad, token_ids, table, moment_one, moment_two):
    section = lax.axis_index("section")
    shard = lax.axis_index("shard")
    rep = lax.axis_index("rep")
    y, x, z_hi = shard // 16, lax.rem(shard // 4, 4), lax.rem(shard, 4)
    on_first = rep == 0
    second, last = pick(on_first, x, y), pick(on_first, y, x)
    quarter = 2 * section + rep

    own_acts = acts[0, 0]
    own_logits = logit_grad[0]
    own_ids = token_ids[0]
    tokens, model = own_acts.shape
    voc = own_logits.shape[1]
    width = model // 4
    part = voc // 4

    pieces = {}
    for a, b in ((1, 0), (1, 1), (0, 1), (0, 0)):
        block = lax.dynamic_slice_in_dim(own_acts, (2 * (section ^ a) + (rep ^ b)) * width, width, 1)
        pieces[a, b] = send(block, quad_pairs(a, b)) if (a, b) != (0, 0) else block

    def from_device(s, r):
        flip = rep != r
        same = jnp.where(flip, pieces[0, 1], pieces[0, 0])
        other = jnp.where(flip, pieces[1, 1], pieces[1, 0])
        return jnp.where(section == s, same, other)

    hidden = jnp.concatenate([from_device(1, 0), from_device(1, 1)], 0)
    cotangent = jnp.concatenate([from_device(0, 0), from_device(0, 1)], 0)

    other_ids = send(own_ids, quad_pairs(0, 1))
    other_logits = send(own_logits, quad_pairs(0, 1))

    ids = jnp.stack([pick(on_first, own_ids, other_ids), pick(on_first, other_ids, own_ids)])
    ids = ids.reshape(2, 64, tokens).transpose(1, 0, 2).reshape(64, 2 * tokens)
    hit = jnp.logical_and(ids >= 0, ids < voc * 64)
    chunk_hot = slots_of(hit, CAP_CHUNK)
    chunk_ids = jnp.sum(jnp.where(chunk_hot, ids[:, None, :] + 1, 0), -1) - 1
    column_ids = chunk_ids.reshape(16, 4 * CAP_CHUNK)
    column_shard = jnp.where(column_ids >= 0, column_ids // voc, -1)
    targets = lax.broadcasted_iota(jnp.int32, (1, 4, 1), 1)
    live = column_shard[:, None, :] >= 0
    to_x = jnp.logical_and(lax.rem(column_shard[:, None, :] // 4, 4) == targets, live)
    to_y = jnp.logical_and(column_shard[:, None, :] // 16 == targets, live)
    to_second = pick(on_first, to_x, to_y)
    route_hot = slots_of(to_second, CAP_ROUTE)
    route_ids = jnp.sum(jnp.where(route_hot, column_ids[:, None, None, :] + 1, 0), -1) - 1
    overflow = jnp.logical_or(
        jnp.max(jnp.sum(hit.astype(jnp.int32), -1)) > CAP_CHUNK,
        jnp.logical_or(
            jnp.max(jnp.sum(to_x.astype(jnp.int32), -1)) > CAP_ROUTE,
            jnp.max(jnp.sum(to_y.astype(jnp.int32), -1)) > CAP_ROUTE,
        ),
    )

    mine = lax.dynamic_index_in_dim(route_ids, second, 1, keepdims=False).reshape(4, 4, CAP_ROUTE)
    mine = pick(on_first, mine, mine.swapaxes(0, 1))
    mine = roll_to(mine, second, 1)
    mine = jnp.where(overflow, -1, mine)
    vocab = shard * voc + lax.broadcasted_iota(jnp.int32, (1, 1, 1, voc), 3)
    slot_weights = (mine[..., None] == vocab).astype(jnp.bfloat16)

    group = 4 * tokens
    first_logits = pick(on_first, own_logits, other_logits).reshape(4, 4, group, voc)
    other_half = pick(on_first, other_logits, own_logits).reshape(4, 4, group, voc)

    def weights_of(offset):
        index = lax.rem(last + offset, 4)

        def rows_of(array):
            return pick(
                on_first,
                lax.dynamic_index_in_dim(array, index, 0, keepdims=False),
                lax.dynamic_index_in_dim(array, index, 1, keepdims=False),
            )

        hot = lax.dynamic_index_in_dim(slot_weights, index, 0, keepdims=False)
        both = jnp.concatenate([rows_of(first_logits), rows_of(other_half)], 1)
        return jnp.concatenate([roll_to(both, second, 0), hot], 1).reshape(-1, voc)

    weights = [weights_of(offset) for offset in range(4)]

    own_hot = lax.dynamic_index_in_dim(chunk_hot, shard, 0, keepdims=False).astype(jnp.bfloat16)
    own_route = lax.dynamic_index_in_dim(route_hot, y * 4 + x, 0, keepdims=False)
    own_route = roll_to(own_route, second, 0).astype(jnp.bfloat16).reshape(4 * CAP_ROUTE, 4 * CAP_CHUNK)

    start_total = lax.cond(
        overflow,
        lambda: full_embedding(own_acts, own_ids, section, shard, quarter, voc, width),
        lambda: jnp.zeros((voc, width), jnp.float32),
    )

    results = None
    for block_from, blocks in SUBS:
        low, wide = block_from * LANE, blocks * LANE
        here = lax.slice_in_dim(hidden, low, low + wide, axis=1)
        there = lax.slice_in_dim(cotangent, low, low + wide, axis=1)
        kept = jnp.dot(own_hot, there, preferred_element_type=jnp.float32).astype(jnp.bfloat16)
        chunk = jnp.concatenate([here, kept], 0)

        up, down, far = (send(chunk, depth_pairs(step)) for step in (1, -1, 2))
        column = jnp.stack([chunk, down, far, up])
        column = roll_to(column, lax.rem(4 - z_hi, 4), 0)
        spoken = column[:, : 2 * tokens].reshape(4, 2, tokens, wide).transpose(1, 0, 2, 3).reshape(8 * tokens, wide)
        kept = column[:, 2 * tokens :].reshape(4 * CAP_CHUNK, wide)

        routed = jnp.dot(own_route, kept, preferred_element_type=jnp.float32).astype(jnp.bfloat16)
        outgoing = [jnp.concatenate([spoken, routed[k * CAP_ROUTE : (k + 1) * CAP_ROUTE]], 0) for k in range(4)]
        up = send(outgoing[1], second_pairs(1))
        down = send(outgoing[3], second_pairs(-1))
        far = send(outgoing[2], second_pairs(2))
        plane = jnp.concatenate([outgoing[0], down, far, up], 0)

        half = plane.shape[0] // 2
        lower, upper = plane[:half], plane[half:]
        before_lower = send(lower, last_pairs(1))
        after_upper = send(upper, last_pairs(-1))
        before_upper = send(upper, last_pairs(1))
        after_lower = send(lower, last_pairs(-1))
        far_lower = send(before_lower, last_pairs(1))
        far_upper = send(after_upper, last_pairs(-1))
        total = lax.slice_in_dim(start_total, low, low + wide, axis=1) + dot_rows(weights[0], plane)
        for offset, first, block in (
            (3, True, before_lower),
            (1, False, after_upper),
            (3, False, before_upper),
            (1, True, after_lower),
            (2, True, far_lower),
            (2, False, far_upper),
        ):
            chosen = weights[offset][:half] if first else weights[offset][half:]
            total = total + dot_rows(chosen, block)

        for a, b in ((0, 0), (0, 1), (1, 0), (1, 1)):
            block = lax.dynamic_slice_in_dim(total, (2 * (section ^ a) + (rep ^ b)) * part, part, 0)
            if (a, b) != (0, 0):
                block = send(block, quad_pairs(a, b))
            step = wide if wide == width else LANE
            place = (2 * (section ^ a) + (rep ^ b)) * (width // step) + low // step
            results = adamw_part(
                place.reshape(1).astype(jnp.int32), block, table, moment_one, moment_two, results, step
            )
    return tuple(results)


def solution(mesh):
    rows = P(("shard", "section", "rep"), None)
    return jax.shard_map(
        local,
        mesh=mesh,
        in_specs=(P("section", "rep", "shard", None), P("rep", None, "shard"), P("rep", None), rows, rows, rows),
        out_specs=(rows, rows, rows),
        check_vma=False,
    )
```

time: 318 us -> 124 us (0.39)
  waiting for transfers between devices: 287 us -> 56.7 us
  starting transfers between devices: 0.12 us -> 29.2 us
  between operations: 13.8 us -> 3.12 us
  other arithmetic: 5.99 us -> 14.5 us
  local copies, waits for them, and re-layouts: 0.01 us -> 7.07 us
  Pallas kernels: 0 us -> 4.99 us
  matrix products: 11.3 us -> 7.67 us
    all_gather x1 -> x0, waiting for transfers between devices: 146 us -> none  [local(): lax.all_gather(fold_input[0], 'shard', axis=0, tiled=True)]
    reduce_scatter x1 -> x0, waiting for transfers between devices: 101 us -> none  [local(): lax.psum_scatter(summed, 'section', scatter_dimension=0, tiled=True)]
    ppermute x0 -> x20, waiting for transfers between devices: none -> 56.7 us  [send(): return lax.ppermute(array, AXES, table)]
    psum x1 -> x0, waiting for transfers between devices: 38.7 us -> none  [local(): summed = lax.psum(folded, 'rep')]
    ppermute x0 -> x20, starting transfers between devices: none -> 29.2 us  [send(): return lax.ppermute(array, AXES, table)]
    concatenate x0 -> x12, other arithmetic: none -> 5.54 us  [the longest x5 4 us: roll_to(): jnp.concatenate([array, head], axis)]
    sub x1 -> x3, other arithmetic: 5.28 us -> 0.03 us  [the longest x1 0.02 us: local(): jnp.sum(jnp.where(route_hot, column_ids[:, None, None, :] + 1, 0), -1) - 1]
    unnamed x4 -> x17, local copies, waits for them, and re-layouts: 0.01 us -> 5.13 us
  transfers between devices with their start and end apart: 3 -> 20, of which waited for: 3 -> 10; matrix products, arithmetic and copies ran while one was open for 0% -> 22% of each run, Pallas kernels for 0% -> 3%
where the time goes in v1:
time: 124 us
  waiting for transfers between devices  56.7 us (46%)
  starting transfers between devices  29.2 us (24%)
  other arithmetic  14.5 us (12%)
  matrix products  7.67 us (6%)
  local copies, waits for them, and re-layouts  7.07 us (6%)
  Pallas kernels  4.99 us (4%)
  between operations  3.12 us (3%)
    ppermute x20, waiting for transfers between devices, send(): return lax.ppermute(array, AXES, table)  56.7 us
    ppermute x20, starting transfers between devices, send(): return lax.ppermute(array, AXES, table)  29.2 us
    dot_general x7, matrix products, dot_rows(): lax.dot_general(weights, rows, (((0,), (0,)), ((), ())), preferred_elemen...  7.36 us
    unnamed x17, local copies, waits for them, and re-layouts  5.13 us
    pallas_call x4, Pallas kernels, adamw_part(): pl.pallas_call(adamw_kernel, grid_spec=pltpu.PrefetchScalarGridSpec(num_s...  4.99 us
    concatenate x5, other arithmetic, roll_to(): jnp.concatenate([array, head], axis)  4 us
  transfers between devices with their start and end apart: 20, of which 10 were waited for; matrix products, arithmetic and copies ran while one was open for 22% of the time, Pallas kernels for 3%

profile of v1, /device:TPU:1, one launch (start us, length us, event | category | flops | bytes accessed | tf_op | source)
XLA Modules:
  0.0 123.6 jit_solution(1983589078495438335)
XLA Ops:
  2.3 3.3 %collective-permute-start.3 = (s32[1536]{0:T(1024)S(1)}, s32[1536]{0:T(1024)S(1)}, u32[]{:S(2)}, u32[]{:S(2)}) collective-permute-start(s32[1536]{0:T(1024)S(1)} %reduce.3), channel_id=1, source_target_pairs={{0,1},{1,0},{2,3},{3,2},{4,5},{5,4},{6,7},{7,6},{8,9},{9,8},{10,11... | collective-permute-start | bytes 18440 | tf_op jit(solution)/shard_map/ppermute | solution.py:53
  5.8 2.0 %collective-permute-start.6 = (bf16[24,1152]{1,0:T(8,128)(2,1)S(1)}, bf16[24,1152]{1,0:T(8,128)(2,1)S(1)}, u32[]{:S(2)}, u32[]{:S(2)}) collective-permute-start(bf16[24,1152]{1,0:T(8,128)(2,1)S(1)} %get-tuple-element.290), channel_id=1, source_target_pairs={{0,129},{1,128},{2,131},{3,130},{4,133},{5,132},{6,135},{7,134},{8... | collective-permute-start | bytes 165896 | tf_op jit(solution)/shard_map/ppermute | solution.py:53
  9.2 1.2 select_reduce_fusion.1
  11.3 1.2 select_reduce_fusion
  13.2 5.3 %collective-permute-start.9 = (bf16[64,1152]{1,0:T(8,128)(2,1)S(1)}, bf16[64,1152]{1,0:T(8,128)(2,1)S(1)}, u32[]{:S(2)}, u32[]{:S(2)}) collective-permute-start(bf16[64,1152]{1,0:T(8,128)(2,1)S(1)} %pad_maximum_fusion.8), channel_id=1, source_target_pairs={{0,4},{1,5},{2,6},{3,7},{4,0},{5,1},{6,2},{7,3},{8,12},{9,13},{10,... | collective-permute-start | bytes 442376 | tf_op jit(solution)/shard_map/ppermute | solution.py:53
  18.4 2.4 %collective-permute-start.10 = (bf16[64,1152]{1,0:T(8,128)(2,1)S(1)}, bf16[64,1152]{1,0:T(8,128)(2,1)S(1)}, u32[]{:S(2)}, u32[]{:S(2)}) collective-permute-start(bf16[64,1152]{1,0:T(8,128)(2,1)S(1)} %pad_maximum_fusion.8), channel_id=1, source_target_pairs={{0,2},{1,3},{2,4},{3,5},{4,6},{5,7},{6,0},{7,1},{8,10},{9,11},{10,... | collective-permute-start | bytes 442376 | tf_op jit(solution)/shard_map/ppermute | solution.py:53
  20.8 11.9 %collective-permute-done.8 = bf16[64,1152]{1,0:T(8,128)(2,1)S(1)} collective-permute-done((bf16[64,1152]{1,0:T(8,128)(2,1)S(1)}, bf16[64,1152]{1,0:T(8,128)(2,1)S(1)}, u32[]{:S(2)}, u32[]{:S(2)}) %collective-permute-start.8) | collective-permute-done | bytes 147488 | tf_op jit(solution)/shard_map/ppermute | solution.py:53
  34.5 1.2 pad_maximum_fusion.2
  35.7 2.7 %collective-permute-start.11 = (bf16[208,1152]{1,0:T(8,128)(2,1)}, bf16[208,1152]{1,0:T(8,128)(2,1)S(1)}, u32[]{:S(2)}, u32[]{:S(2)}) collective-permute-start(bf16[208,1152]{1,0:T(8,128)(2,1)} %get-tuple-element.281), channel_id=1, source_target_pairs={{0,24},{1,97},{2,26},{3,99},{4,28},{5,101},{6,30},{7,103},{8,0},{9... | collective-permute-start | bytes 1437704 | tf_op jit(solution)/shard_map/ppermute | solution.py:53
  45.3 7.1 %collective-permute-done.12 = bf16[208,1152]{1,0:T(8,128)(2,1)} collective-permute-done((bf16[208,1152]{1,0:T(8,128)(2,1)}, bf16[208,1152]{1,0:T(8,128)(2,1)}, u32[]{:S(2)}, u32[]{:S(2)}) %collective-permute-start.12) | collective-permute-done | bytes 479264 | tf_op jit(solution)/shard_map/ppermute | solution.py:53
  52.4 1.9 %constant_dynamic-update-slice_fusion.1 = (bf16[832,1152]{1,0:T(8,128)(2,1)}, bf16[416,1152]{1,0:T(8,128)(2,1)S(1)}) fusion(bf16[832,1152]{1,0:T(8,128)(2,1)} %constant_dynamic-update-slice_fusion.2, bf16[208,1152]{1,0:T(8,128)(2,1)} %collective-permute-done.12), kind=kLoop, calls=%fused_computation.122 | loop fusion | bytes 1437696
  54.3 3.1 %collective-permute-done.13 = bf16[208,1152]{1,0:T(8,128)(2,1)S(1)} collective-permute-done((bf16[208,1152]{1,0:T(8,128)(2,1)}, bf16[208,1152]{1,0:T(8,128)(2,1)S(1)}, u32[]{:S(2)}, u32[]{:S(2)}) %collective-permute-start.13) | collective-permute-done | bytes 479264 | tf_op jit(solution)/shard_map/ppermute | solution.py:53
  59.1 1.8 %collective-permute-start.15 = (bf16[416,1152]{1,0:T(8,128)(2,1)S(1)}, bf16[416,1152]{1,0:T(8,128)(2,1)S(1)}, u32[]{:S(2)}, u32[]{:S(2)}) collective-permute-start(bf16[416,1152]{1,0:T(8,128)(2,1)S(1)} %get-tuple-element.278), channel_id=1, source_target_pairs={{0,96},{1,25},{2,98},{3,27},{4,100},{5,29},{6,102},{7,31},{8,104},... | collective-permute-start | bytes 2875400 | tf_op jit(solution)/shard_map/ppermute | solution.py:53
  61.0 1.1 collective-permute-start.17
  62.5 1.5 %broadcast_select_fusion = (bf16[1536,384]{1,0:T(8,128)(2,1)S(1)}, bf16[1536,384]{1,0:T(8,128)(2,1)S(1)}) fusion(bf16[1536,384]{1,0:T(8,128)(2,1)} %collective-permute-done.4, pred[]{:T(512)S(6)} %eq.146, bf16[1,1536,384]{2,1,0:T(8,128)(2,1)S(1)} %copy-done.3), kind=kLoop, calls=%fused_computation.20 | loop fusion | flops 1179648 | bytes 4718593 | tf_op jit(solution)/shard_map/jit(_where)/select_n | solution.py:57
  64.4 1.0 fusion.19
  65.4 1.0 fusion.17
  66.4 1.0 fusion.15
  68.6 3.5 %collective-permute-done.15 = bf16[416,1152]{1,0:T(8,128)(2,1)S(1)} collective-permute-done((bf16[416,1152]{1,0:T(8,128)(2,1)S(1)}, bf16[416,1152]{1,0:T(8,128)(2,1)S(1)}, u32[]{:S(2)}, u32[]{:S(2)}) %collective-permute-start.15) | collective-permute-done | bytes 958496 | tf_op jit(solution)/shard_map/ppermute | solution.py:53
  72.1 3.0 %collective-permute-start.19 = (bf16[416,1152]{1,0:T(8,128)(2,1)S(1)}, bf16[416,1152]{1,0:T(8,128)(2,1)S(1)}, u32[]{:S(2)}, u32[]{:S(2)}) collective-permute-start(bf16[416,1152]{1,0:T(8,128)(2,1)S(1)} %collective-permute-done.15), channel_id=1, source_target_pairs={{0,96},{1,25},{2,98},{3,27},{4,100},{5,29},{6,102},{7,31},{8,104},... | collective-permute-start | bytes 2875400 | tf_op jit(solution)/shard_map/ppermute | solution.py:53
  75.1 7.6 %collective-permute-done.14 = bf16[416,1152]{1,0:T(8,128)(2,1)S(1)} collective-permute-done((bf16[416,1152]{1,0:T(8,128)(2,1)S(1)}, bf16[416,1152]{1,0:T(8,128)(2,1)S(1)}, u32[]{:S(2)}, u32[]{:S(2)}) %collective-permute-start.14) | collective-permute-done | bytes 958496 | tf_op jit(solution)/shard_map/ppermute | solution.py:53
  85.5 3.1 %fusion.11 = f32[384,1152]{1,0:T(8,128)S(1)} fusion(f32[384,1152]{1,0:T(8,128)S(1)} %fusion.57, f32[384,1152]{1,0:T(8,128)S(1)} %fusion.56, f32[384,1152]{1,0:T(8,128)S(1)} %fusion.55, f32[384,1152]{1,0:T(8,128)S(1)} %fusion.54, f32[384,1152]{1,0:T(8,128)S(1)} %get-tuple-element.391, bf16[832,384]{1,0:T(8,128)(2,1)S(1)} %bitcast.134, ...), kind=kOutput, calls=%fused_computation.15 | convolution fusion | flops 738312192 | bytes 13172736 | tf_op jit(solution)/shard_map/dot_general | solution.py:110
  88.6 4.0 %collective-permute-done.19 = bf16[416,1152]{1,0:T(8,128)(2,1)S(1)} collective-permute-done((bf16[416,1152]{1,0:T(8,128)(2,1)S(1)}, bf16[416,1152]{1,0:T(8,128)(2,1)S(1)}, u32[]{:S(2)}, u32[]{:S(2)}) %collective-permute-start.19) | collective-permute-done | bytes 958496 | tf_op jit(solution)/shard_map/ppermute | solution.py:53
  93.4 3.5 %collective-permute-done.18 = bf16[416,1152]{1,0:T(8,128)(2,1)S(1)} collective-permute-done((bf16[416,1152]{1,0:T(8,128)(2,1)S(1)}, bf16[416,1152]{1,0:T(8,128)(2,1)S(1)}, u32[]{:S(2)}, u32[]{:S(2)}) %collective-permute-start.18) | collective-permute-done | bytes 958496 | tf_op jit(solution)/shard_map/ppermute | solution.py:53
  97.8 3.2 %collective-permute-start.22 = (f32[96,1152]{1,0:T(8,128)S(1)}, f32[96,1152]{1,0:T(8,128)S(1)}, u32[]{:S(2)}, u32[]{:S(2)}) collective-permute-start(f32[96,1152]{1,0:T(8,128)S(1)} %get-tuple-element.260), channel_id=1, source_target_pairs={{0,1},{1,0},{2,3},{3,2},{4,5},{5,4},{6,7},{7,6},{8,9},{9,8},{10,11... | collective-permute-start | bytes 1327112 | tf_op jit(solution)/shard_map/ppermute | solution.py:53
  101.4 1.3 %collective-permute-start.20 = (f32[96,1152]{1,0:T(8,128)S(1)}, f32[96,1152]{1,0:T(8,128)S(1)}, u32[]{:S(2)}, u32[]{:S(2)}) collective-permute-start(f32[96,1152]{1,0:T(8,128)S(1)} %get-tuple-element.262), channel_id=1, source_target_pairs={{0,129},{1,128},{2,131},{3,130},{4,133},{5,132},{6,135},{7,134},{8... | collective-permute-start | bytes 1327112 | tf_op jit(solution)/shard_map/ppermute | solution.py:53
  102.7 1.3 %shard_map.85 = (f32[96,4608]{1,0:T(8,128)}, f32[96,4608]{1,0:T(8,128)}, f32[96,4608]{1,0:T(8,128)}) custom-call(s32[1]{0:T(128)} %bitcast.57.where_ref, f32[96,1152]{1,0:T(8,128)S(1)} %get-tuple-element.259.g_ref, f32[96,4608]{1,0:T(8,128)S(1)} %copy-done, f32[96,4608]{1,0:T(8,128)S(1)} %copy-done.1, f32[96,4608]{1,0:T(8,128)S(1)} %copy-done.2), custom_call_target="tpu_custom_call" | custom-call | flops 1769472 | bytes 3096576 | tf_op jit(solution)/shard_map/pallas_call | solution.py:97
  103.9 1.2 %shard_map.86 = (f32[96,4608]{1,0:T(8,128)}, f32[96,4608]{1,0:T(8,128)}, f32[96,4608]{1,0:T(8,128)}) custom-call(s32[1]{0:T(128)} %bitcast.56.where_ref, f32[96,1152]{1,0:T(8,128)S(1)} %collective-permute-done.22.g_ref, f32[96,4608]{1,0:T(8,128)S(1)} %copy-done, ...), custom_call_target="tpu_custom_call", output_to_operand_aliasing={{0}: (5, {}), {1}: (6, {}), {2}: (7, {})} | custom-call | flops 1769472 | bytes 3096576 | tf_op jit(solution)/shard_map/pallas_call | solution.py:97
  105.2 7.5 %collective-permute-done.21.g_ref = f32[96,1152]{1,0:T(8,128)S(1)} collective-permute-done((f32[96,1152]{1,0:T(8,128)S(1)}, f32[96,1152]{1,0:T(8,128)S(1)}, u32[]{:S(2)}, u32[]{:S(2)}) %collective-permute-start.21) | collective-permute-done | bytes 442400 | tf_op jit(solution)/shard_map/ppermute | solution.py:53
  112.7 1.3 %shard_map.87 = (f32[96,4608]{1,0:T(8,128)}, f32[96,4608]{1,0:T(8,128)}, f32[96,4608]{1,0:T(8,128)}) custom-call(s32[1]{0:T(128)} %bitcast.55.where_ref, f32[96,1152]{1,0:T(8,128)S(1)} %collective-permute-done.21.g_ref, f32[96,4608]{1,0:T(8,128)S(1)} %copy-done, ...), custom_call_target="tpu_custom_call", output_to_operand_aliasing={{0}: (5, {}), {1}: (6, {}), {2}: (7, {})} | custom-call | flops 1769472 | bytes 3096576 | tf_op jit(solution)/shard_map/pallas_call | solution.py:97
  113.9 8.4 %collective-permute-done.20.g_ref = f32[96,1152]{1,0:T(8,128)S(1)} collective-permute-done((f32[96,1152]{1,0:T(8,128)S(1)}, f32[96,1152]{1,0:T(8,128)S(1)}, u32[]{:S(2)}, u32[]{:S(2)}) %collective-permute-start.20) | collective-permute-done | bytes 442400 | tf_op jit(solution)/shard_map/ppermute | solution.py:53
  122.3 1.3 %shard_map.88 = (f32[96,4608]{1,0:T(8,128)}, f32[96,4608]{1,0:T(8,128)}, f32[96,4608]{1,0:T(8,128)}) custom-call(s32[1]{0:T(128)} %bitcast.1.where_ref, f32[96,1152]{1,0:T(8,128)S(1)} %collective-permute-done.20.g_ref, f32[96,4608]{1,0:T(8,128)S(1)} %copy-done, f32[96,4608]{1,0:T(8,128)S(1)} %copy-done.1, ...), custom_call_target="tpu_custom_call", output_to_operand_aliasing={{0}: (5, {}), {1}: (6, {}), {2}: (7, {})} | custom-call | flops 1769472 | bytes 3096576 | tf_op jit(solution)/shard_map/pallas_call | solution.py:97
  (103 shorter events, 20.1 us)
Async XLA Ops:
  2.3 5.8 %collective-permute-start.3 = (s32[1536]{0:T(1024)S(1)}, s32[1536]{0:T(1024)S(1)}, u32[]{:S(2)}, u32[]{:S(2)}) collective-permute-start(s32[1536]{0:T(1024)S(1)} %reduce.3), channel_id=1, source_target_pairs={{0,1},{1,0},{2,3},{3,2},{4,5},{5,4},{6,7},{7,6},{8,9},{9,8},{10,11... | collective-permute-start | bytes 18440 | tf_op jit(solution)/shard_map/ppermute | solution.py:53
  5.6 7.3 %collective-permute-start.5 = (bf16[24,1152]{1,0:T(8,128)(2,1)S(1)}, bf16[24,1152]{1,0:T(8,128)(2,1)S(1)}, u32[]{:S(2)}, u32[]{:S(2)}) collective-permute-start(bf16[24,1152]{1,0:T(8,128)(2,1)S(1)} %get-tuple-element.288), channel_id=1, source_target_pairs={{0,1},{1,0},{2,3},{3,2},{4,5},{5,4},{6,7},{7,6},{8,9},{9,8},{10,11... | collective-permute-start | bytes 165896 | tf_op jit(solution)/shard_map/ppermute | solution.py:53
  5.8 7.1 %collective-permute-start.7 = (bf16[24,1152]{1,0:T(8,128)(2,1)S(1)}, bf16[24,1152]{1,0:T(8,128)(2,1)S(1)}, u32[]{:S(2)}, u32[]{:S(2)}) collective-permute-start(bf16[24,1152]{1,0:T(8,128)(2,1)S(1)} %get-tuple-element.289), channel_id=1, source_target_pairs={{0,128},{1,129},{2,130},{3,131},{4,132},{5,133},{6,134},{7,135},{8... | collective-permute-start | bytes 165896 | tf_op jit(solution)/shard_map/ppermute | solution.py:53
  5.8 7.1 %collective-permute-start.6 = (bf16[24,1152]{1,0:T(8,128)(2,1)S(1)}, bf16[24,1152]{1,0:T(8,128)(2,1)S(1)}, u32[]{:S(2)}, u32[]{:S(2)}) collective-permute-start(bf16[24,1152]{1,0:T(8,128)(2,1)S(1)} %get-tuple-element.290), channel_id=1, source_target_pairs={{0,129},{1,128},{2,131},{3,130},{4,133},{5,132},{6,135},{7,134},{8... | collective-permute-start | bytes 165896 | tf_op jit(solution)/shard_map/ppermute | solution.py:53
  7.9 54.7 %collective-permute-start.4 = (bf16[1536,384]{1,0:T(8,128)(2,1)}, bf16[1536,384]{1,0:T(8,128)(2,1)}, u32[]{:S(2)}, u32[]{:S(2)}) collective-permute-start(bf16[1536,384]{1,0:T(8,128)(2,1)} %bitcast.142), channel_id=1, source_target_pairs={{0,1},{1,0},{2,3},{3,2},{4,5},{5,4},{6,7},{7,6},{8,9},{9,8},{10,11... | collective-permute-start | bytes 3538952 | tf_op jit(solution)/shard_map/ppermute | solution.py:53
  13.2 19.5 %collective-permute-start.9 = (bf16[64,1152]{1,0:T(8,128)(2,1)S(1)}, bf16[64,1152]{1,0:T(8,128)(2,1)S(1)}, u32[]{:S(2)}, u32[]{:S(2)}) collective-permute-start(bf16[64,1152]{1,0:T(8,128)(2,1)S(1)} %pad_maximum_fusion.8), channel_id=1, source_target_pairs={{0,4},{1,5},{2,6},{3,7},{4,0},{5,1},{6,2},{7,3},{8,12},{9,13},{10,... | collective-permute-start | bytes 442376 | tf_op jit(solution)/shard_map/ppermute | solution.py:53
  18.4 14.2 %collective-permute-start.8 = (bf16[64,1152]{1,0:T(8,128)(2,1)S(1)}, bf16[64,1152]{1,0:T(8,128)(2,1)S(1)}, u32[]{:S(2)}, u32[]{:S(2)}) collective-permute-start(bf16[64,1152]{1,0:T(8,128)(2,1)S(1)} %pad_maximum_fusion.8), channel_id=1, source_target_pairs={{0,6},{1,7},{2,0},{3,1},{4,2},{5,3},{6,4},{7,5},{8,14},{9,15},{10,... | collective-permute-start | bytes 442376 | tf_op jit(solution)/shard_map/ppermute | solution.py:53
  18.4 14.3 %collective-permute-start.10 = (bf16[64,1152]{1,0:T(8,128)(2,1)S(1)}, bf16[64,1152]{1,0:T(8,128)(2,1)S(1)}, u32[]{:S(2)}, u32[]{:S(2)}) collective-permute-start(bf16[64,1152]{1,0:T(8,128)(2,1)S(1)} %pad_maximum_fusion.8), channel_id=1, source_target_pairs={{0,2},{1,3},{2,4},{3,5},{4,6},{5,7},{6,0},{7,1},{8,10},{9,11},{10,... | collective-permute-start | bytes 442376 | tf_op jit(solution)/shard_map/ppermute | solution.py:53
  35.7 8.7 %collective-permute-start.11 = (bf16[208,1152]{1,0:T(8,128)(2,1)}, bf16[208,1152]{1,0:T(8,128)(2,1)S(1)}, u32[]{:S(2)}, u32[]{:S(2)}) collective-permute-start(bf16[208,1152]{1,0:T(8,128)(2,1)} %get-tuple-element.281), channel_id=1, source_target_pairs={{0,24},{1,97},{2,26},{3,99},{4,28},{5,101},{6,30},{7,103},{8,0},{9... | collective-permute-start | bytes 1437704 | tf_op jit(solution)/shard_map/ppermute | solution.py:53
  42.6 9.8 %collective-permute-start.12 = (bf16[208,1152]{1,0:T(8,128)(2,1)}, bf16[208,1152]{1,0:T(8,128)(2,1)}, u32[]{:S(2)}, u32[]{:S(2)}) collective-permute-start(bf16[208,1152]{1,0:T(8,128)(2,1)} %get-tuple-element.282), channel_id=1, source_target_pairs={{0,16},{1,65},{2,18},{3,67},{4,20},{5,69},{6,22},{7,71},{8,24},{9,... | collective-permute-start | bytes 1437704 | tf_op jit(solution)/shard_map/ppermute | solution.py:53
  43.5 13.8 %collective-permute-start.13 = (bf16[208,1152]{1,0:T(8,128)(2,1)}, bf16[208,1152]{1,0:T(8,128)(2,1)S(1)}, u32[]{:S(2)}, u32[]{:S(2)}) collective-permute-start(bf16[208,1152]{1,0:T(8,128)(2,1)} %get-tuple-element.283), channel_id=1, source_target_pairs={{0,8},{1,33},{2,10},{3,35},{4,12},{5,37},{6,14},{7,39},{8,16},{9,4... | collective-permute-start | bytes 1437704 | tf_op jit(solution)/shard_map/ppermute | solution.py:53
  54.3 8.3 %copy-start.3 = (bf16[1,1536,384]{2,1,0:T(8,128)(2,1)S(1)}, bf16[1,1536,384]{2,1,0:T(8,128)(2,1)}, u32[]{:S(2)}) copy-start(bf16[1,1536,384]{2,1,0:T(8,128)(2,1)} %param.11) | copy-start | bytes 3538948
  58.2 25.9 %collective-permute-start.16 = (bf16[416,1152]{1,0:T(8,128)(2,1)S(1)}, bf16[416,1152]{1,0:T(8,128)(2,1)S(1)}, u32[]{:S(2)}, u32[]{:S(2)}) collective-permute-start(bf16[416,1152]{1,0:T(8,128)(2,1)S(1)} %get-tuple-element.278), channel_id=1, source_target_pairs={{0,32},{1,9},{2,34},{3,11},{4,36},{5,13},{6,38},{7,15},{8,40},{9,1... | collective-permute-start | bytes 2875400 | tf_op jit(solution)/shard_map/ppermute | solution.py:53
  59.1 13.0 %collective-permute-start.15 = (bf16[416,1152]{1,0:T(8,128)(2,1)S(1)}, bf16[416,1152]{1,0:T(8,128)(2,1)S(1)}, u32[]{:S(2)}, u32[]{:S(2)}) collective-permute-start(bf16[416,1152]{1,0:T(8,128)(2,1)S(1)} %get-tuple-element.278), channel_id=1, source_target_pairs={{0,96},{1,25},{2,98},{3,27},{4,100},{5,29},{6,102},{7,31},{8,104},... | collective-permute-start | bytes 2875400 | tf_op jit(solution)/shard_map/ppermute | solution.py:53
  61.0 23.8 %collective-permute-start.17 = (bf16[416,1152]{1,0:T(8,128)(2,1)S(1)}, bf16[416,1152]{1,0:T(8,128)(2,1)S(1)}, u32[]{:S(2)}, u32[]{:S(2)}) collective-permute-start(bf16[416,1152]{1,0:T(8,128)(2,1)S(1)} %pad_maximum_fusion), channel_id=1, source_target_pairs={{0,96},{1,25},{2,98},{3,27},{4,100},{5,29},{6,102},{7,31},{8,104},... | collective-permute-start | bytes 2875400 | tf_op jit(solution)/shard_map/ppermute | solution.py:53
  62.0 20.7 %collective-permute-start.14 = (bf16[416,1152]{1,0:T(8,128)(2,1)S(1)}, bf16[416,1152]{1,0:T(8,128)(2,1)S(1)}, u32[]{:S(2)}, u32[]{:S(2)}) collective-permute-start(bf16[416,1152]{1,0:T(8,128)(2,1)S(1)} %pad_maximum_fusion), channel_id=1, source_target_pairs={{0,32},{1,9},{2,34},{3,11},{4,36},{5,13},{6,38},{7,15},{8,40},{9,1... | collective-permute-start | bytes 2875400 | tf_op jit(solution)/shard_map/ppermute | solution.py:53
  72.1 20.5 %collective-permute-start.19 = (bf16[416,1152]{1,0:T(8,128)(2,1)S(1)}, bf16[416,1152]{1,0:T(8,128)(2,1)S(1)}, u32[]{:S(2)}, u32[]{:S(2)}) collective-permute-start(bf16[416,1152]{1,0:T(8,128)(2,1)S(1)} %collective-permute-done.15), channel_id=1, source_target_pairs={{0,96},{1,25},{2,98},{3,27},{4,100},{5,29},{6,102},{7,31},{8,104},... | collective-permute-start | bytes 2875400 | tf_op jit(solution)/shard_map/ppermute | solution.py:53
  82.7 14.2 %collective-permute-start.18 = (bf16[416,1152]{1,0:T(8,128)(2,1)S(1)}, bf16[416,1152]{1,0:T(8,128)(2,1)S(1)}, u32[]{:S(2)}, u32[]{:S(2)}) collective-permute-start(bf16[416,1152]{1,0:T(8,128)(2,1)S(1)} %collective-permute-done.14), channel_id=1, source_target_pairs={{0,32},{1,9},{2,34},{3,11},{4,36},{5,13},{6,38},{7,15},{8,40},{9,1... | collective-permute-start | bytes 2875400 | tf_op jit(solution)/shard_map/ppermute | solution.py:53
  96.9 5.8 %copy-start.2 = (f32[96,4608]{1,0:T(8,128)S(1)}, f32[96,4608]{1,0:T(8,128)}, u32[]{:S(2)}) copy-start(f32[96,4608]{1,0:T(8,128)} %v_ref.7) | copy-start | bytes 5308420
  97.6 5.1 %copy-start = (f32[96,4608]{1,0:T(8,128)S(1)}, f32[96,4608]{1,0:T(8,128)}, u32[]{:S(2)}) copy-start(f32[96,4608]{1,0:T(8,128)} %t_ref.7) | copy-start | bytes 5308420
  97.6 5.1 %copy-start.1 = (f32[96,4608]{1,0:T(8,128)S(1)}, f32[96,4608]{1,0:T(8,128)}, u32[]{:S(2)}) copy-start(f32[96,4608]{1,0:T(8,128)} %m_ref.7) | copy-start | bytes 5308420
  97.8 6.2 %collective-permute-start.22 = (f32[96,1152]{1,0:T(8,128)S(1)}, f32[96,1152]{1,0:T(8,128)S(1)}, u32[]{:S(2)}, u32[]{:S(2)}) collective-permute-start(f32[96,1152]{1,0:T(8,128)S(1)} %get-tuple-element.260), channel_id=1, source_target_pairs={{0,1},{1,0},{2,3},{3,2},{4,5},{5,4},{6,7},{7,6},{8,9},{9,8},{10,11... | collective-permute-start | bytes 1327112 | tf_op jit(solution)/shard_map/ppermute | solution.py:53
  100.9 11.7 %collective-permute-start.21 = (f32[96,1152]{1,0:T(8,128)S(1)}, f32[96,1152]{1,0:T(8,128)S(1)}, u32[]{:S(2)}, u32[]{:S(2)}) collective-permute-start(f32[96,1152]{1,0:T(8,128)S(1)} %get-tuple-element.261), channel_id=1, source_target_pairs={{0,128},{1,129},{2,130},{3,131},{4,132},{5,133},{6,134},{7,135},{8... | collective-permute-start | bytes 1327112 | tf_op jit(solution)/shard_map/ppermute | solution.py:53
  101.4 20.9 %collective-permute-start.20 = (f32[96,1152]{1,0:T(8,128)S(1)}, f32[96,1152]{1,0:T(8,128)S(1)}, u32[]{:S(2)}, u32[]{:S(2)}) collective-permute-start(f32[96,1152]{1,0:T(8,128)S(1)} %get-tuple-element.262), channel_id=1, source_target_pairs={{0,129},{1,128},{2,131},{3,130},{4,133},{5,132},{6,135},{7,134},{8... | collective-permute-start | bytes 1327112 | tf_op jit(solution)/shard_map/ppermute | solution.py:53

commit v2 on v1

v2 whole, which is shorter than its diff:
```python
import functools

import jax
import jax.numpy as jnp
from jax import lax
from jax.experimental import pallas as pl
from jax.experimental.pallas import tpu as pltpu
from jax.sharding import PartitionSpec as P

corr_first = 1.0 - 0.9**10
corr_second = 1.0 - 0.95**10

AXES = ("section", "shard", "rep")
RING = 4
CAP_CHUNK = 16
CAP_ROUTE = 16
SMALL = pl.CostEstimate(flops=1024, bytes_accessed=1024, transcendentals=0)


def index_of(section, y, x, z_hi, rep):
    return (section * 64 + (y * RING + x) * RING + z_hi) * 2 + rep


def pairs(move):
    out = []
    for section in range(2):
        for y in range(RING):
            for x in range(RING):
                for z_hi in range(RING):
                    for rep in range(2):
                        out.append((index_of(section, y, x, z_hi, rep), index_of(*move(section, y, x, z_hi, rep))))
    return out


def quad_pairs(a, b):
    return pairs(lambda s, y, x, z, r: (s ^ a, y, x, z, r ^ b))


def depth_pairs(step):
    return pairs(lambda s, y, x, z, r: (s, y, x, (z + step) % RING, r))


def second_pairs(step):
    return pairs(lambda s, y, x, z, r: (s, (y + step * r) % RING, (x + step * (1 - r)) % RING, z, r))


def last_pairs(step):
    return pairs(lambda s, y, x, z, r: (s, (y + step * (1 - r)) % RING, (x + step * r) % RING, z, r))


def send(array, table):
    return lax.ppermute(array, AXES, table)


def pick(mask, first, second):
    return jnp.where(mask, first, second)


def roll_to(array, shift, axis):
    size = array.shape[axis]
    head = lax.slice_in_dim(array, 0, size - 1, axis=axis)
    return lax.dynamic_slice_in_dim(jnp.concatenate([array, head], axis), shift, size, axis)


def slots_of(mask, cap):
    size = mask.shape[-1]
    upto = lax.broadcasted_iota(jnp.int32, (size, size), 0) <= lax.broadcasted_iota(jnp.int32, (size, size), 1)
    counts = mask.astype(jnp.int32)
    rank = jnp.sum(counts[..., :, None] * upto.astype(jnp.int32), axis=-2) - 1
    places = lax.broadcasted_iota(jnp.int32, (cap, 1), 0)
    return jnp.logical_and(rank[..., None, :] == places, mask[..., None, :])


def in_hbm(array):
    return pltpu.with_memory_space_constraint(array, pltpu.HBM)


def adamw_kernel(where_ref, g_ref, t_ref, m_ref, v_ref, *refs):
    t_out, m_out, v_out = refs[-3:]
    g = g_ref[...]
    new_one = 0.9 * m_ref[...] + 0.1 * g
    new_two = 0.95 * v_ref[...] + 0.05 * g * g
    update = new_one / corr_first / (jnp.sqrt(new_two / corr_second) + 1e-08)
    t = t_ref[...]
    t_out[...] = t - 0.01 * (update + 0.1 * t)
    m_out[...] = new_one
    v_out[...] = new_two


def adamw_part(where, g, state, previous, *order):
    rows, width = g.shape
    inner = pl.BlockSpec((rows, width), lambda i, where_ref: (0, where_ref[1]))
    wide = pl.BlockSpec((rows, width), lambda i, where_ref: (0, where_ref[0]))
    anywhere = pl.BlockSpec(memory_space=pl.ANY)
    specs = [pl.BlockSpec((rows, width), lambda i, where_ref: (0, 0))] + [inner] * 3 + [anywhere] * len(order)
    args = [g, *state, *order]
    aliases = {}
    if previous is not None:
        aliases = {1 + len(args) + i: i for i in range(3)}
        specs += [anywhere] * 3
        args += list(previous)
    return pl.pallas_call(
        adamw_kernel,
        grid_spec=pltpu.PrefetchScalarGridSpec(num_scalar_prefetch=1, grid=(1,), in_specs=specs, out_specs=[wide] * 3),
        out_shape=[jax.ShapeDtypeStruct((rows, 4 * width), jnp.float32)] * 3,
        input_output_aliases=aliases,
        cost_estimate=SMALL,
        compiler_params=pltpu.CompilerParams(vmem_limit_bytes=8 * 1024 * 1024),
    )(where, *args)


def fetch_kernel(where_ref, *refs):
    sources, outs, sems = refs[:3], refs[4:7], refs[7]
    width = outs[0].shape[1]
    columns = pl.ds(pl.multiple_of(where_ref[0] * width, 128), width)
    copies = [pltpu.make_async_copy(a.at[:, columns], b, sems.at[k]) for k, (a, b) in enumerate(zip(sources, outs))]
    for copy in copies:
        copy.start()
    for copy in copies:
        copy.wait()


def fetch(where, arrays, order):
    anywhere = pl.BlockSpec(memory_space=pl.ANY)
    rows, width = arrays[0].shape
    return pl.pallas_call(
        fetch_kernel,
        in_specs=[pl.BlockSpec(memory_space=pltpu.SMEM)] + [anywhere] * 4,
        out_specs=[pl.BlockSpec(memory_space=pltpu.VMEM)] * 3,
        out_shape=[pltpu.VMEM((rows, width // 2), array.dtype) for array in arrays],
        scratch_shapes=[pltpu.SemaphoreType.DMA((3,))],
        cost_estimate=SMALL,
        compiler_params=pltpu.CompilerParams(vmem_limit_bytes=4 * 1024 * 1024),
    )(where, *map(in_hbm, arrays), order)


def cut_kernel(where_ref, acts, *outs):
    width = outs[0].shape[1]
    for k, out in enumerate(outs):
        out[...] = acts[:, pl.ds(pl.multiple_of(where_ref[k] * width, 128), width)]


def cut_quarters(where, acts):
    rows, model = acts.shape
    vmem = pl.BlockSpec(memory_space=pltpu.VMEM)
    return pl.pallas_call(
        cut_kernel,
        in_specs=[pl.BlockSpec(memory_space=pltpu.SMEM), vmem],
        out_specs=[vmem] * 4,
        out_shape=[jax.ShapeDtypeStruct((rows, model // 4), acts.dtype)] * 4,
        cost_estimate=SMALL,
        compiler_params=pltpu.CompilerParams(vmem_limit_bytes=4 * 1024 * 1024),
    )(where, in_hbm(acts))


def spread_kernel(where_ref, route, *refs):
    pieces, outs = refs[:4], refs[4:]
    spoken = pieces[0].shape[0] - CAP_CHUNK
    routed = jnp.dot(route[:, :CAP_CHUNK], pieces[0][spoken:, :], preferred_element_type=jnp.float32)
    for k in range(1, 4):
        columns = slice(k * CAP_CHUNK, (k + 1) * CAP_CHUNK)
        routed += jnp.dot(route[:, columns], pieces[k][spoken:, :], preferred_element_type=jnp.float32)
    routed = routed.astype(jnp.bfloat16)
    for k in range(4):
        low = pl.multiple_of(((where_ref[0] + k) & 3) * spoken, 16)
        for out in outs:
            out[pl.ds(low, spoken), :] = pieces[k][:spoken, :]
        outs[k][4 * spoken :, :] = routed[k * CAP_ROUTE : (k + 1) * CAP_ROUTE]


def spread(z_hi, route, pieces):
    tall, width = pieces[0].shape
    rows = 4 * (tall - CAP_CHUNK) + CAP_ROUTE
    return pl.pallas_call(
        spread_kernel,
        in_specs=[pl.BlockSpec(memory_space=pltpu.SMEM)] + [pl.BlockSpec(memory_space=pltpu.VMEM)] * 5,
        out_specs=[pl.BlockSpec(memory_space=pltpu.VMEM)] * 4,
        out_shape=[jax.ShapeDtypeStruct((rows, width), jnp.bfloat16)] * 4,
        cost_estimate=SMALL,
        compiler_params=pltpu.CompilerParams(vmem_limit_bytes=4 * 1024 * 1024),
    )(z_hi.reshape(1), route, *pieces)


def join_kernel(first, second, *refs):
    out = refs[-1]
    rows = first.shape[0]
    out[:rows, :] = first[...]
    out[rows:, :] = second[...]


def join(first, second, *order):
    rows, width = first.shape
    vmem = pl.BlockSpec(memory_space=pltpu.VMEM)
    return pl.pallas_call(
        join_kernel,
        in_specs=[vmem, vmem] + [pl.BlockSpec(memory_space=pl.ANY)] * len(order),
        out_specs=vmem,
        out_shape=jax.ShapeDtypeStruct((2 * rows, width), first.dtype),
        cost_estimate=SMALL,
        compiler_params=pltpu.CompilerParams(vmem_limit_bytes=4 * 1024 * 1024),
    )(first, second, *order)


def prepare_kernel(group, where_ref, ids_ref, own_hbm, other_hbm, pass_in, *outs):
    weights, flags, largest = outs[:8], outs[8], outs[9]
    own, other, sems = outs[11:]
    copies = [pltpu.make_async_copy(a, b, sems.at[k]) for k, (a, b) in enumerate(zip((own_hbm, other_hbm), (own, other)))]
    for copy in copies:
        copy.start()
    voc = own.shape[1]
    tokens = group // 4
    rows = 2 * group + CAP_ROUTE
    ids = ids_ref[...]
    spots = ids.shape[1]
    hit = ids < voc * 64
    home = jnp.where(hit, ids // voc, -1)
    place = lax.broadcasted_iota(jnp.int32, ids.shape, 1) // (2 * tokens)
    most = jnp.int32(0)
    for k in range(4):
        in_chunk = jnp.sum(jnp.where(jnp.logical_and(hit, place == k), 1, 0), 1, keepdims=True)
        to_x = jnp.sum(jnp.where(jnp.logical_and(hit, (home >> 2) & 3 == k), 1, 0), 1, keepdims=True)
        to_y = jnp.sum(jnp.where(jnp.logical_and(hit, home >> 4 == k), 1, 0), 1, keepdims=True)
        excess = jnp.maximum(in_chunk - CAP_CHUNK, jnp.maximum(to_x, to_y) - CAP_ROUTE)
        most = jnp.maximum(most, jnp.max(excess))
    flags[0] = most
    mine = jnp.where(where_ref[34] == 0, (home >> 2) & 3, home >> 4) == where_ref[32]
    mine = jnp.logical_and(hit, mine)
    upto = lax.broadcasted_iota(jnp.int32, (spots, spots), 0) <= lax.broadcasted_iota(jnp.int32, (spots, spots), 1)
    rank = jnp.dot(
        jnp.where(mine, 1.0, 0.0).astype(jnp.bfloat16),
        jnp.where(upto, 1.0, 0.0).astype(jnp.bfloat16),
        preferred_element_type=jnp.float32,
    ).astype(jnp.int32)
    rank = jnp.where(jnp.logical_and(mine, most <= 0), rank, 0)
    number = lax.broadcasted_iota(jnp.int32, (CAP_ROUTE, spots), 0) + 1
    columns = lax.broadcasted_iota(jnp.int32, (CAP_ROUTE, voc), 1) + where_ref[33]
    flags[1] = jnp.sum(jnp.where(jnp.logical_and(mine, home * voc == where_ref[33]), 1, 0))

    slots = []
    for c in range(16):
        chosen = rank[c : c + 1, :] == number
        slots.append(jnp.sum(jnp.where(chosen, ids[c : c + 1, :] + 1, 0), 1, keepdims=True) - 1)
    slots = jnp.concatenate(slots, 0)
    for copy in copies:
        copy.wait()
    top = jnp.float32(0)
    for n in range(16):
        out, low = weights[n // 2], n % 2 * rows
        at = pl.multiple_of(where_ref[n] * group, 16)
        first, second = own[pl.ds(at, group), :], other[pl.ds(at, group), :]
        for z in range(4):
            both = [array[z * tokens : (z + 1) * tokens, :] for array in (first, second)]
            out[low + 2 * z * tokens : low + 2 * (z + 1) * tokens, :] = jnp.concatenate(both, 0)
        top = jnp.maximum(top, jnp.max(jnp.abs(first.astype(jnp.float32))))
        top = jnp.maximum(top, jnp.max(jnp.abs(second.astype(jnp.float32))))
        picked = jnp.full((CAP_ROUTE, 1), -1, jnp.int32)
        for c in range(16):
            picked = jnp.where(where_ref[16 + n] == c, slots[c * CAP_ROUTE : (c + 1) * CAP_ROUTE, :], picked)
        out[low + 2 * group : low + rows, :] = jnp.where(picked == columns, 1.0, 0.0).astype(jnp.bfloat16)
    largest[0] = top


def prepare(where, ids, own, other, passing, group):
    voc = own.shape[1]
    rows = 2 * (2 * group + CAP_ROUTE)
    vmem, smem = pl.BlockSpec(memory_space=pltpu.VMEM), pl.BlockSpec(memory_space=pltpu.SMEM)
    anywhere = pl.BlockSpec(memory_space=pl.ANY)
    return pl.pallas_call(
        functools.partial(prepare_kernel, group),
        in_specs=[smem, vmem] + [anywhere] * 3,
        out_specs=[vmem] * 8 + [smem, smem, anywhere],
        out_shape=[pltpu.VMEM((rows, voc), jnp.bfloat16)] * 8
        + [jax.ShapeDtypeStruct((2,), jnp.int32), jax.ShapeDtypeStruct((1,), jnp.float32)]
        + [jax.ShapeDtypeStruct(passing.shape, passing.dtype)],
        input_output_aliases={4: 10},
        scratch_shapes=[pltpu.VMEM(own.shape, own.dtype)] * 2 + [pltpu.SemaphoreType.DMA((2,))],
        cost_estimate=SMALL,
        compiler_params=pltpu.CompilerParams(vmem_limit_bytes=8 * 1024 * 1024),
    )(where, ids, in_hbm(own), other, passing)


def add_products(total, products):
    for weights, rows in products:
        total = total + dot_rows(weights, rows)
    return total


def dot_rows(weights, rows):
    return lax.dot_general(weights, rows, (((0,), (0,)), ((), ())), preferred_element_type=jnp.float32)


def full_embedding(acts, own_ids, section, shard, quarter, voc, width):
    tokens = acts.shape[0]
    step = pairs(lambda s, y, x, z, r: (s, (y + (x + (z + 1) // RING) // RING) % RING, (x + (z + 1) // RING) % RING, (z + 1) % RING, r))
    rows = shard * voc + lax.broadcasted_iota(jnp.int32, (1, voc), 1)

    def body(i, state):
        current, total = state
        source = lax.rem(shard - i + 64, 64)
        ids = lax.dynamic_slice_in_dim(own_ids, source * tokens, tokens, 0)
        hot = jnp.logical_and(ids[:, None] == rows, section == 0).astype(jnp.bfloat16)
        return send(current, step), total + dot_rows(hot, current)

    total = lax.fori_loop(0, 64, body, (acts, jnp.zeros((voc, acts.shape[1]), jnp.float32)))[1]
    total = total + send(total, quad_pairs(0, 1))
    total = total + send(total, quad_pairs(1, 0))
    return lax.dynamic_slice_in_dim(total, quarter * width, width, 1)


def local(acts, logit_grad, token_ids, table, moment_one, moment_two):
    section = lax.axis_index("section")
    shard = lax.axis_index("shard")
    rep = lax.axis_index("rep")
    y, x, z_hi = shard >> 4, (shard >> 2) & 3, shard & 3
    on_first = rep == 0
    second, last = pick(on_first, x, y), pick(on_first, y, x)
    quarter = 2 * section + rep

    own_acts = acts[0, 0]
    own_logits = logit_grad[0]
    tokens, model = own_acts.shape
    voc = own_logits.shape[1]
    width = model // 4
    part = voc // 4

    pieces = {}
    flips = ((1, 0), (1, 1), (0, 1), (0, 0))
    takers = jnp.stack([2 * (section ^ a) + (rep ^ b) for a, b in flips]).astype(jnp.int32)
    for (a, b), block in zip(flips, cut_quarters(takers, own_acts)):
        pieces[a, b] = send(block, quad_pairs(a, b)) if (a, b) != (0, 0) else block

    hidden = jnp.concatenate([jnp.where(section == 1, pieces[0, b], pieces[1, b]) for b in (0, 1)], 0)
    cotangent = jnp.concatenate([jnp.where(section == 0, pieces[0, b], pieces[1, b]) for b in (0, 1)], 0)

    other_ids = send(token_ids, quad_pairs(0, 1))
    other_logits = send(own_logits, quad_pairs(0, 1))

    ids = jnp.concatenate([token_ids, other_ids], 0)
    own_chunk = lax.dynamic_slice_in_dim(ids, shard * tokens, tokens, 1).reshape(2 * tokens)
    own_hot = slots_of(own_chunk < voc * 64, CAP_CHUNK).astype(jnp.bfloat16)

    kept = jnp.dot(own_hot, cotangent, preferred_element_type=jnp.float32).astype(jnp.bfloat16)
    chunk = jnp.concatenate([hidden, kept], 0)

    down, far, up = (send(chunk, depth_pairs(step)) for step in (-1, 2, 1))

    targets = lax.broadcasted_iota(jnp.int32, (1, 4, 1), 1)

    def routes(shards):
        live = shards[:, None, :] >= 0
        to_x = jnp.logical_and((shards[:, None, :] >> 2) & 3 == targets, live)
        to_y = jnp.logical_and(shards[:, None, :] >> 4 == targets, live)
        return to_x, to_y

    def kept_ids(ids):
        hit = ids < voc * 64
        hot = slots_of(hit, CAP_CHUNK)
        return hit, (jnp.sum(jnp.where(hot, ids[:, None, :] + 1, 0), -1) - 1).reshape(-1, 4 * CAP_CHUNK)

    def shards_of(column_ids):
        return jnp.where(column_ids >= 0, column_ids // voc, -1)

    own_column = lax.dynamic_slice_in_dim(ids, (shard >> 2) * 4 * tokens, 4 * tokens, 1)
    own_column = own_column.reshape(2, 4, tokens).transpose(1, 0, 2).reshape(4, 2 * tokens)
    own_route = slots_of(pick(on_first, *routes(shards_of(kept_ids(own_column)[1]))), CAP_ROUTE)[0]
    own_route = roll_to(own_route, second, 0).reshape(4 * CAP_ROUTE, 4, CAP_CHUNK)
    own_route = roll_to(own_route, z_hi, 1).astype(jnp.bfloat16).reshape(4 * CAP_ROUTE, 4 * CAP_CHUNK)

    outgoing = list(spread(z_hi, own_route, [chunk, down, far, up]))

    columns = ids.reshape(2, 16, 4, tokens).transpose(1, 2, 0, 3).reshape(16, 8 * tokens)
    turning = [(second + k) & 3 for k in range(4)]
    order = [((last + offset) & 3, turn) for offset in range(4) for turn in turning]
    places = [pick(on_first, 4 * fixed + turn, 4 * turn + fixed) for fixed, turn in order]
    where = jnp.stack([*places, *places, second, shard * voc, rep]).astype(jnp.int32)
    *weights, flags, largest, outgoing[2] = prepare(
        where, columns, own_logits, other_logits, outgoing[2], 4 * tokens
    )
    weights = [weights[2 * k : 2 * k + 2] for k in range(4)]
    plane = [outgoing[0], *(send(outgoing[k], second_pairs(step)) for k, step in ((3, -1), (2, 2), (1, 1)))]
    overflow, touched = flags[0] > 0, flags[1] > 0

    start_total = lax.cond(
        overflow,
        lambda: full_embedding(own_acts, token_ids[0], section, shard, quarter, voc, width),
        lambda: jnp.zeros((voc, width), jnp.float32),
    )

    lower, upper = join(plane[0], plane[1], largest, *plane[2:]), join(plane[2], plane[3], largest, plane[1])
    before, behind = [send(lower, last_pairs(1))], [send(upper, last_pairs(-1))]
    total = add_products(start_total, [(weights[0][0], lower), (weights[0][1], upper)])
    before.append(send(upper, last_pairs(1)))
    behind.append(send(lower, last_pairs(-1)))
    far = send(before[0], last_pairs(1)), send(behind[0], last_pairs(-1))
    total = add_products(total, [(weights[3][0], before[0]), (weights[1][1], behind[0])])
    total = add_products(total, [(weights[3][1], before[1]), (weights[1][0], behind[1])])
    total = add_products(total, [(weights[2][0], far[0]), (weights[2][1], far[1])])

    bound = 6.0 * 2 * 64 * tokens * (largest[0] + touched.astype(jnp.float32))
    bound = jnp.where(jnp.logical_or(overflow, bound <= 0), 6.0 * 2 * 64 * tokens * 2, bound)
    scale = 32768.0 / bound

    sent = {}
    for a, b in ((1, 0), (1, 1), (0, 1), (0, 0)):
        row = (2 * (section ^ a) + (rep ^ b)) * part
        block = lax.dynamic_slice_in_dim(total, row, part, 0)
        if a:
            block = (block * scale).astype(jnp.float16)
        sent[a, b] = send(block, quad_pairs(a, b)) if (a, b) != (0, 0) else block
    state = (table, moment_one, moment_two)
    across = fetch((section ^ 1).reshape(1).astype(jnp.int32), state, sent[0, 0])
    results = None
    for a, b in ((0, 0), (0, 1), (1, 0), (1, 1)):
        place = 2 * (section ^ a) + (rep ^ b)
        if a:
            block = sent[a, b].astype(jnp.float32) * (1.0 / scale)
            results = adamw_part(jnp.stack([place, rep ^ b]).astype(jnp.int32), block, across, results)
        else:
            place = jnp.stack([place, place]).astype(jnp.int32)
            results = adamw_part(place, sent[a, b], list(map(in_hbm, state)), results, across[0])
    return tuple(results)


def solution(mesh):
    rows = P(("shard", "section", "rep"), None)
    return jax.shard_map(
        local,
        mesh=mesh,
        in_specs=(P("section", "rep", "shard", None), P("rep", None, "shard"), P("rep", None), rows, rows, rows),
        out_specs=(rows, rows, rows),
        check_vma=False,
    )
```

time: 124 us -> 110 us (0.89)
  waiting for transfers between devices: 56.7 us -> 33.7 us
  Pallas kernels: 4.99 us -> 17.5 us
  other arithmetic: 14.5 us -> 2.82 us
  starting transfers between devices: 29.2 us -> 35.6 us
  matrix products: 7.67 us -> 10.6 us
    ppermute x20, waiting for transfers between devices: 56.7 us -> 33.7 us  [send(): return lax.ppermute(array, AXES, table)]
    pallas_call x0 -> x6, Pallas kernels: none -> 7.57 us  [the longest x1 3.1 us: prepare(): pl.pallas_call(functools.partial(prepare_kernel, group), in_specs=[smem,...]
    ppermute x20, starting transfers between devices: 29.2 us -> 35.6 us  [send(): return lax.ppermute(array, AXES, table)]
    pallas_call x4, Pallas kernels: 4.99 us -> 9.92 us  [adamw_part(): pl.pallas_call(adamw_kernel, grid_spec=pltpu.PrefetchScalarGridSpec(num_s...]
    concatenate x5 -> x1, other arithmetic: 4 us -> 0.04 us  [roll_to(): jnp.concatenate([array, head], axis)]
    dot_general x7 -> x8, matrix products: 7.36 us -> 10.4 us  [dot_rows(): lax.dot_general(weights, rows, (((0,), (0,)), ((), ())), preferred_elemen...]
    unnamed x17 -> x15, local copies, waits for them, and re-layouts: 5.13 us -> 2.54 us
    reduce_sum x4 -> x1, other arithmetic: 2.6 us -> 0.15 us  [kept_ids(): jnp.sum(jnp.where(hot, ids[:, None, :] + 1, 0), -1) - 1]
  transfers between devices with their start and end apart: 20 -> 20, of which waited for: 10 -> 10; matrix products, arithmetic and copies ran while one was open for 22% -> 15% of each run, Pallas kernels for 3% -> 8%
where the time goes in v2:
time: 110 us; the launch traced here: 109 us
  starting transfers between devices  35.6 us (32%)
  waiting for transfers between devices  33.7 us (31%)
  Pallas kernels  17.5 us (16%)
  matrix products  10.6 us (10%)
  local copies, waits for them, and re-layouts  6.04 us (5%)
  between operations  3.08 us (3%)
  other arithmetic  2.82 us (3%)
    ppermute x20, starting transfers between devices, send(): return lax.ppermute(array, AXES, table)  35.6 us
    ppermute x20, waiting for transfers between devices, send(): return lax.ppermute(array, AXES, table)  33.7 us
    dot_general x8, matrix products, dot_rows(): lax.dot_general(weights, rows, (((0,), (0,)), ((), ())), preferred_elemen...  10.4 us
    pallas_call x4, Pallas kernels, adamw_part(): pl.pallas_call(adamw_kernel, grid_spec=pltpu.PrefetchScalarGridSpec(num_s...  9.92 us
    pallas_call x1, Pallas kernels, prepare(): pl.pallas_call(functools.partial(prepare_kernel, group), in_specs=[smem,...  3.1 us
    unnamed x15, local copies, waits for them, and re-layouts  2.54 us
  transfers between devices with their start and end apart: 20, of which 10 were waited for; matrix products, arithmetic and copies ran while one was open for 15% of the time, Pallas kernels for 8%

profile of v2, /device:TPU:1, one launch (start us, length us, event | category | flops | bytes accessed | tf_op | source)
XLA Modules:
  0.0 109.5 jit_solution(4499739687053248417)
XLA Ops:
  0.6 1.6 %copy.65 = bf16[1,1,24,4608]{3,2,1,0:T(8,128)(2,1)} copy(bf16[1,1,24,4608]{3,2,1,0:T(8,128)(2,1)} %param.10) | data formatting | bytes 442368
  3.3 3.3 %collective-permute-start.6 = (bf16[24,1152]{1,0:T(8,128)(2,1)S(1)}, bf16[24,1152]{1,0:T(8,128)(2,1)S(1)}, u32[]{:S(2)}, u32[]{:S(2)}) collective-permute-start(bf16[24,1152]{1,0:T(8,128)(2,1)S(1)} %get-tuple-element.224), channel_id=1, source_target_pairs={{0,1},{1,0},{2,3},{3,2},{4,5},{5,4},{6,7},{7,6},{8,9},{9,8},{10,11... | collective-permute-start | bytes 165896 | tf_op jit(solution)/shard_map/ppermute | solution.py:52
  6.7 1.4 %collective-permute-start.5 = (bf16[24,1152]{1,0:T(8,128)(2,1)S(1)}, bf16[24,1152]{1,0:T(8,128)(2,1)S(1)}, u32[]{:S(2)}, u32[]{:S(2)}) collective-permute-start(bf16[24,1152]{1,0:T(8,128)(2,1)S(1)} %get-tuple-element.223), channel_id=1, source_target_pairs={{0,128},{1,129},{2,130},{3,131},{4,132},{5,133},{6,134},{7,135},{8... | collective-permute-start | bytes 165896 | tf_op jit(solution)/shard_map/ppermute | solution.py:52
  13.5 1.3 %collective-permute-start.10 = (bf16[64,1152]{1,0:T(8,128)(2,1)S(1)}, bf16[64,1152]{1,0:T(8,128)(2,1)S(1)}, u32[]{:S(2)}, u32[]{:S(2)}) collective-permute-start(bf16[64,1152]{1,0:T(8,128)(2,1)S(1)} %pad_maximum_fusion.refs_0_), channel_id=1, source_target_pairs={{0,2},{1,3},{2,4},{3,5},{4,6},{5,7},{6,0},{7,1},{8,10},{9,11},{10,... | collective-permute-start | bytes 442376 | tf_op jit(solution)/shard_map/ppermute | solution.py:52
  14.8 3.1 %collective-permute-start.8 = (bf16[64,1152]{1,0:T(8,128)(2,1)S(1)}, bf16[64,1152]{1,0:T(8,128)(2,1)S(1)}, u32[]{:S(2)}, u32[]{:S(2)}) collective-permute-start(bf16[64,1152]{1,0:T(8,128)(2,1)S(1)} %pad_maximum_fusion.refs_0_), channel_id=1, source_target_pairs={{0,6},{1,7},{2,0},{3,1},{4,2},{5,3},{6,4},{7,5},{8,14},{9,15},{10,... | collective-permute-start | bytes 442376 | tf_op jit(solution)/shard_map/ppermute | solution.py:52
  17.9 4.4 %collective-permute-start.9 = (bf16[64,1152]{1,0:T(8,128)(2,1)S(1)}, bf16[64,1152]{1,0:T(8,128)(2,1)S(1)}, u32[]{:S(2)}, u32[]{:S(2)}) collective-permute-start(bf16[64,1152]{1,0:T(8,128)(2,1)S(1)} %pad_maximum_fusion.refs_0_), channel_id=1, source_target_pairs={{0,4},{1,5},{2,6},{3,7},{4,0},{5,1},{6,2},{7,3},{8,12},{9,13},{10,... | collective-permute-start | bytes 442376 | tf_op jit(solution)/shard_map/ppermute | solution.py:52
  22.7 6.7 %collective-permute-done.8.refs_1_ = bf16[64,1152]{1,0:T(8,128)(2,1)S(1)} collective-permute-done((bf16[64,1152]{1,0:T(8,128)(2,1)S(1)}, bf16[64,1152]{1,0:T(8,128)(2,1)S(1)}, u32[]{:S(2)}, u32[]{:S(2)}) %collective-permute-start.8) | collective-permute-done | bytes 147488 | tf_op jit(solution)/shard_map/ppermute | solution.py:52
  29.4 1.8 %collective-permute-done.9.refs_2_ = bf16[64,1152]{1,0:T(8,128)(2,1)S(1)} collective-permute-done((bf16[64,1152]{1,0:T(8,128)(2,1)S(1)}, bf16[64,1152]{1,0:T(8,128)(2,1)S(1)}, u32[]{:S(2)}, u32[]{:S(2)}) %collective-permute-start.9) | collective-permute-done | bytes 147488 | tf_op jit(solution)/shard_map/ppermute | solution.py:52
  31.5 2.8 %collective-permute-start.11 = (bf16[208,1152]{1,0:T(8,128)(2,1)S(1)}, bf16[208,1152]{1,0:T(8,128)(2,1)S(1)}, u32[]{:S(2)}, u32[]{:S(2)}) collective-permute-start(bf16[208,1152]{1,0:T(8,128)(2,1)S(1)} %get-tuple-element.230), channel_id=1, source_target_pairs={{0,24},{1,97},{2,26},{3,99},{4,28},{5,101},{6,30},{7,103},{8,0},{9... | collective-permute-start | bytes 1437704 | tf_op jit(solution)/shard_map/ppermute | solution.py:52
  34.4 3.1 %shard_map.87 = (bf16[416,384]{1,0:T(8,128)(2,1)S(1)}, bf16[416,384]{1,0:T(8,128)(2,1)S(1)}, bf16[416,384]{1,0:T(8,128)(2,1)S(1)}, bf16[416,384]{1,0:T(8,128)(2,...) custom-call(s32[35]{0:T(128)S(1)} %stack.135.where_ref, ...), custom_call_target="tpu_custom_call", output_to_operand_aliasing={{10}: (4, {})} | custom-call | flops 1024 | bytes 1024 | tf_op jit(solution)/shard_map/pallas_call | solution.py:268
  37.5 1.7 %collective-permute-start.12 = (bf16[208,1152]{1,0:T(8,128)(2,1)S(1)}, bf16[208,1152]{1,0:T(8,128)(2,1)S(1)}, u32[]{:S(2)}, u32[]{:S(2)}) collective-permute-start(bf16[208,1152]{1,0:T(8,128)(2,1)S(1)} %get-tuple-element.232), channel_id=1, source_target_pairs={{0,16},{1,65},{2,18},{3,67},{4,20},{5,69},{6,22},{7,71},{8,24},{9,... | collective-permute-start | bytes 1437704 | tf_op jit(solution)/shard_map/ppermute | solution.py:52
  40.0 8.5 %collective-permute-done.13.refs_2_.second = bf16[208,1152]{1,0:T(8,128)(2,1)S(1)} collective-permute-done((bf16[208,1152]{1,0:T(8,128)(2,1)S(1)}, bf16[208,1152]{1,0:T(8,128)(2,1)S(1)}, u32[]{:S(2)}, u32[]{:S(2)}) %collective-permute-start.13) | collective-permute-done | bytes 479264 | tf_op jit(solution)/shard_map/ppermute | solution.py:52
  51.1 1.7 %collective-permute-start.15 = (bf16[416,1152]{1,0:T(8,128)(2,1)S(1)}, bf16[416,1152]{1,0:T(8,128)(2,1)}, u32[]{:S(2)}, u32[]{:S(2)}) collective-permute-start(bf16[416,1152]{1,0:T(8,128)(2,1)S(1)} %shard_map.89), channel_id=1, source_target_pairs={{0,96},{1,25},{2,98},{3,27},{4,100},{5,29},{6,102},{7,31},{8,104},... | collective-permute-start | bytes 2875400 | tf_op jit(solution)/shard_map/ppermute | solution.py:52
  55.6 1.5 %conditional.1 = (f32[384,1152]{1,0:T(8,128)}) conditional(s32[]{:T(128)} %convert_element_type.71, () %tuple.34, (s32[1,1536]{1,0:T(1,128)S(1)}, s32[]{:T(128)}, s32[]{:T(128)}, bf16[24,4608]{1,0:T(8,128)(2,1)}, s32[]{:T(128)}) %tuple.64), branch_computations={%region_4.5_spmd, %region_5.8_spmd} | conditional | flops 90704272 | bytes 98885480 | solution.py:383
  55.8 1.3 %broadcast.435 = f32[384,1152]{1,0:T(8,128)} broadcast(f32[]{:T(128)} %constant.109.clone), dimensions={} | broadcast | bytes 1769476 | tf_op jit(solution)/shard_map/broadcast.1
  57.2 2.7 %collective-permute-start.17 = (bf16[416,1152]{1,0:T(8,128)(2,1)S(1)}, bf16[416,1152]{1,0:T(8,128)(2,1)S(1)}, u32[]{:S(2)}, u32[]{:S(2)}) collective-permute-start(bf16[416,1152]{1,0:T(8,128)(2,1)S(1)} %shard_map.88), channel_id=1, source_target_pairs={{0,96},{1,25},{2,98},{3,27},{4,100},{5,29},{6,102},{7,31},{8,104},... | collective-permute-start | bytes 2875400 | tf_op jit(solution)/shard_map/ppermute | solution.py:52
  59.8 1.7 %fusion.43 = f32[384,1152]{1,0:T(8,128)S(1)} fusion(bf16[416,384]{1,0:T(8,128)(2,1)} %copy-done.2, bf16[416,1152]{1,0:T(8,128)(2,1)S(1)} %shard_map.89), kind=kOutput, calls=%fused_computation.97 | convolution fusion | flops 368050176 | bytes 3047424 | tf_op jit(solution)/shard_map/dot_general | solution.py:289
  61.5 2.2 %collective-permute-done.14 = bf16[416,1152]{1,0:T(8,128)(2,1)} collective-permute-done((bf16[416,1152]{1,0:T(8,128)(2,1)S(1)}, bf16[416,1152]{1,0:T(8,128)(2,1)}, u32[]{:S(2)}, u32[]{:S(2)}) %collective-permute-start.14) | collective-permute-done | bytes 958496 | tf_op jit(solution)/shard_map/ppermute | solution.py:52
  64.3 2.8 %collective-permute-start.19 = (bf16[416,1152]{1,0:T(8,128)(2,1)}, bf16[416,1152]{1,0:T(8,128)(2,1)S(1)}, u32[]{:S(2)}, u32[]{:S(2)}) collective-permute-start(bf16[416,1152]{1,0:T(8,128)(2,1)} %collective-permute-done.15), channel_id=1, source_target_pairs={{0,96},{1,25},{2,98},{3,27},{4,100},{5,29},{6,102},{7,31},{8,104},... | collective-permute-start | bytes 2875400 | tf_op jit(solution)/shard_map/ppermute | solution.py:52
  67.1 1.9 %fusion.44 = f32[384,1152]{1,0:T(8,128)S(1)} fusion(bf16[416,384]{1,0:T(8,128)(2,1)S(1)} %copy-done.1, bf16[416,1152]{1,0:T(8,128)(2,1)} %collective-permute-done.14), kind=kOutput, calls=%fused_computation.98 | convolution fusion | flops 368050176 | bytes 3047424 | tf_op jit(solution)/shard_map/dot_general | solution.py:289
  69.0 1.9 %fusion.45 = f32[384,1152]{1,0:T(8,128)S(1)} fusion(bf16[416,384]{1,0:T(8,128)(2,1)S(1)} %get-tuple-element.236, bf16[416,1152]{1,0:T(8,128)(2,1)} %collective-permute-done.15), kind=kOutput, calls=%fused_computation.99 | convolution fusion | flops 368050176 | bytes 3047424 | tf_op jit(solution)/shard_map/dot_general | solution.py:289
  70.9 3.0 %collective-permute-done.16 = bf16[416,1152]{1,0:T(8,128)(2,1)} collective-permute-done((bf16[416,1152]{1,0:T(8,128)(2,1)S(1)}, bf16[416,1152]{1,0:T(8,128)(2,1)}, u32[]{:S(2)}, u32[]{:S(2)}) %collective-permute-start.16) | collective-permute-done | bytes 958496 | tf_op jit(solution)/shard_map/ppermute | solution.py:52
  73.9 1.9 %fusion.46 = f32[384,1152]{1,0:T(8,128)S(1)} fusion(bf16[416,384]{1,0:T(8,128)(2,1)S(1)} %get-tuple-element.237, bf16[416,1152]{1,0:T(8,128)(2,1)} %collective-permute-done.16), kind=kOutput, calls=%fused_computation.100 | convolution fusion | flops 368050176 | bytes 3047424 | tf_op jit(solution)/shard_map/dot_general | solution.py:289
  78.4 6.4 %collective-permute-done.19 = bf16[416,1152]{1,0:T(8,128)(2,1)S(1)} collective-permute-done((bf16[416,1152]{1,0:T(8,128)(2,1)}, bf16[416,1152]{1,0:T(8,128)(2,1)S(1)}, u32[]{:S(2)}, u32[]{:S(2)}) %collective-permute-start.19) | collective-permute-done | bytes 958496 | tf_op jit(solution)/shard_map/ppermute | solution.py:52
  86.3 4.8 %collective-permute-start.21 = (f16[96,1152]{1,0:T(8,128)(2,1)S(1)}, f16[96,1152]{1,0:T(8,128)(2,1)S(1)}, u32[]{:S(2)}, u32[]{:S(2)}) collective-permute-start(f16[96,1152]{1,0:T(8,128)(2,1)S(1)} %get-tuple-element.301), channel_id=1, source_target_pairs={{0,128},{1,129},{2,130},{3,131},{4,132},{5,133},{6,134},{7,135},{8... | collective-permute-start | bytes 663560 | tf_op jit(solution)/shard_map/ppermute | solution.py:52
  91.2 3.7 %collective-permute-start.22 = (f32[96,1152]{1,0:T(8,128)S(1)}, f32[96,1152]{1,0:T(8,128)S(1)}, u32[]{:S(2)}, u32[]{:S(2)}) collective-permute-start(f32[96,1152]{1,0:T(8,128)S(1)} %get-tuple-element.300), channel_id=1, source_target_pairs={{0,1},{1,0},{2,3},{3,2},{4,5},{5,4},{6,7},{7,6},{8,9},{9,8},{10,11... | collective-permute-start | bytes 1327112 | tf_op jit(solution)/shard_map/ppermute | solution.py:52
  94.9 1.7 %shard_map.90 = (f32[96,2304]{1,0:T(8,128)S(1)}, f32[96,2304]{1,0:T(8,128)S(1)}, f32[96,2304]{1,0:T(8,128)S(1)}) custom-call(s32[1]{0:T(128)} %bitcast.34.where_ref, f32[96,4608]{1,0:T(8,128)} %t_ref.3, f32[96,4608]{1,0:T(8,128)} %m_ref.3, f32[96,4608]{1,0:T(8,128)} %v_ref.3, f32[96,1152]{1,0:T(8,128)S(1)} %get-tuple-element.302.refs_3_.g_ref), custom_call_target="tpu_custom_call" | custom-call | flops 1024 | bytes 1024 | tf_op jit(solution)/shard_map/pallas_call | solution.py:126
  96.7 3.2 %shard_map.91 = (f32[96,4608]{1,0:T(8,128)}, f32[96,4608]{1,0:T(8,128)}, f32[96,4608]{1,0:T(8,128)}) custom-call(s32[2]{0:T(128)S(1)} %pad_add_fusion.5.where_ref, f32[96,1152]{1,0:T(8,128)S(1)} %get-tuple-element.302.refs_3_.g_ref, f32[96,4608]{1,0:T(8,128)} %t_ref.3, f32[96,4608]{1,0:T(8,128)} %m_ref.3, f32[96,4608]{1,0:T(8,128)} %v_ref.3, ...), custom_call_target="tpu_custom_call" | custom-call | flops 1024 | bytes 1024 | tf_op jit(solution)/shard_map/pallas_call | solution.py:102
  99.9 2.8 %collective-permute-done.20 = f16[96,1152]{1,0:T(8,128)(2,1)S(1)} collective-permute-done((f16[96,1152]{1,0:T(8,128)(2,1)S(1)}, f16[96,1152]{1,0:T(8,128)(2,1)S(1)}, u32[]{:S(2)}, u32[]{:S(2)}) %collective-permute-start.20) | collective-permute-done | bytes 221216 | tf_op jit(solution)/shard_map/ppermute | solution.py:52
  102.8 3.2 %shard_map.92 = (f32[96,4608]{1,0:T(8,128)}, f32[96,4608]{1,0:T(8,128)}, f32[96,4608]{1,0:T(8,128)}) custom-call(s32[2]{0:T(128)S(1)} %pad_add_fusion.4.where_ref, f32[96,1152]{1,0:T(8,128)S(1)} %collective-permute-done.22.g_ref, f32[96,4608]{1,0:T(8,128)} %t_ref.3, f32[96,4608]{1,0:T(8,128)} %m_ref.3, ...), custom_call_target="tpu_custom_call", output_to_operand_aliasing={{0}: (6, {}), {1}: (7, {}), {2}: (8, {})} | custom-call | flops 1024 | bytes 1024 | tf_op jit(solution)/shard_map/pallas_call | solution.py:102
  105.9 1.8 %shard_map.93 = (f32[96,4608]{1,0:T(8,128)}, f32[96,4608]{1,0:T(8,128)}, f32[96,4608]{1,0:T(8,128)}) custom-call(s32[2]{0:T(128)S(1)} %pad_add_fusion.3.where_ref, f32[96,1152]{1,0:T(8,128)S(1)} %convert_multiply_fusion.g_ref, f32[96,2304]{1,0:T(8,128)S(1)} %get-tuple-element.241.refs_0_.t_ref, ...), custom_call_target="tpu_custom_call", output_to_operand_aliasing={{0}: (5, {}), {1}: (6, {}), {2}: (7, {})} | custom-call | flops 1024 | bytes 1024 | tf_op jit(solution)/shard_map/pallas_call | solution.py:102
  107.7 1.8 %shard_map.94 = (f32[96,4608]{1,0:T(8,128)}, f32[96,4608]{1,0:T(8,128)}, f32[96,4608]{1,0:T(8,128)}) custom-call(s32[2]{0:T(128)S(1)} %pad_add_fusion.1.where_ref, f32[96,1152]{1,0:T(8,128)S(1)} %convert_multiply_fusion.1.g_ref, f32[96,2304]{1,0:T(8,128)S(1)} %get-tuple-element.241.refs_0_.t_ref, ...), custom_call_target="tpu_custom_call", output_to_operand_aliasing={{0}: (5, {}), {1}: (6, {}), {2}: (7, {})} | custom-call | flops 1024 | bytes 1024 | tf_op jit(solution)/shard_map/pallas_call | solution.py:102
  (98 shorter events, 16.0 us)
Async XLA Ops:
  0.6 21.7 %copy-start.6 = (s32[1,1536]{1,0:T(1,128)S(1)}, s32[1,1536]{1,0:T(1,128)}, u32[]{:S(2)}) copy-start(s32[1,1536]{1,0:T(1,128)} %param.12) | copy-start | bytes 18436
  3.3 9.9 %collective-permute-start.6 = (bf16[24,1152]{1,0:T(8,128)(2,1)S(1)}, bf16[24,1152]{1,0:T(8,128)(2,1)S(1)}, u32[]{:S(2)}, u32[]{:S(2)}) collective-permute-start(bf16[24,1152]{1,0:T(8,128)(2,1)S(1)} %get-tuple-element.224), channel_id=1, source_target_pairs={{0,1},{1,0},{2,3},{3,2},{4,5},{5,4},{6,7},{7,6},{8,9},{9,8},{10,11... | collective-permute-start | bytes 165896 | tf_op jit(solution)/shard_map/ppermute | solution.py:52
  6.7 6.6 %collective-permute-start.7 = (bf16[24,1152]{1,0:T(8,128)(2,1)S(1)}, bf16[24,1152]{1,0:T(8,128)(2,1)S(1)}, u32[]{:S(2)}, u32[]{:S(2)}) collective-permute-start(bf16[24,1152]{1,0:T(8,128)(2,1)S(1)} %get-tuple-element.225), channel_id=1, source_target_pairs={{0,129},{1,128},{2,131},{3,130},{4,133},{5,132},{6,135},{7,134},{8... | collective-permute-start | bytes 165896 | tf_op jit(solution)/shard_map/ppermute | solution.py:52
  6.7 6.6 %collective-permute-start.5 = (bf16[24,1152]{1,0:T(8,128)(2,1)S(1)}, bf16[24,1152]{1,0:T(8,128)(2,1)S(1)}, u32[]{:S(2)}, u32[]{:S(2)}) collective-permute-start(bf16[24,1152]{1,0:T(8,128)(2,1)S(1)} %get-tuple-element.223), channel_id=1, source_target_pairs={{0,128},{1,129},{2,130},{3,131},{4,132},{5,133},{6,134},{7,135},{8... | collective-permute-start | bytes 165896 | tf_op jit(solution)/shard_map/ppermute | solution.py:52
  8.1 1.7 %collective-permute-start.3 = (s32[1,1536]{1,0:T(1,128)}, s32[1,1536]{1,0:T(1,128)S(1)}, u32[]{:S(2)}, u32[]{:S(2)}) collective-permute-start(s32[1,1536]{1,0:T(1,128)} %param.12), channel_id=1, source_target_pairs={{0,1},{1,0},{2,3},{3,2},{4,5},{5,4},{6,7},{7,6},{8,9},{9,8},{10,11... | collective-permute-start | bytes 18440 | tf_op jit(solution)/shard_map/ppermute | solution.py:52
  8.8 25.5 %collective-permute-start.4 = (bf16[1536,384]{1,0:T(8,128)(2,1)}, bf16[1536,384]{1,0:T(8,128)(2,1)S(1)}, u32[]{:S(2)}, u32[]{:S(2)}) collective-permute-start(bf16[1536,384]{1,0:T(8,128)(2,1)} %bitcast.64), channel_id=1, source_target_pairs={{0,1},{1,0},{2,3},{3,2},{4,5},{5,4},{6,7},{7,6},{8,9},{9,8},{10,11... | collective-permute-start | bytes 3538952 | tf_op jit(solution)/shard_map/ppermute | solution.py:52
  13.5 9.2 %collective-permute-start.10 = (bf16[64,1152]{1,0:T(8,128)(2,1)S(1)}, bf16[64,1152]{1,0:T(8,128)(2,1)S(1)}, u32[]{:S(2)}, u32[]{:S(2)}) collective-permute-start(bf16[64,1152]{1,0:T(8,128)(2,1)S(1)} %pad_maximum_fusion.refs_0_), channel_id=1, source_target_pairs={{0,2},{1,3},{2,4},{3,5},{4,6},{5,7},{6,0},{7,1},{8,10},{9,11},{10,... | collective-permute-start | bytes 442376 | tf_op jit(solution)/shard_map/ppermute | solution.py:52
  14.8 14.6 %collective-permute-start.8 = (bf16[64,1152]{1,0:T(8,128)(2,1)S(1)}, bf16[64,1152]{1,0:T(8,128)(2,1)S(1)}, u32[]{:S(2)}, u32[]{:S(2)}) collective-permute-start(bf16[64,1152]{1,0:T(8,128)(2,1)S(1)} %pad_maximum_fusion.refs_0_), channel_id=1, source_target_pairs={{0,6},{1,7},{2,0},{3,1},{4,2},{5,3},{6,4},{7,5},{8,14},{9,15},{10,... | collective-permute-start | bytes 442376 | tf_op jit(solution)/shard_map/ppermute | solution.py:52
  17.9 13.3 %collective-permute-start.9 = (bf16[64,1152]{1,0:T(8,128)(2,1)S(1)}, bf16[64,1152]{1,0:T(8,128)(2,1)S(1)}, u32[]{:S(2)}, u32[]{:S(2)}) collective-permute-start(bf16[64,1152]{1,0:T(8,128)(2,1)S(1)} %pad_maximum_fusion.refs_0_), channel_id=1, source_target_pairs={{0,4},{1,5},{2,6},{3,7},{4,0},{5,1},{6,2},{7,3},{8,12},{9,13},{10,... | collective-permute-start | bytes 442376 | tf_op jit(solution)/shard_map/ppermute | solution.py:52
  31.5 8.5 %collective-permute-start.11 = (bf16[208,1152]{1,0:T(8,128)(2,1)S(1)}, bf16[208,1152]{1,0:T(8,128)(2,1)S(1)}, u32[]{:S(2)}, u32[]{:S(2)}) collective-permute-start(bf16[208,1152]{1,0:T(8,128)(2,1)S(1)} %get-tuple-element.230), channel_id=1, source_target_pairs={{0,24},{1,97},{2,26},{3,99},{4,28},{5,101},{6,30},{7,103},{8,0},{9... | collective-permute-start | bytes 1437704 | tf_op jit(solution)/shard_map/ppermute | solution.py:52
  34.4 14.2 %collective-permute-start.13 = (bf16[208,1152]{1,0:T(8,128)(2,1)S(1)}, bf16[208,1152]{1,0:T(8,128)(2,1)S(1)}, u32[]{:S(2)}, u32[]{:S(2)}) collective-permute-start(bf16[208,1152]{1,0:T(8,128)(2,1)S(1)} %get-tuple-element.233), channel_id=1, source_target_pairs={{0,8},{1,33},{2,10},{3,35},{4,12},{5,37},{6,14},{7,39},{8,16},{9,4... | collective-permute-start | bytes 1437704 | tf_op jit(solution)/shard_map/ppermute | solution.py:52
  37.5 11.8 %copy-start.3 = (bf16[416,384]{1,0:T(8,128)(2,1)}, bf16[416,384]{1,0:T(8,128)(2,1)S(1)}, u32[]{:S(2)}) copy-start(bf16[416,384]{1,0:T(8,128)(2,1)S(1)} %get-tuple-element.228) | copy-start | bytes 958468
  37.5 13.7 %copy-start = (bf16[416,384]{1,0:T(8,128)(2,1)}, bf16[416,384]{1,0:T(8,128)(2,1)S(1)}, u32[]{:S(2)}) copy-start(bf16[416,384]{1,0:T(8,128)(2,1)S(1)} %get-tuple-element.235) | copy-start | bytes 958468
  37.5 15.4 %copy-start.2 = (bf16[416,384]{1,0:T(8,128)(2,1)}, bf16[416,384]{1,0:T(8,128)(2,1)S(1)}, u32[]{:S(2)}) copy-start(bf16[416,384]{1,0:T(8,128)(2,1)S(1)} %get-tuple-element.234) | copy-start | bytes 958468
  37.5 11.0 %collective-permute-start.12 = (bf16[208,1152]{1,0:T(8,128)(2,1)S(1)}, bf16[208,1152]{1,0:T(8,128)(2,1)S(1)}, u32[]{:S(2)}, u32[]{:S(2)}) collective-permute-start(bf16[208,1152]{1,0:T(8,128)(2,1)S(1)} %get-tuple-element.232), channel_id=1, source_target_pairs={{0,16},{1,65},{2,18},{3,67},{4,20},{5,69},{6,22},{7,71},{8,24},{9,... | collective-permute-start | bytes 1437704 | tf_op jit(solution)/shard_map/ppermute | solution.py:52
  49.3 14.4 %collective-permute-start.14 = (bf16[416,1152]{1,0:T(8,128)(2,1)S(1)}, bf16[416,1152]{1,0:T(8,128)(2,1)}, u32[]{:S(2)}, u32[]{:S(2)}) collective-permute-start(bf16[416,1152]{1,0:T(8,128)(2,1)S(1)} %shard_map.88), channel_id=1, source_target_pairs={{0,32},{1,9},{2,34},{3,11},{4,36},{5,13},{6,38},{7,15},{8,40},{9,1... | collective-permute-start | bytes 2875400 | tf_op jit(solution)/shard_map/ppermute | solution.py:52
  51.1 13.2 %collective-permute-start.15 = (bf16[416,1152]{1,0:T(8,128)(2,1)S(1)}, bf16[416,1152]{1,0:T(8,128)(2,1)}, u32[]{:S(2)}, u32[]{:S(2)}) collective-permute-start(bf16[416,1152]{1,0:T(8,128)(2,1)S(1)} %shard_map.89), channel_id=1, source_target_pairs={{0,96},{1,25},{2,98},{3,27},{4,100},{5,29},{6,102},{7,31},{8,104},... | collective-permute-start | bytes 2875400 | tf_op jit(solution)/shard_map/ppermute | solution.py:52
  53.0 20.9 %collective-permute-start.16 = (bf16[416,1152]{1,0:T(8,128)(2,1)S(1)}, bf16[416,1152]{1,0:T(8,128)(2,1)}, u32[]{:S(2)}, u32[]{:S(2)}) collective-permute-start(bf16[416,1152]{1,0:T(8,128)(2,1)S(1)} %shard_map.89), channel_id=1, source_target_pairs={{0,32},{1,9},{2,34},{3,11},{4,36},{5,13},{6,38},{7,15},{8,40},{9,1... | collective-permute-start | bytes 2875400 | tf_op jit(solution)/shard_map/ppermute | solution.py:52
  57.2 10.0 %copy-start.1 = (bf16[416,384]{1,0:T(8,128)(2,1)S(1)}, bf16[416,384]{1,0:T(8,128)(2,1)}, u32[]{:S(2)}) copy-start(bf16[416,384]{1,0:T(8,128)(2,1)} %copy-done) | copy-start | bytes 958468
  57.2 18.7 %collective-permute-start.17 = (bf16[416,1152]{1,0:T(8,128)(2,1)S(1)}, bf16[416,1152]{1,0:T(8,128)(2,1)S(1)}, u32[]{:S(2)}, u32[]{:S(2)}) collective-permute-start(bf16[416,1152]{1,0:T(8,128)(2,1)S(1)} %shard_map.88), channel_id=1, source_target_pairs={{0,96},{1,25},{2,98},{3,27},{4,100},{5,29},{6,102},{7,31},{8,104},... | collective-permute-start | bytes 2875400 | tf_op jit(solution)/shard_map/ppermute | solution.py:52
  63.7 21.8 %collective-permute-start.18 = (bf16[416,1152]{1,0:T(8,128)(2,1)}, bf16[416,1152]{1,0:T(8,128)(2,1)S(1)}, u32[]{:S(2)}, u32[]{:S(2)}) collective-permute-start(bf16[416,1152]{1,0:T(8,128)(2,1)} %collective-permute-done.14), channel_id=1, source_target_pairs={{0,32},{1,9},{2,34},{3,11},{4,36},{5,13},{6,38},{7,15},{8,40},{9,1... | collective-permute-start | bytes 2875400 | tf_op jit(solution)/shard_map/ppermute | solution.py:52
  64.3 20.4 %collective-permute-start.19 = (bf16[416,1152]{1,0:T(8,128)(2,1)}, bf16[416,1152]{1,0:T(8,128)(2,1)S(1)}, u32[]{:S(2)}, u32[]{:S(2)}) collective-permute-start(bf16[416,1152]{1,0:T(8,128)(2,1)} %collective-permute-done.15), channel_id=1, source_target_pairs={{0,96},{1,25},{2,98},{3,27},{4,100},{5,29},{6,102},{7,31},{8,104},... | collective-permute-start | bytes 2875400 | tf_op jit(solution)/shard_map/ppermute | solution.py:52
  75.8 1.0 copy-start.4
  75.8 1.6 %copy-start.5 = (f32[384,1152]{1,0:T(8,128)S(1)}, f32[384,1152]{1,0:T(8,128)}, u32[]{:S(2)}) copy-start(f32[384,1152]{1,0:T(8,128)} %get-tuple-element.396) | copy-start | bytes 5308420
  86.3 13.5 %collective-permute-start.21 = (f16[96,1152]{1,0:T(8,128)(2,1)S(1)}, f16[96,1152]{1,0:T(8,128)(2,1)S(1)}, u32[]{:S(2)}, u32[]{:S(2)}) collective-permute-start(f16[96,1152]{1,0:T(8,128)(2,1)S(1)} %get-tuple-element.301), channel_id=1, source_target_pairs={{0,128},{1,129},{2,130},{3,131},{4,132},{5,133},{6,134},{7,135},{8... | collective-permute-start | bytes 663560 | tf_op jit(solution)/shard_map/ppermute | solution.py:52
  91.2 11.5 %collective-permute-start.22 = (f32[96,1152]{1,0:T(8,128)S(1)}, f32[96,1152]{1,0:T(8,128)S(1)}, u32[]{:S(2)}, u32[]{:S(2)}) collective-permute-start(f32[96,1152]{1,0:T(8,128)S(1)} %get-tuple-element.300), channel_id=1, source_target_pairs={{0,1},{1,0},{2,3},{3,2},{4,5},{5,4},{6,7},{7,6},{8,9},{9,8},{10,11... | collective-permute-start | bytes 1327112 | tf_op jit(solution)/shard_map/ppermute | solution.py:52
  94.9 7.8 %collective-permute-start.20 = (f16[96,1152]{1,0:T(8,128)(2,1)S(1)}, f16[96,1152]{1,0:T(8,128)(2,1)S(1)}, u32[]{:S(2)}, u32[]{:S(2)}) collective-permute-start(f16[96,1152]{1,0:T(8,128)(2,1)S(1)} %get-tuple-element.303), channel_id=1, source_target_pairs={{0,129},{1,128},{2,131},{3,130},{4,133},{5,132},{6,135},{7,134},{8... | collective-permute-start | bytes 663560 | tf_op jit(solution)/shard_map/ppermute | solution.py:52

commit v3 on v2

v3 whole, which is shorter than its diff:
```python
import functools

import jax
import jax.numpy as jnp
from jax import lax
from jax.experimental import pallas as pl
from jax.experimental.pallas import tpu as pltpu
from jax.sharding import PartitionSpec as P

corr_first = 1.0 - 0.9**10
corr_second = 1.0 - 0.95**10

AXES = ("section", "shard", "rep")
RING = 4
VOC_SHARD = 384
CAP_CHUNK = 16
CAP_ROUTE = 32
PARTS = (640, 512)
HALF = 640
SMALL = pl.CostEstimate(flops=1024, bytes_accessed=1024, transcendentals=0)


def index_of(section, y, x, z_hi, rep):
    return (section * 64 + (y * RING + x) * RING + z_hi) * 2 + rep


def pairs(move):
    out = []
    for section in range(2):
        for y in range(RING):
            for x in range(RING):
                for z_hi in range(RING):
                    for rep in range(2):
                        out.append((index_of(section, y, x, z_hi, rep), index_of(*move(section, y, x, z_hi, rep))))
    return out


def quad_pairs(a, b):
    return pairs(lambda s, y, x, z, r: (s ^ a, y, x, z, r ^ b))


def depth_pairs(step):
    return pairs(lambda s, y, x, z, r: (s, y, x, (z + step) % RING, r))


def second_pairs(step):
    return pairs(lambda s, y, x, z, r: (s, (y + step * r) % RING, (x + step * (1 - r)) % RING, z, r))


def last_pairs(step):
    return pairs(lambda s, y, x, z, r: (s, (y + step * (1 - r)) % RING, (x + step * r) % RING, z, r))


def pair_pairs(a, b):
    return pairs(lambda s, y, x, z, r: (s ^ a, y ^ r, x ^ (1 - r), z, r ^ b))


def send(array, table):
    return lax.ppermute(array, AXES, table)


def pick(mask, first, second):
    return jnp.where(mask, first, second)


def in_hbm(array):
    return pltpu.with_memory_space_constraint(array, pltpu.HBM)


def adamw_kernel(where_ref, held_ref, *refs):
    parts = len(PARTS)
    firsts, seconds = refs[:parts], refs[parts : 2 * parts]
    t_ref, m_ref, v_ref = refs[2 * parts : 2 * parts + 3]
    t_out, m_out, v_out, held_out = refs[-4:]
    held_out[...] = jnp.full(held_out.shape, held_ref[0], jnp.float32)
    low = 0
    for first, second in zip(firsts, seconds):
        at = (slice(None), slice(low, low + first.shape[1]))
        low += first.shape[1]
        g = jnp.where(pl.program_id(0) == 0, first[...], second[...])
        new_one = 0.9 * m_ref[at] + 0.1 * g
        new_two = 0.95 * v_ref[at] + 0.05 * g * g
        update = new_one / corr_first / (jnp.sqrt(new_two / corr_second) + 1e-08)
        t = t_ref[at]
        t_out[at] = t - 0.01 * (update + 0.1 * t)
        m_out[at] = new_one
        v_out[at] = new_two


def adamw_pair(where, held, first, second, state, previous, *order):
    rows, width = first[0].shape[0], sum(PARTS)
    inner = pl.BlockSpec((rows, width), lambda i, where_ref: (0, where_ref[2 + i]))
    wide = pl.BlockSpec((rows, width), lambda i, where_ref: (0, where_ref[i]))
    small = pl.BlockSpec((8, 128), lambda i, where_ref: (0, 0))
    anywhere = pl.BlockSpec(memory_space=pl.ANY)
    blocks = [*first, *second]
    specs = [pl.BlockSpec(memory_space=pltpu.SMEM)]
    specs += [pl.BlockSpec(block.shape, lambda i, where_ref: (0, 0)) for block in blocks]
    specs += [inner] * 3 + [anywhere] * len(order)
    args = [held, *blocks, *state, *order]
    aliases = {}
    if previous is not None:
        aliases = {1 + len(args) + i: i for i in range(3)}
        specs += [anywhere] * 3
        args += list(previous)
    return pl.pallas_call(
        adamw_kernel,
        grid_spec=pltpu.PrefetchScalarGridSpec(
            num_scalar_prefetch=1, grid=(2,), in_specs=specs, out_specs=[wide] * 3 + [small]
        ),
        out_shape=[jax.ShapeDtypeStruct((rows, 4 * width), jnp.float32)] * 3
        + [jax.ShapeDtypeStruct((8, 128), jnp.float32)],
        input_output_aliases=aliases,
        cost_estimate=SMALL,
        compiler_params=pltpu.CompilerParams(vmem_limit_bytes=10 * 1024 * 1024),
    )(where, *args)


def fetch_kernel(where_ref, *refs):
    sources, outs, sems = refs[:3], refs[4:7], refs[7]
    width = outs[0].shape[1]
    columns = pl.ds(pl.multiple_of(where_ref[0] * width, 128), width)
    copies = [pltpu.make_async_copy(a.at[:, columns], b, sems.at[k]) for k, (a, b) in enumerate(zip(sources, outs))]
    for copy in copies:
        copy.start()
    for copy in copies:
        copy.wait()


def fetch(where, arrays, order):
    anywhere = pl.BlockSpec(memory_space=pl.ANY)
    rows, width = arrays[0].shape
    return pl.pallas_call(
        fetch_kernel,
        in_specs=[pl.BlockSpec(memory_space=pltpu.SMEM)] + [anywhere] * 4,
        out_specs=[pl.BlockSpec(memory_space=pltpu.VMEM)] * 3,
        out_shape=[pltpu.VMEM((rows, width // 2), array.dtype) for array in arrays],
        scratch_shapes=[pltpu.SemaphoreType.DMA((3,))],
        cost_estimate=SMALL,
        compiler_params=pltpu.CompilerParams(vmem_limit_bytes=4 * 1024 * 1024),
    )(where, *map(in_hbm, arrays), order)


def cut_kernel(where_ref, ids, acts, *outs):
    width = outs[0].shape[1]
    for k, out in enumerate(outs[:4]):
        out[...] = acts[:, pl.ds(pl.multiple_of(where_ref[k] * width, 128), width)]
    outs[4][...] = ids[...]


def cut_quarters(where, ids, acts):
    rows, model = acts.shape
    vmem = pl.BlockSpec(memory_space=pltpu.VMEM)
    return pl.pallas_call(
        cut_kernel,
        in_specs=[pl.BlockSpec(memory_space=pltpu.SMEM)] + [vmem] * 2,
        out_specs=[vmem] * 5,
        out_shape=[pltpu.VMEM((rows, model // 4), acts.dtype)] * 4 + [pltpu.VMEM(ids.shape, ids.dtype)],
        cost_estimate=SMALL,
        compiler_params=pltpu.CompilerParams(vmem_limit_bytes=4 * 1024 * 1024),
    )(where, ids, in_hbm(acts))


def by_column(own_ids, other_ids, spots):
    sides = []
    for ids in (own_ids, other_ids):
        sides.append(jnp.concatenate([ids[:, c * spots : (c + 1) * spots] for c in range(16)], 0))
    return jnp.concatenate(sides, 1)


def spots_of(size, dim):
    at = lax.broadcasted_iota(jnp.int32, (size, size), dim)
    side, at = jnp.where(at < size // 2, 0, 1), jnp.where(at < size // 2, at, at - size // 2)
    tokens = size // 8
    z = jnp.where(at < tokens, 0, jnp.where(at < 2 * tokens, 1, jnp.where(at < 3 * tokens, 2, 3)))
    return z, at - z * tokens + side * tokens


def count(flags, upto):
    as_number = lambda mask: jnp.where(mask, 1.0, 0.0).astype(jnp.bfloat16)
    return jnp.dot(as_number(flags), as_number(upto), preferred_element_type=jnp.float32).astype(jnp.int32)


def chunk_kernel(where_ref, own_ids, other_ids, *refs):
    pieces, chunk, route = refs[:4], refs[4], refs[5]
    section, column, z_hi, second, rep = (where_ref[k] for k in range(5))
    tokens, width = pieces[0].shape
    here, there = (pieces[3], pieces[2]), (pieces[0], pieces[1])
    hidden = [jnp.where(section == 1, here[b][...], there[b][...]) for b in (0, 1)]
    cotangent = [jnp.where(section == 0, here[b][...], there[b][...]) for b in (0, 1)]
    chunk[: 2 * tokens, :] = jnp.concatenate(hidden, 0)

    ids = by_column(own_ids, other_ids, 4 * tokens)
    size = ids.shape[1]
    rows = lax.broadcasted_iota(jnp.int32, ids.shape, 0)
    ids = jnp.sum(jnp.where(rows == column, ids, 0), 0, keepdims=True)
    hit = ids < VOC_SHARD * 64
    home = jnp.where(hit, ids // VOC_SHARD, 0)
    pair = jnp.where(rep == 0, (home >> 3) & 1, home >> 5)
    z_from, t_from = spots_of(size, 0)
    z_to, t_to = spots_of(size, 1)
    in_chunk = jnp.logical_and(z_from == z_to, t_from <= t_to)
    in_column = jnp.logical_or(z_from < z_to, in_chunk)
    eight = lambda row: jnp.broadcast_to(row, (8, size))
    slot = count(eight(hit), in_chunk)[:1]
    as_number = lambda mask: jnp.where(mask, 1.0, 0.0).astype(jnp.bfloat16)

    number = lax.broadcasted_iota(jnp.int32, (CAP_CHUNK, size), 0) + 1
    mine = jnp.logical_and(hit, z_to[:1] == z_hi)
    chosen = as_number(jnp.logical_and(slot == number, mine))
    token = lax.broadcasted_iota(jnp.int32, (size, 2 * tokens), 1)
    token = as_number(token == t_from[:, : 2 * tokens])
    chosen = jnp.dot(chosen, token, preferred_element_type=jnp.float32).astype(jnp.bfloat16)
    both = jnp.concatenate(cotangent, 0)
    chunk[2 * tokens :, :] = jnp.dot(chosen, both, preferred_element_type=jnp.float32).astype(jnp.bfloat16)

    kept = jnp.logical_and(hit, slot <= CAP_CHUNK)
    candidate = ((z_to[:1] - z_hi) & 3) * CAP_CHUNK + slot - 1
    same = lax.broadcasted_iota(jnp.int32, (size, size), 0) == lax.broadcasted_iota(jnp.int32, (size, size), 1)
    candidate = jnp.sum(jnp.where(same, jnp.where(kept, candidate, -1), 0), 1, keepdims=True)
    places = as_number(candidate == lax.broadcasted_iota(jnp.int32, (size, 4 * CAP_CHUNK), 1))
    number = lax.broadcasted_iota(jnp.int32, (CAP_ROUTE, size), 0) + 1
    for d in range(4):
        wanted = jnp.logical_and(kept, pair == ((second + d) & 3) >> 1)
        rank = count(eight(wanted), in_column)[:1]
        going = as_number(jnp.logical_and(rank == number, wanted))
        route[d * CAP_ROUTE : (d + 1) * CAP_ROUTE, :] = jnp.dot(
            going, places, preferred_element_type=jnp.float32
        ).astype(jnp.bfloat16)


def build_chunk(where, own_ids, other_ids, pieces):
    tokens, width = pieces[0].shape
    vmem = pl.BlockSpec(memory_space=pltpu.VMEM)
    return pl.pallas_call(
        chunk_kernel,
        in_specs=[pl.BlockSpec(memory_space=pltpu.SMEM)] + [vmem] * 6,
        out_specs=[vmem] * 2,
        out_shape=[
            jax.ShapeDtypeStruct((2 * tokens + CAP_CHUNK, width), jnp.bfloat16),
            jax.ShapeDtypeStruct((4 * CAP_ROUTE, 4 * CAP_CHUNK), jnp.bfloat16),
        ],
        cost_estimate=SMALL,
        compiler_params=pltpu.CompilerParams(vmem_limit_bytes=4 * 1024 * 1024),
    )(where, own_ids, other_ids, *pieces)


def spread_kernel(where_ref, route, *refs):
    pieces, outs, routed = refs[:4], refs[4:8], refs[8]
    spoken, width = pieces[0].shape[0] - CAP_CHUNK, pieces[0].shape[1]
    total = jnp.dot(route[:, :CAP_CHUNK], pieces[0][spoken:, :], preferred_element_type=jnp.float32)
    for k in range(1, 4):
        columns = slice(k * CAP_CHUNK, (k + 1) * CAP_CHUNK)
        total += jnp.dot(route[:, columns], pieces[k][spoken:, :], preferred_element_type=jnp.float32)
    routed[...] = total.astype(jnp.bfloat16)
    for d, out in enumerate(outs):
        columns = pl.ds(pl.multiple_of(((where_ref[1] + d) & 1) * (width - HALF), 128), HALF)
        for k in range(4):
            low = pl.multiple_of(((where_ref[0] + k) & 3) * spoken, 16)
            out[pl.ds(low, spoken), :] = pieces[k][:spoken, columns]
        out[4 * spoken :, :] = routed[d * CAP_ROUTE : (d + 1) * CAP_ROUTE, columns]


def spread(where, route, pieces):
    tall, width = pieces[0].shape
    rows = 4 * (tall - CAP_CHUNK) + CAP_ROUTE
    return pl.pallas_call(
        spread_kernel,
        in_specs=[pl.BlockSpec(memory_space=pltpu.SMEM)] + [pl.BlockSpec(memory_space=pltpu.VMEM)] * 5,
        out_specs=[pl.BlockSpec(memory_space=pltpu.VMEM)] * 4,
        out_shape=[pltpu.VMEM((rows, HALF), jnp.bfloat16)] * 4,
        scratch_shapes=[pltpu.VMEM((4 * CAP_ROUTE, width), jnp.bfloat16)],
        cost_estimate=SMALL,
        compiler_params=pltpu.CompilerParams(vmem_limit_bytes=6 * 1024 * 1024),
    )(where, route, *pieces)


def join_kernel(first, second, *refs):
    out = refs[-1]
    rows = first.shape[0]
    out[:rows, :] = first[...]
    out[rows:, :] = second[...]


def join(first, second, *order):
    rows, width = first.shape
    vmem = pl.BlockSpec(memory_space=pltpu.VMEM)
    return pl.pallas_call(
        join_kernel,
        in_specs=[vmem, vmem] + [pl.BlockSpec(memory_space=pl.ANY)] * len(order),
        out_specs=vmem,
        out_shape=jax.ShapeDtypeStruct((2 * rows, width), first.dtype),
        cost_estimate=SMALL,
        compiler_params=pltpu.CompilerParams(vmem_limit_bytes=4 * 1024 * 1024),
    )(first, second, *order)


def again_kernel(_, *refs):
    half = len(refs) // 2
    for array, out in zip(refs[:half], refs[half:]):
        out[...] = array[...]


def again(order, *arrays):
    vmem = pl.BlockSpec(memory_space=pltpu.VMEM)
    return pl.pallas_call(
        again_kernel,
        in_specs=[pl.BlockSpec(memory_space=pl.ANY)] + [vmem] * len(arrays),
        out_specs=[vmem] * len(arrays),
        out_shape=[jax.ShapeDtypeStruct(array.shape, array.dtype) for array in arrays],
        cost_estimate=SMALL,
        compiler_params=pltpu.CompilerParams(vmem_limit_bytes=6 * 1024 * 1024),
    )(order, *arrays)


def prepare_kernel(group, where_ref, own_ids, other_ids, *refs):
    logits, weights, flags, largest = refs[:4], refs[4:12], refs[12], refs[13]
    own, other, sems = refs[14:]
    voc = own.shape[1]
    tokens = group // 4
    rows = 2 * group + CAP_ROUTE

    def load(shard):
        pair = logits[2 * shard : 2 * shard + 2]
        return [pltpu.make_async_copy(a, b, sems.at[k]) for k, (a, b) in enumerate(zip(pair, (own, other)))]

    for copy in load(0):
        copy.start()
    ids = by_column(own_ids, other_ids, group)
    spots = ids.shape[1]
    hit = ids < voc * 64
    home = jnp.where(hit, ids // voc, -1)
    z_from, t_from = spots_of(spots, 0)
    z_to, t_to = spots_of(spots, 1)
    place = z_to[:16]
    most = jnp.int32(0)
    for k in range(4):
        excess = jnp.sum(jnp.where(jnp.logical_and(hit, place == k), 1, 0), 1, keepdims=True) - CAP_CHUNK
        most = jnp.maximum(most, jnp.max(excess))
    for k in range(2):
        to_x = jnp.sum(jnp.where(jnp.logical_and(hit, (home >> 3) & 1 == k), 1, 0), 1, keepdims=True)
        to_y = jnp.sum(jnp.where(jnp.logical_and(hit, home >> 5 == k), 1, 0), 1, keepdims=True)
        most = jnp.maximum(most, jnp.max(jnp.maximum(to_x, to_y)) - CAP_ROUTE)
    flags[0] = most
    mine = jnp.where(where_ref[19] == 0, (home >> 3) & 1, home >> 5) == where_ref[16] >> 1
    mine = jnp.logical_and(hit, mine)
    rank = count(mine, jnp.logical_or(z_from < z_to, jnp.logical_and(z_from == z_to, t_from <= t_to)))
    rank = jnp.where(jnp.logical_and(mine, most <= 0), rank, 0)
    number = lax.broadcasted_iota(jnp.int32, (CAP_ROUTE, spots), 0) + 1
    for k in range(2):
        flags[1 + k] = jnp.sum(jnp.where(jnp.logical_and(hit, home * voc == where_ref[17 + k]), 1, 0))

    slots = []
    for c in range(16):
        chosen = rank[c : c + 1, :] == number
        slots.append(jnp.sum(jnp.where(chosen, ids[c : c + 1, :] + 1, 0), 1, keepdims=True) - 1)
    slots = jnp.concatenate(slots, 0)
    for shard in range(2):
        for copy in load(shard):
            copy.wait()
        wide = slice(shard * voc, (shard + 1) * voc)
        columns = lax.broadcasted_iota(jnp.int32, (CAP_ROUTE, voc), 1) + where_ref[17 + shard]
        top = jnp.zeros((8, voc), jnp.float32)
        for n in range(16):
            out, low = weights[n // 2], n % 2 * rows
            at = pl.multiple_of(where_ref[n] * group, 16)
            first, second = own[pl.ds(at, group), :], other[pl.ds(at, group), :]
            for z in range(4):
                both = [array[z * tokens : (z + 1) * tokens, :] for array in (first, second)]
                out[low + 2 * z * tokens : low + 2 * (z + 1) * tokens, wide] = jnp.concatenate(both, 0)
            for array in (first, second):
                size = jnp.abs(array.astype(jnp.float32)).reshape(group // 8, 8, voc)
                top = jnp.maximum(top, jnp.max(size, 0))
            picked = jnp.full((CAP_ROUTE, 1), -1, jnp.int32)
            for c in range(16):
                picked = jnp.where(where_ref[n] == c, slots[c * CAP_ROUTE : (c + 1) * CAP_ROUTE, :], picked)
            out[low + 2 * group : low + rows, wide] = jnp.where(picked == columns, 1.0, 0.0).astype(jnp.bfloat16)
        largest[shard] = jnp.max(top)
        if shard == 0:
            for copy in load(1):
                copy.start()


def prepare(where, own_ids, other_ids, logits, order, group):
    voc = logits[0].shape[1]
    rows = 2 * (2 * group + CAP_ROUTE)
    vmem, smem = pl.BlockSpec(memory_space=pltpu.VMEM), pl.BlockSpec(memory_space=pltpu.SMEM)

    def kernel(where_ref, own_ids, other_ids, *refs):
        prepare_kernel(group, where_ref, own_ids, other_ids, *refs[:4], *refs[5:])

    return pl.pallas_call(
        kernel,
        in_specs=[smem, vmem, vmem] + [pl.BlockSpec(memory_space=pl.ANY)] * 5,
        out_specs=[vmem] * 8 + [smem, smem],
        out_shape=[pltpu.VMEM((rows, 2 * voc), jnp.bfloat16)] * 8
        + [jax.ShapeDtypeStruct((3,), jnp.int32), jax.ShapeDtypeStruct((2,), jnp.float32)],
        scratch_shapes=[pltpu.VMEM(logits[0].shape, logits[0].dtype)] * 2 + [pltpu.SemaphoreType.DMA((2,))],
        cost_estimate=SMALL,
        compiler_params=pltpu.CompilerParams(vmem_limit_bytes=8 * 1024 * 1024),
    )(where, own_ids, other_ids, in_hbm(logits[0]), *logits[1:], order)


def add_products(total, products):
    for weights, rows in products:
        total = total + dot_rows(weights, rows)
    return total


def dot_rows(weights, rows):
    return lax.dot_general(weights, rows, (((0,), (0,)), ((), ())), preferred_element_type=jnp.float32)


def full_embedding(rows, ids, shard, vocab, low):
    tokens = rows.shape[0] // 2
    step = pairs(lambda s, y, x, z, r: (s, (y + (x + (z + 1) // RING) // RING) % RING, (x + (z + 1) // RING) % RING, (z + 1) % RING, r))

    def body(i, state):
        current, total = state
        source = (shard - i) & 63
        here = lax.dynamic_slice_in_dim(ids, source * tokens, tokens, 1).reshape(2 * tokens, 1)
        part = lax.dynamic_slice_in_dim(current, low, HALF, 1)
        return send(current, step), total + dot_rows((here == vocab).astype(jnp.bfloat16), part)

    return lax.fori_loop(0, 64, body, (rows, jnp.zeros((vocab.shape[1], HALF), jnp.float32)))[1]


def local(acts, logit_grad, token_ids, table, moment_one, moment_two):
    section = lax.axis_index("section")
    shard = lax.axis_index("shard")
    rep = lax.axis_index("rep")
    y, x, z_hi = shard >> 4, (shard >> 2) & 3, shard & 3
    on_first = rep == 0
    second, last = pick(on_first, x, y), pick(on_first, y, x)

    own_logits = logit_grad[0]
    assert own_logits.shape[1] == VOC_SHARD
    tokens, model = acts.shape[2:]
    voc = own_logits.shape[1]
    width = model // 4
    part = voc // 4

    pieces = {}
    flips = ((1, 0), (1, 1), (0, 1), (0, 0))
    takers = jnp.stack([2 * (section ^ a) + (rep ^ b) for a, b in flips]).astype(jnp.int32)
    *quarters, own_ids = cut_quarters(takers, token_ids, acts[0, 0])
    for (a, b), block in zip(flips, quarters):
        pieces[a, b] = send(block, quad_pairs(a, b)) if (a, b) != (0, 0) else block

    other_ids = send(own_ids, quad_pairs(0, 1))
    other_logits = send(own_logits, quad_pairs(0, 1))
    logits = [own_logits, other_logits] + [send(array, pair_pairs(0, 0)) for array in (own_logits, other_logits)]

    where = jnp.stack([section, shard >> 2, z_hi, second, rep]).astype(jnp.int32)
    chunk, own_route = build_chunk(where, token_ids, other_ids, [pieces[flip] for flip in flips])

    far, down = (send(chunk, depth_pairs(step)) for step in (2, -1))
    up = send(chunk, depth_pairs(1))

    outgoing = list(spread(jnp.stack([z_hi, second]).astype(jnp.int32), own_route, [chunk, down, far, up]))
    plane = [outgoing[0], *(send(outgoing[k], second_pairs(step)) for k, step in ((3, -1), (2, 2), (1, 1)))]

    partner = pick(on_first, shard ^ 4, shard ^ 16)
    turning = [(second + k) & 3 for k in range(4)]
    order = [((last + offset) & 3, turn) for offset in range(4) for turn in turning]
    places = [pick(on_first, 4 * fixed + turn, 4 * turn + fixed) for fixed, turn in order]
    where = jnp.stack([*places, second, shard * voc, partner * voc, rep]).astype(jnp.int32)
    *weights, flags, largest = prepare(where, token_ids, other_ids, logits, outgoing[1], 4 * tokens)
    weights = [weights[2 * k : 2 * k + 2] for k in range(4)]
    overflow = flags[0] > 0

    places = lax.broadcasted_iota(jnp.int32, (1, voc), 1)
    vocab = jnp.concatenate([shard * voc + places, partner * voc + places], 1)
    def all_rows():
        ids = jnp.concatenate([token_ids, other_ids], 0)
        rows = jnp.concatenate([jnp.where(section == 0, pieces[0, b], pieces[1, b]) for b in (0, 1)], 0)
        return full_embedding(rows, ids, shard, vocab, (second & 1) * (width - HALF))

    start_total = lax.cond(
        overflow,
        all_rows,
        lambda: jnp.zeros((2 * voc, HALF), jnp.float32),
    )

    lower, upper = join(plane[0], plane[1], largest, *plane[2:]), join(plane[2], plane[3], largest, plane[1])
    before, behind = [send(lower, last_pairs(1))], [send(upper, last_pairs(-1))]
    total = add_products(start_total, [(weights[0][0], lower), (weights[0][1], upper)])
    late_lower, late_upper = again(upper, lower, upper)
    before.append(send(late_upper, last_pairs(1)))
    behind.append(send(late_lower, last_pairs(-1)))
    far = send(before[0], last_pairs(1)), send(behind[0], last_pairs(-1))
    total = add_products(total, [(weights[3][0], before[0]), (weights[1][1], behind[0])])
    total = add_products(total, [(weights[3][1], before[1]), (weights[1][0], behind[1])])
    total = add_products(total, [(weights[2][0], far[0]), (weights[2][1], far[1])])

    most = 6.0 * 2 * 64 * tokens
    bound = most * (largest + (flags[1:] > 0).astype(jnp.float32))
    bound = jnp.where(jnp.logical_or(overflow, bound <= 0), 2 * most, bound)
    scale = 32768.0 / bound

    sent = {}
    for a, b, p in ((1, 0, 0), (1, 1, 0), (1, 0, 1), (1, 1, 1), (0, 0, 1), (0, 1, 1), (0, 1, 0), (0, 0, 0)):
        row = p * voc + (2 * (section ^ a) + (rep ^ b)) * part
        block = lax.dynamic_slice_in_dim(total, row, part, 0)
        if a or p:
            block = (block * scale[p]).astype(jnp.float16)
        table_of = pair_pairs(a, b) if p else quad_pairs(a, b)
        sent[a, b, p] = send(block, table_of) if (a, b, p) != (0, 0, 0) else block

    def parts_of(a, b, unscale):
        low_first = pick(rep == b, x, y) & 1 == 0
        here, there = [
            block.astype(jnp.float32) * unscale if block.dtype == jnp.float16 else block
            for block in (sent[a, b, 0], sent[a, b, 1])
        ]
        return [jnp.where(low_first, here, there), jnp.where(low_first, there, here)[:, HALF - PARTS[1] :]]

    state = (table, moment_one, moment_two)
    across = fetch((section ^ 1).reshape(1).astype(jnp.int32), state, sent[0, 1, 0])
    unscale = 1.0 / scale[0]
    near = [2 * section + rep, 2 * section + (rep ^ 1)]
    here = jnp.stack(near * 2).astype(jnp.int32)
    blocks = [parts_of(0, b, unscale) for b in (0, 1)]
    *results, unscale = adamw_pair(here, unscale.reshape(1), *blocks, list(map(in_hbm, state)), None, across[0])
    blocks = [parts_of(1, b, unscale[:1, :1]) for b in (0, 1)]
    there = jnp.stack([2 * (section ^ 1) + rep, 2 * (section ^ 1) + (rep ^ 1), rep, rep ^ 1]).astype(jnp.int32)
    return tuple(adamw_pair(there, 1.0 / scale[:1], *blocks, across, results)[:3])


def solution(mesh):
    rows = P(("shard", "section", "rep"), None)
    return jax.shard_map(
        local,
        mesh=mesh,
        in_specs=(P("section", "rep", "shard", None), P("rep", None, "shard"), P("rep", None), rows, rows, rows),
        out_specs=(rows, rows, rows),
        check_vma=False,
    )
```

time: 110 us -> 104 us (0.945)
  waiting for transfers between devices: 33.7 us -> 21.5 us
  Pallas kernels: 17.5 us -> 21.7 us
  starting transfers between devices: 35.6 us -> 37.9 us
    ppermute x20 -> x26, waiting for transfers between devices: 33.7 us -> 21.5 us  [send(): return lax.ppermute(array, AXES, table)]
    ppermute x20 -> x26, starting transfers between devices: 35.6 us -> 37.9 us  [send(): return lax.ppermute(array, AXES, table)]
    pallas_call x1, Pallas kernels: 0.35 us -> 2.02 us  [spread(): pl.pallas_call(spread_kernel, in_specs=[pl.BlockSpec(memory_space=pltpu.S...]
    lt x2 -> x0, other arithmetic: 1.52 us -> none  [the longest x1 0.77 us: local(): own_hot = slots_of(own_chunk < voc * 64, CAP_CHUNK).astype(jnp.bfloat16)]
    mul x2 -> x4, other arithmetic: 0.06 us -> 1.44 us  [parts_of(): block.astype(jnp.float32) * unscale]
    convert_element_type x5 -> x1, other arithmetic: 0.04 us -> 1.31 us  [local(): block = (block * scale[p]).astype(jnp.float16)]
    pallas_call x5, Pallas kernels: 13 us -> 14.2 us  [the longest x2 6.5 us: adamw_pair(): pl.pallas_call(adamw_kernel, grid_spec=pltpu.PrefetchScalarGridSpec(num_s...]
    unnamed x15 -> x44, local copies, waits for them, and re-layouts: 2.54 us -> 2.73 us
  transfers between devices with their start and end apart: 20 -> 26, of which waited for: 10 -> 13; matrix products, arithmetic and copies ran while one was open for 15% -> 14% of each run, Pallas kernels for 8% -> 16%
where the time goes in v3:
time: 104 us
  starting transfers between devices  37.9 us (36%)
  Pallas kernels  21.7 us (21%)
  waiting for transfers between devices  21.5 us (21%)
  matrix products  11.4 us (11%)
  local copies, waits for them, and re-layouts  5.45 us (5%)
  other arithmetic  3.25 us (3%)
  between operations  2.43 us (2%)
    ppermute x26, starting transfers between devices, send(): return lax.ppermute(array, AXES, table)  37.9 us
    ppermute x26, waiting for transfers between devices, send(): return lax.ppermute(array, AXES, table)  21.5 us
    dot_general x8, matrix products, dot_rows(): lax.dot_general(weights, rows, (((0,), (0,)), ((), ())), preferred_elemen...  11.4 us
    pallas_call x2, Pallas kernels, adamw_pair(): pl.pallas_call(adamw_kernel, grid_spec=pltpu.PrefetchScalarGridSpec(num_s...  6.5 us
    pallas_call x1, Pallas kernels, prepare(): pl.pallas_call(kernel, in_specs=[smem, vmem, vmem] + [pl.BlockSpec(memory...  5.09 us
    unnamed x44, local copies, waits for them, and re-layouts  2.73 us
    pallas_call x2, Pallas kernels, join(): pl.pallas_call(join_kernel, in_specs=[vmem, vmem] + [pl.BlockSpec(memory_...  2.1 us
  transfers between devices with their start and end apart: 26, of which 13 were waited for; matrix products, arithmetic and copies ran while one was open for 14% of the time, Pallas kernels for 16%

profile of v3, /device:TPU:1, one launch (start us, length us, event | category | flops | bytes accessed | tf_op | source)
XLA Modules:
  0.0 103.6 jit_solution(3418268840287384641)
XLA Ops:
  0.6 3.3 %collective-permute-start.2 = (bf16[1536,384]{1,0:T(8,128)(2,1)}, bf16[1536,384]{1,0:T(8,128)(2,1)S(1)}, u32[]{:S(2)}, u32[]{:S(2)}) collective-permute-start(bf16[1536,384]{1,0:T(8,128)(2,1)} %bitcast.54), channel_id=1, source_target_pairs={{0,1},{1,0},{2,3},{3,2},{4,5},{5,4},{6,7},{7,6},{8,9},{9,8},{10,11... | collective-permute-start | bytes 3538952 | tf_op jit(solution)/shard_map/ppermute | solution.py:59
  4.0 2.7 %collective-permute-done.2.refs_1_ = bf16[1536,384]{1,0:T(8,128)(2,1)S(1)} collective-permute-done((bf16[1536,384]{1,0:T(8,128)(2,1)}, bf16[1536,384]{1,0:T(8,128)(2,1)S(1)}, u32[]{:S(2)}, u32[]{:S(2)}) %collective-permute-start.2) | collective-permute-done | bytes 1179680 | tf_op jit(solution)/shard_map/ppermute | solution.py:59
  6.7 1.6 %shard_map.85 = (bf16[24,1152]{1,0:T(8,128)(2,1)}, bf16[24,1152]{1,0:T(8,128)(2,1)}, bf16[24,1152]{1,0:T(8,128)(2,1)}, bf16[24,1152]{1,0:T(8,128)(2,1)S(1)}, s32[1,1536]{1,0:T(1,128)S(1)}) custom-call(s32[4]{0:T(128)S(1)} %pad_add_fusion.4.where_ref, s32[1,1536]{1,0:T(1,128)} %own_ids.3, bf16[24,4608]{1,0:T(8,128)(2,1)} %bitcast.57), custom_call_target="tpu_custom_call" | custom-call | flops 1024 | bytes 1024 | tf_op jit(solution)/shard_map/pallas_call | solution.py:154
  9.3 1.4 %collective-permute-start.5 = (bf16[24,1152]{1,0:T(8,128)(2,1)}, bf16[24,1152]{1,0:T(8,128)(2,1)}, u32[]{:S(2)}, u32[]{:S(2)}) collective-permute-start(bf16[24,1152]{1,0:T(8,128)(2,1)} %get-tuple-element.242), channel_id=1, source_target_pairs={{0,128},{1,129},{2,130},{3,131},{4,132},{5,133},{6,134},{7,135},{8... | collective-permute-start | bytes 165896 | tf_op jit(solution)/shard_map/ppermute | solution.py:59
  11.3 1.6 %collective-permute-done.5.refs_0_ = bf16[24,1152]{1,0:T(8,128)(2,1)} collective-permute-done((bf16[24,1152]{1,0:T(8,128)(2,1)}, bf16[24,1152]{1,0:T(8,128)(2,1)}, u32[]{:S(2)}, u32[]{:S(2)}) %collective-permute-start.5) | collective-permute-done | bytes 55328 | tf_op jit(solution)/shard_map/ppermute | solution.py:59
  12.9 2.1 %collective-permute-done.6.refs_1_ = bf16[24,1152]{1,0:T(8,128)(2,1)} collective-permute-done((bf16[24,1152]{1,0:T(8,128)(2,1)}, bf16[24,1152]{1,0:T(8,128)(2,1)}, u32[]{:S(2)}, u32[]{:S(2)}) %collective-permute-start.6) | collective-permute-done | bytes 55328 | tf_op jit(solution)/shard_map/ppermute | solution.py:59
  15.0 1.7 %shard_map.86 = (bf16[64,1152]{1,0:T(8,128)(2,1)S(1)}, bf16[128,64]{1,0:T(8,128)(2,1)S(1)}) custom-call(s32[5]{0:T(128)S(1)} %stack.145.where_ref, s32[1,1536]{1,0:T(1,128)} %own_ids.3, s32[1,1536]{1,0:T(1,128)S(1)} %collective-permute-done.1.other_ids, bf16[24,1152]{1,0:T(8,128)(2,1)} %collective-permute-done.5.refs_0_, ...), custom_call_target="tpu_custom_call" | custom-call | flops 1024 | bytes 1024 | tf_op jit(solution)/shard_map/pallas_call | solution.py:235
  16.7 5.5 %collective-permute-start.8 = (bf16[64,1152]{1,0:T(8,128)(2,1)S(1)}, bf16[64,1152]{1,0:T(8,128)(2,1)S(1)}, u32[]{:S(2)}, u32[]{:S(2)}) collective-permute-start(bf16[64,1152]{1,0:T(8,128)(2,1)S(1)} %get-tuple-element.247.refs_0_), channel_id=1, source_target_pairs={{0,6},{1,7},{2,0},{3,1},{4,2},{5,3},{6,4},{7,5},{8,14},{9,15},{10,... | collective-permute-start | bytes 442376 | tf_op jit(solution)/shard_map/ppermute | solution.py:59
  23.2 2.3 %collective-permute-start.10 = (bf16[64,1152]{1,0:T(8,128)(2,1)S(1)}, bf16[64,1152]{1,0:T(8,128)(2,1)S(1)}, u32[]{:S(2)}, u32[]{:S(2)}) collective-permute-start(bf16[64,1152]{1,0:T(8,128)(2,1)S(1)} %get-tuple-element.247.refs_0_), channel_id=1, source_target_pairs={{0,2},{1,3},{2,4},{3,5},{4,6},{5,7},{6,0},{7,1},{8,10},{9,11},{10,... | collective-permute-start | bytes 442376 | tf_op jit(solution)/shard_map/ppermute | solution.py:59
  25.5 1.6 %collective-permute-done.8.refs_1_ = bf16[64,1152]{1,0:T(8,128)(2,1)S(1)} collective-permute-done((bf16[64,1152]{1,0:T(8,128)(2,1)S(1)}, bf16[64,1152]{1,0:T(8,128)(2,1)S(1)}, u32[]{:S(2)}, u32[]{:S(2)}) %collective-permute-start.8) | collective-permute-done | bytes 147488 | tf_op jit(solution)/shard_map/ppermute | solution.py:59
  27.0 7.3 %collective-permute-done.9.refs_2_ = bf16[64,1152]{1,0:T(8,128)(2,1)S(1)} collective-permute-done((bf16[64,1152]{1,0:T(8,128)(2,1)S(1)}, bf16[64,1152]{1,0:T(8,128)(2,1)S(1)}, u32[]{:S(2)}, u32[]{:S(2)}) %collective-permute-start.9) | collective-permute-done | bytes 147488 | tf_op jit(solution)/shard_map/ppermute | solution.py:59
  34.4 2.0 %shard_map.87 = (bf16[224,640]{1,0:T(8,128)(2,1)S(1)}, bf16[224,640]{1,0:T(8,128)(2,1)}, bf16[224,640]{1,0:T(8,128)(2,1)}, bf16[224,640]{1,0:T(8,128)(2,1)}) custom-call(s32[2]{0:T(128)S(1)} %pad_add_fusion.5.where_ref, bf16[128,64]{1,0:T(8,128)(2,1)S(1)} %get-tuple-element.246.route, bf16[64,1152]{1,0:T(8,128)(2,1)S(1)} %get-tuple-element.247.refs_0_, ...), custom_call_target="tpu_custom_call" | custom-call | flops 1024 | bytes 1024 | tf_op jit(solution)/shard_map/pallas_call | solution.py:267
  37.2 2.7 %collective-permute-start.11 = (bf16[224,640]{1,0:T(8,128)(2,1)}, bf16[224,640]{1,0:T(8,128)(2,1)}, u32[]{:S(2)}, u32[]{:S(2)}) collective-permute-start(bf16[224,640]{1,0:T(8,128)(2,1)} %get-tuple-element.253), channel_id=1, source_target_pairs={{0,24},{1,97},{2,26},{3,99},{4,28},{5,101},{6,30},{7,103},{8,0},{9... | collective-permute-start | bytes 860168 | tf_op jit(solution)/shard_map/ppermute | solution.py:59
  41.1 5.1 %shard_map.88 = (bf16[448,768]{1,0:T(8,128)(2,1)S(1)}, bf16[448,768]{1,0:T(8,128)(2,1)S(1)}, bf16[448,768]{1,0:T(8,128)(2,1)S(1)}, bf16[448,768]{1,0:T(8,128)(2,...) custom-call(s32[20]{0:T(128)S(1)} %stack.137.where_ref, ...), custom_call_target="tpu_custom_call" | custom-call | flops 1024 | bytes 1024 | tf_op jit(solution)/shard_map/pallas_call | solution.py:392
  47.6 3.0 %collective-permute-done.13.refs_2_.second = bf16[224,640]{1,0:T(8,128)(2,1)} collective-permute-done((bf16[224,640]{1,0:T(8,128)(2,1)}, bf16[224,640]{1,0:T(8,128)(2,1)}, u32[]{:S(2)}, u32[]{:S(2)}) %collective-permute-start.13) | collective-permute-done | bytes 286752 | tf_op jit(solution)/shard_map/ppermute | solution.py:59
  50.6 1.1 %shard_map.90._.refs_1_ = bf16[448,640]{1,0:T(8,128)(2,1)S(1)} custom-call(bf16[224,640]{1,0:T(8,128)(2,1)} %collective-permute-done.12.refs_1_.first, bf16[224,640]{1,0:T(8,128)(2,1)} %collective-permute-done.13.refs_2_.second, f32[2]{0:T(128)S(1)} %get-tuple-element.250.refs_0_, bf16[224,640]{1,0:T(8,128)(2,1)} %collective-permute-done.11.second.refs_1_), custom_call_target="tpu_custom_call" | custom-call | flops 1024 | bytes 1024 | tf_op jit(solution)/shard_map/pallas_call | solution.py:288
  54.1 2.6 %collective-permute-start.15 = (bf16[448,640]{1,0:T(8,128)(2,1)S(1)}, bf16[448,640]{1,0:T(8,128)(2,1)}, u32[]{:S(2)}, u32[]{:S(2)}) collective-permute-start(bf16[448,640]{1,0:T(8,128)(2,1)S(1)} %shard_map.90._.refs_1_), channel_id=1, source_target_pairs={{0,96},{1,25},{2,98},{3,27},{4,100},{5,29},{6,102},{7,31},{8,104},... | collective-permute-start | bytes 1720328 | tf_op jit(solution)/shard_map/ppermute | solution.py:59
  58.9 1.4 %conditional.1 = (f32[768,640]{1,0:T(8,128)}) conditional(s32[]{:T(128)} %convert_element_type.46, () %tuple.35, (s32[]{:T(128)}, bf16[24,1152]{1,0:T(8,128)(2,1)S(1)}, bf16[24,1152]{1,0:T(8,128)(2,1)}, bf16[24,1152]{1,0:T(8,128)(2,1)}, bf16[24,1152]{1,0:T(8,128)(2,1)}, /*index=5*/s32[1,1536]{1,0:T(1,128)S(1)}, s32[1,1536]{1,0:T(1,128)S(1)}, ...), branch_computations={%region_0.1_spmd, %region_1.4_spmd} | conditional | flops 48485392 | bytes 5246637 | solution.py:479
  58.9 1.4 %broadcast.28 = f32[768,640]{1,0:T(8,128)} broadcast(f32[]{:T(128)} %constant.84.clone), dimensions={} | broadcast | bytes 1966084 | tf_op jit(solution)/shard_map/broadcast.5
  63.4 3.5 %collective-permute-start.19 = (bf16[448,640]{1,0:T(8,128)(2,1)}, bf16[448,640]{1,0:T(8,128)(2,1)S(1)}, u32[]{:S(2)}, u32[]{:S(2)}) collective-permute-start(bf16[448,640]{1,0:T(8,128)(2,1)} %collective-permute-done.15), channel_id=1, source_target_pairs={{0,96},{1,25},{2,98},{3,27},{4,100},{5,29},{6,102},{7,31},{8,104},... | collective-permute-start | bytes 1720328 | tf_op jit(solution)/shard_map/ppermute | solution.py:59
  66.8 1.9 %fusion.12 = f32[768,640]{1,0:T(8,128)S(1)} fusion(bf16[448,768]{1,0:T(8,128)(2,1)S(1)} %copy-done.11, bf16[448,640]{1,0:T(8,128)(2,1)} %collective-permute-done.15), kind=kOutput, calls=%fused_computation.50 | convolution fusion | flops 440401920 | bytes 3227648 | tf_op jit(solution)/shard_map/dot_general | solution.py:411
  68.7 1.9 %fusion.11 = f32[768,640]{1,0:T(8,128)S(1)} fusion(bf16[448,768]{1,0:T(8,128)(2,1)S(1)} %copy-done.9, bf16[448,640]{1,0:T(8,128)(2,1)} %collective-permute-done.14), kind=kOutput, calls=%fused_computation.49 | convolution fusion | flops 440401920 | bytes 3227648 | tf_op jit(solution)/shard_map/dot_general | solution.py:411
  70.7 1.9 %fusion.14 = f32[768,640]{1,0:T(8,128)S(1)} fusion(bf16[448,768]{1,0:T(8,128)(2,1)S(1)} %copy-done.7, bf16[448,640]{1,0:T(8,128)(2,1)} %collective-permute-done.17), kind=kOutput, calls=%fused_computation.52 | convolution fusion | flops 440401920 | bytes 3227648 | tf_op jit(solution)/shard_map/dot_general | solution.py:411
  72.7 1.9 %fusion.13 = f32[768,640]{1,0:T(8,128)S(1)} fusion(bf16[448,768]{1,0:T(8,128)(2,1)S(1)} %copy-done.5, bf16[448,640]{1,0:T(8,128)(2,1)} %collective-permute-done.16), kind=kOutput, calls=%fused_computation.51 | convolution fusion | flops 440401920 | bytes 3227648 | tf_op jit(solution)/shard_map/dot_general | solution.py:411
  76.4 1.3 %add_add_fusion = f32[768,640]{1,0:T(8,128)S(1)} fusion(f32[768,640]{1,0:T(8,128)S(1)} %fusion.15, f32[768,640]{1,0:T(8,128)S(1)} %fusion.14, f32[768,640]{1,0:T(8,128)S(1)} %fusion.13, f32[768,640]{1,0:T(8,128)S(1)} %fusion.12, f32[768,640]{1,0:T(8,128)S(1)} %fusion.11, f32[768,640]{1,0:T(8,128)S(1)} %fusion.10, f32[768,640]{1,0:T(8,128)S(1)} %copy-done.20, ...), kind=kOutput, calls=%fused_computation.11 | convolution fusion | flops 444334080 | bytes 18956288 | tf_op jit(solution)/shard_map/dot_general | solution.py:411
  77.7 1.3 %multiply_convert_fusion = (f16[96,640]{1,0:T(8,128)(2,1)S(1)}, f16[96,640]{1,0:T(8,128)(2,1)S(1)}, f16[96,640]{1,0:T(8,128)(2,1)S(1)}, f16[96,640]{1,0:T(8,128)...) fusion(f32[768,640]{1,0:T(8,128)S(1)} %add_add_fusion, ...), kind=kLoop, calls=%fused_computation.13 | loop fusion | flops 737280 | bytes 2703396 | tf_op jit(solution)/shard_map/convert_element_type | solution.py:506
  80.8 4.7 %collective-permute-start.24 = (f16[96,640]{1,0:T(8,128)(2,1)S(1)}, f16[96,640]{1,0:T(8,128)(2,1)S(1)}, u32[]{:S(2)}, u32[]{:S(2)}) collective-permute-start(f16[96,640]{1,0:T(8,128)(2,1)S(1)} %get-tuple-element.316), channel_id=1, source_target_pairs={{0,136},{1,161},{2,138},{3,163},{4,140},{5,165},{6,142},{7,167},{8... | collective-permute-start | bytes 368648 | tf_op jit(solution)/shard_map/ppermute | solution.py:59
  85.5 4.3 %collective-permute-start.23 = (f16[96,640]{1,0:T(8,128)(2,1)S(1)}, f16[96,640]{1,0:T(8,128)(2,1)S(1)}, u32[]{:S(2)}, u32[]{:S(2)}) collective-permute-start(f16[96,640]{1,0:T(8,128)(2,1)S(1)} %get-tuple-element.317), channel_id=1, source_target_pairs={{0,9},{1,32},{2,11},{3,34},{4,13},{5,36},{6,15},{7,38},{8,1},{9,40... | collective-permute-start | bytes 368648 | tf_op jit(solution)/shard_map/ppermute | solution.py:59
  89.8 2.5 %collective-permute-start.26 = (f16[96,640]{1,0:T(8,128)(2,1)S(1)}, f16[96,640]{1,0:T(8,128)(2,1)S(1)}, u32[]{:S(2)}, u32[]{:S(2)}) collective-permute-start(f16[96,640]{1,0:T(8,128)(2,1)S(1)} %get-tuple-element.314), channel_id=1, source_target_pairs={{0,137},{1,160},{2,139},{3,162},{4,141},{5,164},{6,143},{7,166},{8... | collective-permute-start | bytes 368648 | tf_op jit(solution)/shard_map/ppermute | solution.py:59
  93.0 1.7 %shard_map.92 = (f32[96,2304]{1,0:T(8,128)S(1)}, f32[96,2304]{1,0:T(8,128)S(1)}, f32[96,2304]{1,0:T(8,128)S(1)}) custom-call(s32[1]{0:T(128)} %bitcast.34.where_ref, f32[96,4608]{1,0:T(8,128)} %refs_4_.1, f32[96,4608]{1,0:T(8,128)} %refs_5_.1, f32[96,4608]{1,0:T(8,128)} %refs_6_.1, f32[96,640]{1,0:T(8,128)S(1)} %collective-permute-done.22.refs_3_), custom_call_target="tpu_custom_call" | custom-call | flops 1024 | bytes 1024 | tf_op jit(solution)/shard_map/pallas_call | solution.py:133
  94.7 3.8 %shard_map.93 = (f32[96,4608]{1,0:T(8,128)}, f32[96,4608]{1,0:T(8,128)}, f32[96,4608]{1,0:T(8,128)}, f32[8,128]{1,0:T(8,128)S(1)}) custom-call(s32[4]{0:T(128)S(1)} %pad_add_fusion.6.where_ref, f32[1]{0:T(128)} %bitcast.32.held_ref, f32[96,640]{1,0:T(8,128)S(1)} %get-tuple-element.330.refs_0_, f32[96,512]{1,0:T(8,128)S(1)} %dynamic-slice_select_fusion.1.refs_1_, ...), custom_call_target="tpu_custom_call" | custom-call | flops 1024 | bytes 1024 | tf_op jit(solution)/shard_map/pallas_call | solution.py:106
  100.8 2.7 %shard_map.94 = (f32[96,4608]{1,0:T(8,128)}, f32[96,4608]{1,0:T(8,128)}, f32[96,4608]{1,0:T(8,128)}, f32[8,128]{1,0:T(8,128)}) custom-call(s32[4]{0:T(128)S(1)} %pad_add_fusion.2.where_ref, f32[1]{0:T(128)S(6)} %div.10.held_ref, f32[96,640]{1,0:T(8,128)S(1)} %get-tuple-element.325.refs_0_, ...), custom_call_target="tpu_custom_call", output_to_operand_aliasing={{0}: (9, {}), {1}: (10, {}), {2}: (11, {})} | custom-call | flops 1024 | bytes 1024 | tf_op jit(solution)/shard_map/pallas_call | solution.py:106
  (104 shorter events, 18.6 us)
Async XLA Ops:
  0.6 6.0 %collective-permute-start.2 = (bf16[1536,384]{1,0:T(8,128)(2,1)}, bf16[1536,384]{1,0:T(8,128)(2,1)S(1)}, u32[]{:S(2)}, u32[]{:S(2)}) collective-permute-start(bf16[1536,384]{1,0:T(8,128)(2,1)} %bitcast.54), channel_id=1, source_target_pairs={{0,1},{1,0},{2,3},{3,2},{4,5},{5,4},{6,7},{7,6},{8,9},{9,8},{10,11... | collective-permute-start | bytes 3538952 | tf_op jit(solution)/shard_map/ppermute | solution.py:59
  4.0 37.1 %collective-permute-start.3 = (bf16[1536,384]{1,0:T(8,128)(2,1)}, bf16[1536,384]{1,0:T(8,128)(2,1)S(1)}, u32[]{:S(2)}, u32[]{:S(2)}) collective-permute-start(bf16[1536,384]{1,0:T(8,128)(2,1)} %bitcast.55), channel_id=1, source_target_pairs={{0,8},{1,33},{2,10},{3,35},{4,12},{5,37},{6,14},{7,39},{8,0},{9,41... | collective-permute-start | bytes 3538952 | tf_op jit(solution)/shard_map/ppermute | solution.py:59
  6.6 34.5 %collective-permute-start.4 = (bf16[1536,384]{1,0:T(8,128)(2,1)S(1)}, bf16[1536,384]{1,0:T(8,128)(2,1)S(1)}, u32[]{:S(2)}, u32[]{:S(2)}) collective-permute-start(bf16[1536,384]{1,0:T(8,128)(2,1)S(1)} %collective-permute-done.2.refs_1_), channel_id=1, source_target_pairs={{0,8},{1,33},{2,10},{3,35},{4,12},{5,37},{6,14},{7,39},{8,0},{9,41... | collective-permute-start | bytes 3538952 | tf_op jit(solution)/shard_map/ppermute | solution.py:59
  9.0 2.2 %collective-permute-start.1 = (s32[1,1536]{1,0:T(1,128)S(1)}, s32[1,1536]{1,0:T(1,128)S(1)}, u32[]{:S(2)}, u32[]{:S(2)}) collective-permute-start(s32[1,1536]{1,0:T(1,128)S(1)} %get-tuple-element.241), channel_id=1, source_target_pairs={{0,1},{1,0},{2,3},{3,2},{4,5},{5,4},{6,7},{7,6},{8,9},{9,8},{10,11... | collective-permute-start | bytes 18440 | tf_op jit(solution)/shard_map/ppermute | solution.py:59
  9.3 3.5 %collective-permute-start.5 = (bf16[24,1152]{1,0:T(8,128)(2,1)}, bf16[24,1152]{1,0:T(8,128)(2,1)}, u32[]{:S(2)}, u32[]{:S(2)}) collective-permute-start(bf16[24,1152]{1,0:T(8,128)(2,1)} %get-tuple-element.242), channel_id=1, source_target_pairs={{0,128},{1,129},{2,130},{3,131},{4,132},{5,133},{6,134},{7,135},{8... | collective-permute-start | bytes 165896 | tf_op jit(solution)/shard_map/ppermute | solution.py:59
  10.7 4.3 %collective-permute-start.6 = (bf16[24,1152]{1,0:T(8,128)(2,1)}, bf16[24,1152]{1,0:T(8,128)(2,1)}, u32[]{:S(2)}, u32[]{:S(2)}) collective-permute-start(bf16[24,1152]{1,0:T(8,128)(2,1)} %get-tuple-element.243), channel_id=1, source_target_pairs={{0,129},{1,128},{2,131},{3,130},{4,133},{5,132},{6,135},{7,134},{8... | collective-permute-start | bytes 165896 | tf_op jit(solution)/shard_map/ppermute | solution.py:59
  11.1 3.9 %collective-permute-start.7 = (bf16[24,1152]{1,0:T(8,128)(2,1)}, bf16[24,1152]{1,0:T(8,128)(2,1)}, u32[]{:S(2)}, u32[]{:S(2)}) collective-permute-start(bf16[24,1152]{1,0:T(8,128)(2,1)} %get-tuple-element.244), channel_id=1, source_target_pairs={{0,1},{1,0},{2,3},{3,2},{4,5},{5,4},{6,7},{7,6},{8,9},{9,8},{10,11... | collective-permute-start | bytes 165896 | tf_op jit(solution)/shard_map/ppermute | solution.py:59
  16.7 10.4 %collective-permute-start.8 = (bf16[64,1152]{1,0:T(8,128)(2,1)S(1)}, bf16[64,1152]{1,0:T(8,128)(2,1)S(1)}, u32[]{:S(2)}, u32[]{:S(2)}) collective-permute-start(bf16[64,1152]{1,0:T(8,128)(2,1)S(1)} %get-tuple-element.247.refs_0_), channel_id=1, source_target_pairs={{0,6},{1,7},{2,0},{3,1},{4,2},{5,3},{6,4},{7,5},{8,14},{9,15},{10,... | collective-permute-start | bytes 442376 | tf_op jit(solution)/shard_map/ppermute | solution.py:59
  22.2 12.1 %collective-permute-start.9 = (bf16[64,1152]{1,0:T(8,128)(2,1)S(1)}, bf16[64,1152]{1,0:T(8,128)(2,1)S(1)}, u32[]{:S(2)}, u32[]{:S(2)}) collective-permute-start(bf16[64,1152]{1,0:T(8,128)(2,1)S(1)} %get-tuple-element.247.refs_0_), channel_id=1, source_target_pairs={{0,4},{1,5},{2,6},{3,7},{4,0},{5,1},{6,2},{7,3},{8,12},{9,13},{10,... | collective-permute-start | bytes 442376 | tf_op jit(solution)/shard_map/ppermute | solution.py:59
  23.2 11.3 %collective-permute-start.10 = (bf16[64,1152]{1,0:T(8,128)(2,1)S(1)}, bf16[64,1152]{1,0:T(8,128)(2,1)S(1)}, u32[]{:S(2)}, u32[]{:S(2)}) collective-permute-start(bf16[64,1152]{1,0:T(8,128)(2,1)S(1)} %get-tuple-element.247.refs_0_), channel_id=1, source_target_pairs={{0,2},{1,3},{2,4},{3,5},{4,6},{5,7},{6,0},{7,1},{8,10},{9,11},{10,... | collective-permute-start | bytes 442376 | tf_op jit(solution)/shard_map/ppermute | solution.py:59
  37.2 9.9 %collective-permute-start.11 = (bf16[224,640]{1,0:T(8,128)(2,1)}, bf16[224,640]{1,0:T(8,128)(2,1)}, u32[]{:S(2)}, u32[]{:S(2)}) collective-permute-start(bf16[224,640]{1,0:T(8,128)(2,1)} %get-tuple-element.253), channel_id=1, source_target_pairs={{0,24},{1,97},{2,26},{3,99},{4,28},{5,101},{6,30},{7,103},{8,0},{9... | collective-permute-start | bytes 860168 | tf_op jit(solution)/shard_map/ppermute | solution.py:59
  39.9 7.6 %collective-permute-start.12 = (bf16[224,640]{1,0:T(8,128)(2,1)}, bf16[224,640]{1,0:T(8,128)(2,1)}, u32[]{:S(2)}, u32[]{:S(2)}) collective-permute-start(bf16[224,640]{1,0:T(8,128)(2,1)} %get-tuple-element.254), channel_id=1, source_target_pairs={{0,16},{1,65},{2,18},{3,67},{4,20},{5,69},{6,22},{7,71},{8,24},{9,... | collective-permute-start | bytes 860168 | tf_op jit(solution)/shard_map/ppermute | solution.py:59
  40.3 10.3 %collective-permute-start.13 = (bf16[224,640]{1,0:T(8,128)(2,1)}, bf16[224,640]{1,0:T(8,128)(2,1)}, u32[]{:S(2)}, u32[]{:S(2)}) collective-permute-start(bf16[224,640]{1,0:T(8,128)(2,1)} %get-tuple-element.248.refs_4_), channel_id=1, source_target_pairs={{0,8},{1,33},{2,10},{3,35},{4,12},{5,37},{6,14},{7,39},{8,16},{9,4... | collective-permute-start | bytes 860168 | tf_op jit(solution)/shard_map/ppermute | solution.py:59
  41.1 10.6 %copy-start.17 = (bf16[224,640]{1,0:T(8,128)(2,1)S(1)}, bf16[224,640]{1,0:T(8,128)(2,1)}, u32[]{:S(2)}) copy-start(bf16[224,640]{1,0:T(8,128)(2,1)} %copy-done.16) | copy-start | bytes 860164
  47.1 6.9 %copy-start.4 = (bf16[448,768]{1,0:T(8,128)(2,1)}, bf16[448,768]{1,0:T(8,128)(2,1)S(1)}, u32[]{:S(2)}) copy-start(bf16[448,768]{1,0:T(8,128)(2,1)S(1)} %get-tuple-element.258) | copy-start | bytes 2064388
  47.1 6.9 %copy-start.6 = (bf16[448,768]{1,0:T(8,128)(2,1)}, bf16[448,768]{1,0:T(8,128)(2,1)S(1)}, u32[]{:S(2)}) copy-start(bf16[448,768]{1,0:T(8,128)(2,1)S(1)} %get-tuple-element.260) | copy-start | bytes 2064388
  47.1 6.9 %copy-start.8 = (bf16[448,768]{1,0:T(8,128)(2,1)}, bf16[448,768]{1,0:T(8,128)(2,1)S(1)}, u32[]{:S(2)}) copy-start(bf16[448,768]{1,0:T(8,128)(2,1)S(1)} %get-tuple-element.256) | copy-start | bytes 2064388
  47.1 6.9 %copy-start.10 = (bf16[448,768]{1,0:T(8,128)(2,1)}, bf16[448,768]{1,0:T(8,128)(2,1)S(1)}, u32[]{:S(2)}) copy-start(bf16[448,768]{1,0:T(8,128)(2,1)S(1)} %get-tuple-element.257) | copy-start | bytes 2064388
  47.1 6.9 %copy-start.12 = (bf16[448,768]{1,0:T(8,128)(2,1)}, bf16[448,768]{1,0:T(8,128)(2,1)S(1)}, u32[]{:S(2)}) copy-start(bf16[448,768]{1,0:T(8,128)(2,1)S(1)} %get-tuple-element.251) | copy-start | bytes 2064388
  52.7 10.4 %collective-permute-start.14 = (bf16[448,640]{1,0:T(8,128)(2,1)S(1)}, bf16[448,640]{1,0:T(8,128)(2,1)}, u32[]{:S(2)}, u32[]{:S(2)}) collective-permute-start(bf16[448,640]{1,0:T(8,128)(2,1)S(1)} %shard_map.89.refs_0_), channel_id=1, source_target_pairs={{0,32},{1,9},{2,34},{3,11},{4,36},{5,13},{6,38},{7,15},{8,40},{9,1... | collective-permute-start | bytes 1720328 | tf_op jit(solution)/shard_map/ppermute | solution.py:59
  54.1 9.3 %collective-permute-start.15 = (bf16[448,640]{1,0:T(8,128)(2,1)S(1)}, bf16[448,640]{1,0:T(8,128)(2,1)}, u32[]{:S(2)}, u32[]{:S(2)}) collective-permute-start(bf16[448,640]{1,0:T(8,128)(2,1)S(1)} %shard_map.90._.refs_1_), channel_id=1, source_target_pairs={{0,96},{1,25},{2,98},{3,27},{4,100},{5,29},{6,102},{7,31},{8,104},... | collective-permute-start | bytes 1720328 | tf_op jit(solution)/shard_map/ppermute | solution.py:59
  57.4 13.3 %collective-permute-start.17 = (bf16[448,640]{1,0:T(8,128)(2,1)}, bf16[448,640]{1,0:T(8,128)(2,1)}, u32[]{:S(2)}, u32[]{:S(2)}) collective-permute-start(bf16[448,640]{1,0:T(8,128)(2,1)} %get-tuple-element.261), channel_id=1, source_target_pairs={{0,96},{1,25},{2,98},{3,27},{4,100},{5,29},{6,102},{7,31},{8,104},... | collective-permute-start | bytes 1720328 | tf_op jit(solution)/shard_map/ppermute | solution.py:59
  58.0 14.6 %collective-permute-start.16 = (bf16[448,640]{1,0:T(8,128)(2,1)S(1)}, bf16[448,640]{1,0:T(8,128)(2,1)}, u32[]{:S(2)}, u32[]{:S(2)}) collective-permute-start(bf16[448,640]{1,0:T(8,128)(2,1)S(1)} %get-tuple-element.259), channel_id=1, source_target_pairs={{0,32},{1,9},{2,34},{3,11},{4,36},{5,13},{6,38},{7,15},{8,40},{9,1... | collective-permute-start | bytes 1720328 | tf_op jit(solution)/shard_map/ppermute | solution.py:59
  63.2 12.2 %collective-permute-start.18 = (bf16[448,640]{1,0:T(8,128)(2,1)}, bf16[448,640]{1,0:T(8,128)(2,1)S(1)}, u32[]{:S(2)}, u32[]{:S(2)}) collective-permute-start(bf16[448,640]{1,0:T(8,128)(2,1)} %collective-permute-done.14), channel_id=1, source_target_pairs={{0,32},{1,9},{2,34},{3,11},{4,36},{5,13},{6,38},{7,15},{8,40},{9,1... | collective-permute-start | bytes 1720328 | tf_op jit(solution)/shard_map/ppermute | solution.py:59
  63.4 12.8 %collective-permute-start.19 = (bf16[448,640]{1,0:T(8,128)(2,1)}, bf16[448,640]{1,0:T(8,128)(2,1)S(1)}, u32[]{:S(2)}, u32[]{:S(2)}) collective-permute-start(bf16[448,640]{1,0:T(8,128)(2,1)} %collective-permute-done.15), channel_id=1, source_target_pairs={{0,96},{1,25},{2,98},{3,27},{4,100},{5,29},{6,102},{7,31},{8,104},... | collective-permute-start | bytes 1720328 | tf_op jit(solution)/shard_map/ppermute | solution.py:59
  79.0 10.8 %collective-permute-start.21 = (f16[96,640]{1,0:T(8,128)(2,1)S(1)}, f16[96,640]{1,0:T(8,128)(2,1)S(1)}, u32[]{:S(2)}, u32[]{:S(2)}) collective-permute-start(f16[96,640]{1,0:T(8,128)(2,1)S(1)} %get-tuple-element.319), channel_id=1, source_target_pairs={{0,8},{1,33},{2,10},{3,35},{4,12},{5,37},{6,14},{7,39},{8,0},{9,41... | collective-permute-start | bytes 368648 | tf_op jit(solution)/shard_map/ppermute | solution.py:59
  80.8 18.3 %collective-permute-start.24 = (f16[96,640]{1,0:T(8,128)(2,1)S(1)}, f16[96,640]{1,0:T(8,128)(2,1)S(1)}, u32[]{:S(2)}, u32[]{:S(2)}) collective-permute-start(f16[96,640]{1,0:T(8,128)(2,1)S(1)} %get-tuple-element.316), channel_id=1, source_target_pairs={{0,136},{1,161},{2,138},{3,163},{4,140},{5,165},{6,142},{7,167},{8... | collective-permute-start | bytes 368648 | tf_op jit(solution)/shard_map/ppermute | solution.py:59
  85.5 7.4 %collective-permute-start.23 = (f16[96,640]{1,0:T(8,128)(2,1)S(1)}, f16[96,640]{1,0:T(8,128)(2,1)S(1)}, u32[]{:S(2)}, u32[]{:S(2)}) collective-permute-start(f16[96,640]{1,0:T(8,128)(2,1)S(1)} %get-tuple-element.317), channel_id=1, source_target_pairs={{0,9},{1,32},{2,11},{3,34},{4,13},{5,36},{6,15},{7,38},{8,1},{9,40... | collective-permute-start | bytes 368648 | tf_op jit(solution)/shard_map/ppermute | solution.py:59
  89.8 3.1 %collective-permute-start.22 = (f32[96,640]{1,0:T(8,128)S(1)}, f32[96,640]{1,0:T(8,128)S(1)}, u32[]{:S(2)}, u32[]{:S(2)}) collective-permute-start(f32[96,640]{1,0:T(8,128)S(1)} %get-tuple-element.318), channel_id=1, source_target_pairs={{0,1},{1,0},{2,3},{3,2},{4,5},{5,4},{6,7},{7,6},{8,9},{9,8},{10,11... | collective-permute-start | bytes 737288 | tf_op jit(solution)/shard_map/ppermute | solution.py:59
  89.8 9.3 %collective-permute-start.20 = (f16[96,640]{1,0:T(8,128)(2,1)S(1)}, f16[96,640]{1,0:T(8,128)(2,1)S(1)}, u32[]{:S(2)}, u32[]{:S(2)}) collective-permute-start(f16[96,640]{1,0:T(8,128)(2,1)S(1)} %get-tuple-element.320), channel_id=1, source_target_pairs={{0,128},{1,129},{2,130},{3,131},{4,132},{5,133},{6,134},{7,135},{8... | collective-permute-start | bytes 368648 | tf_op jit(solution)/shard_map/ppermute | solution.py:59
  89.8 10.0 %collective-permute-start.26 = (f16[96,640]{1,0:T(8,128)(2,1)S(1)}, f16[96,640]{1,0:T(8,128)(2,1)S(1)}, u32[]{:S(2)}, u32[]{:S(2)}) collective-permute-start(f16[96,640]{1,0:T(8,128)(2,1)S(1)} %get-tuple-element.314), channel_id=1, source_target_pairs={{0,137},{1,160},{2,139},{3,162},{4,141},{5,164},{6,143},{7,166},{8... | collective-permute-start | bytes 368648 | tf_op jit(solution)/shard_map/ppermute | solution.py:59
  92.9 7.2 %collective-permute-start.25 = (f16[96,640]{1,0:T(8,128)(2,1)S(1)}, f16[96,640]{1,0:T(8,128)(2,1)S(1)}, u32[]{:S(2)}, u32[]{:S(2)}) collective-permute-start(f16[96,640]{1,0:T(8,128)(2,1)S(1)} %get-tuple-element.315), channel_id=1, source_target_pairs={{0,129},{1,128},{2,131},{3,130},{4,133},{5,132},{6,135},{7,134},{8... | collective-permute-start | bytes 368648 | tf_op jit(solution)/shard_map/ppermute | solution.py:59
  (16 other events, 54.3 us)

commit v4 on v3

--- a/solution.py
+++ b/solution.py
@@ -91,7 +91,7 @@
     rows, width = first[0].shape[0], sum(PARTS)
     inner = pl.BlockSpec((rows, width), lambda i, where_ref: (0, where_ref[2 + i]))
     wide = pl.BlockSpec((rows, width), lambda i, where_ref: (0, where_ref[i]))
-    small = pl.BlockSpec((8, 128), lambda i, where_ref: (0, 0))
+    small = pl.BlockSpec((1, 1), lambda i, where_ref: (0, 0))
     anywhere = pl.BlockSpec(memory_space=pl.ANY)
     blocks = [*first, *second]
     specs = [pl.BlockSpec(memory_space=pltpu.SMEM)]
@@ -109,7 +109,7 @@
             num_scalar_prefetch=1, grid=(2,), in_specs=specs, out_specs=[wide] * 3 + [small]
         ),
         out_shape=[jax.ShapeDtypeStruct((rows, 4 * width), jnp.float32)] * 3
-        + [jax.ShapeDtypeStruct((8, 128), jnp.float32)],
+        + [jax.ShapeDtypeStruct((1, 1), jnp.float32)],
         input_output_aliases=aliases,
         cost_estimate=SMALL,
         compiler_params=pltpu.CompilerParams(vmem_limit_bytes=10 * 1024 * 1024),
@@ -182,7 +182,12 @@
 
 
 def chunk_kernel(where_ref, own_ids, other_ids, *refs):
-    pieces, chunk, route = refs[:4], refs[4], refs[5]
+    pieces, logits, (chunk, route, copied), (held, sems) = refs[:4], refs[4:6], refs[6:9], refs[9:]
+    tall = logits[0].shape[0]
+    loads = [pltpu.make_async_copy(array, held.at[k], sems.at[k]) for k, array in enumerate(logits)]
+    stores = [pltpu.make_async_copy(held.at[k], copied.at[pl.ds(k * tall, tall)], sems.at[2 + k]) for k in range(2)]
+    for load in loads:
+        load.start()
     section, column, z_hi, second, rep = (where_ref[k] for k in range(5))
     tokens, width = pieces[0].shape
     here, there = (pieces[3], pieces[2]), (pieces[0], pieces[1])
@@ -190,6 +195,9 @@
     cotangent = [jnp.where(section == 0, here[b][...], there[b][...]) for b in (0, 1)]
     chunk[: 2 * tokens, :] = jnp.concatenate(hidden, 0)
 
+    for load, store in zip(loads, stores):
+        load.wait()
+        store.start()
     ids = by_column(own_ids, other_ids, 4 * tokens)
     size = ids.shape[1]
     rows = lax.broadcasted_iota(jnp.int32, ids.shape, 0)
@@ -227,22 +235,26 @@
         route[d * CAP_ROUTE : (d + 1) * CAP_ROUTE, :] = jnp.dot(
             going, places, preferred_element_type=jnp.float32
         ).astype(jnp.bfloat16)
-
-
-def build_chunk(where, own_ids, other_ids, pieces):
+    for store in stores:
+        store.wait()
+
+
+def build_chunk(where, own_ids, other_ids, pieces, logits):
     tokens, width = pieces[0].shape
     vmem = pl.BlockSpec(memory_space=pltpu.VMEM)
     return pl.pallas_call(
         chunk_kernel,
-        in_specs=[pl.BlockSpec(memory_space=pltpu.SMEM)] + [vmem] * 6,
-        out_specs=[vmem] * 2,
+        in_specs=[pl.BlockSpec(memory_space=pltpu.SMEM)] + [vmem] * 6 + [pl.BlockSpec(memory_space=pl.ANY)] * 2,
+        out_specs=[vmem] * 2 + [pl.BlockSpec(memory_space=pl.ANY)],
         out_shape=[
             jax.ShapeDtypeStruct((2 * tokens + CAP_CHUNK, width), jnp.bfloat16),
             jax.ShapeDtypeStruct((4 * CAP_ROUTE, 4 * CAP_CHUNK), jnp.bfloat16),
+            pltpu.HBM((2 * logits[0].shape[0], logits[0].shape[1]), logits[0].dtype),
         ],
-        cost_estimate=SMALL,
-        compiler_params=pltpu.CompilerParams(vmem_limit_bytes=4 * 1024 * 1024),
-    )(where, own_ids, other_ids, *pieces)
+        scratch_shapes=[pltpu.VMEM((2, *logits[0].shape), logits[0].dtype), pltpu.SemaphoreType.DMA((4,))],
+        cost_estimate=SMALL,
+        compiler_params=pltpu.CompilerParams(vmem_limit_bytes=6 * 1024 * 1024),
+    )(where, own_ids, other_ids, *pieces, in_hbm(logits[0]), logits[1])
 
 
 def spread_kernel(where_ref, route, *refs):
@@ -314,14 +326,15 @@
 
 
 def prepare_kernel(group, where_ref, own_ids, other_ids, *refs):
-    logits, weights, flags, largest = refs[:4], refs[4:12], refs[12], refs[13]
-    own, other, sems = refs[14:]
+    logits, weights, flags, largest = refs[:2], refs[2:10], refs[10], refs[11]
+    own, other, sems = refs[12:]
+    tall = own.shape[0]
     voc = own.shape[1]
     tokens = group // 4
     rows = 2 * group + CAP_ROUTE
 
     def load(shard):
-        pair = logits[2 * shard : 2 * shard + 2]
+        pair = [logits[shard].at[pl.ds(k * tall, tall)] for k in range(2)]
         return [pltpu.make_async_copy(a, b, sems.at[k]) for k, (a, b) in enumerate(zip(pair, (own, other)))]
 
     for copy in load(0):
@@ -387,18 +400,19 @@
     vmem, smem = pl.BlockSpec(memory_space=pltpu.VMEM), pl.BlockSpec(memory_space=pltpu.SMEM)
 
     def kernel(where_ref, own_ids, other_ids, *refs):
-        prepare_kernel(group, where_ref, own_ids, other_ids, *refs[:4], *refs[5:])
+        prepare_kernel(group, where_ref, own_ids, other_ids, *refs[:2], *refs[3:])
 
     return pl.pallas_call(
         kernel,
-        in_specs=[smem, vmem, vmem] + [pl.BlockSpec(memory_space=pl.ANY)] * 5,
+        in_specs=[smem, vmem, vmem] + [pl.BlockSpec(memory_space=pl.ANY)] * 3,
         out_specs=[vmem] * 8 + [smem, smem],
         out_shape=[pltpu.VMEM((rows, 2 * voc), jnp.bfloat16)] * 8
         + [jax.ShapeDtypeStruct((3,), jnp.int32), jax.ShapeDtypeStruct((2,), jnp.float32)],
-        scratch_shapes=[pltpu.VMEM(logits[0].shape, logits[0].dtype)] * 2 + [pltpu.SemaphoreType.DMA((2,))],
+        scratch_shapes=[pltpu.VMEM((logits[0].shape[0] // 2, voc), logits[0].dtype)] * 2
+        + [pltpu.SemaphoreType.DMA((2,))],
         cost_estimate=SMALL,
         compiler_params=pltpu.CompilerParams(vmem_limit_bytes=8 * 1024 * 1024),
-    )(where, own_ids, other_ids, in_hbm(logits[0]), *logits[1:], order)
+    )(where, own_ids, other_ids, *logits, order)
 
 
 def add_products(total, products):
@@ -449,10 +463,12 @@
 
     other_ids = send(own_ids, quad_pairs(0, 1))
     other_logits = send(own_logits, quad_pairs(0, 1))
-    logits = [own_logits, other_logits] + [send(array, pair_pairs(0, 0)) for array in (own_logits, other_logits)]
 
     where = jnp.stack([section, shard >> 2, z_hi, second, rep]).astype(jnp.int32)
-    chunk, own_route = build_chunk(where, token_ids, other_ids, [pieces[flip] for flip in flips])
+    chunk, own_route, both = build_chunk(
+        where, token_ids, other_ids, [pieces[flip] for flip in flips], [own_logits, other_logits]
+    )
+    logits = [both, send(both, pair_pairs(0, 0))]
 
     far, down = (send(chunk, depth_pairs(step)) for step in (2, -1))
     up = send(chunk, depth_pairs(1))
@@ -522,7 +538,7 @@
     here = jnp.stack(near * 2).astype(jnp.int32)
     blocks = [parts_of(0, b, unscale) for b in (0, 1)]
     *results, unscale = adamw_pair(here, unscale.reshape(1), *blocks, list(map(in_hbm, state)), None, across[0])
-    blocks = [parts_of(1, b, unscale[:1, :1]) for b in (0, 1)]
+    blocks = [parts_of(1, b, unscale) for b in (0, 1)]
     there = jnp.stack([2 * (section ^ 1) + rep, 2 * (section ^ 1) + (rep ^ 1), rep, rep ^ 1]).astype(jnp.int32)
     return tuple(adamw_pair(there, 1.0 / scale[:1], *blocks, across, results)[:3])
 

time: 104 us -> 98.9 us (0.951)
  starting transfers between devices: 37.9 us -> 35.1 us
  waiting for transfers between devices: 21.5 us -> 19.3 us
  Pallas kernels: 21.7 us -> 20.6 us
    ppermute x26 -> x25, starting transfers between devices: 37.9 us -> 35.1 us  [send(): return lax.ppermute(array, AXES, table)]
    ppermute x26 -> x25, waiting for transfers between devices: 21.5 us -> 19.3 us  [send(): return lax.ppermute(array, AXES, table)]
    pallas_call x2, Pallas kernels: 2.1 us -> 0.09 us  [join(): pl.pallas_call(join_kernel, in_specs=[vmem, vmem] + [pl.BlockSpec(memory_...]
    pallas_call x1, Pallas kernels: 1.68 us -> 3.45 us  [build_chunk(): pl.pallas_call(chunk_kernel, in_specs=[pl.BlockSpec(memory_space=pltpu.SM...]
    unnamed x44 -> x58, local copies, waits for them, and re-layouts: 2.73 us -> 4.03 us
  transfers between devices with their start and end apart: 26 -> 25, of which waited for: 13 -> 12; matrix products, arithmetic and copies ran while one was open for 14% -> 14% of each run, Pallas kernels for 16% -> 15%
where the time goes in v4:
time: 98.9 us; the launch traced here: 98.4 us
  starting transfers between devices  35.1 us (35%)
  Pallas kernels  20.6 us (21%)
  waiting for transfers between devices  19.3 us (20%)
  matrix products  11.4 us (12%)
  local copies, waits for them, and re-layouts  6.3 us (6%)
  other arithmetic  3.29 us (3%)
  between operations  2.4 us (2%)
    ppermute x25, starting transfers between devices, send(): return lax.ppermute(array, AXES, table)  35.1 us
    ppermute x25, waiting for transfers between devices, send(): return lax.ppermute(array, AXES, table)  19.3 us
    dot_general x8, matrix products, dot_rows(): lax.dot_general(weights, rows, (((0,), (0,)), ((), ())), preferred_elemen...  11.4 us
    pallas_call x2, Pallas kernels, adamw_pair(): pl.pallas_call(adamw_kernel, grid_spec=pltpu.PrefetchScalarGridSpec(num_s...  6.53 us
    pallas_call x1, Pallas kernels, prepare(): pl.pallas_call(kernel, in_specs=[smem, vmem, vmem] + [pl.BlockSpec(memory...  4.65 us
    unnamed x58, local copies, waits for them, and re-layouts  4.03 us
    pallas_call x1, Pallas kernels, build_chunk(): pl.pallas_call(chunk_kernel, in_specs=[pl.BlockSpec(memory_space=pltpu.SM...  3.45 us
  transfers between devices with their start and end apart: 25, of which 12 were waited for; matrix products, arithmetic and copies ran while one was open for 14% of the time, Pallas kernels for 15%

profile of v4, /device:TPU:1, one launch (start us, length us, event | category | flops | bytes accessed | tf_op | source)
XLA Modules:
  0.0 98.4 jit_solution(14416892124674174158)
XLA Ops:
  0.6 3.3 %collective-permute-start.5 = (bf16[1536,384]{1,0:T(8,128)(2,1)}, bf16[1536,384]{1,0:T(8,128)(2,1)S(1)}, u32[]{:S(2)}, u32[]{:S(2)}) collective-permute-start(bf16[1536,384]{1,0:T(8,128)(2,1)} %bitcast.54), channel_id=1, source_target_pairs={{0,1},{1,0},{2,3},{3,2},{4,5},{5,4},{6,7},{7,6},{8,9},{9,8},{10,11... | collective-permute-start | bytes 3538952 | tf_op jit(solution)/shard_map/ppermute | solution.py:59
  5.1 1.7 %collective-permute-start.3 = (bf16[24,1152]{1,0:T(8,128)(2,1)S(1)}, bf16[24,1152]{1,0:T(8,128)(2,1)S(1)}, u32[]{:S(2)}, u32[]{:S(2)}) collective-permute-start(bf16[24,1152]{1,0:T(8,128)(2,1)S(1)} %get-tuple-element.244), channel_id=1, source_target_pairs={{0,129},{1,128},{2,131},{3,130},{4,133},{5,132},{6,135},{7,134},{8... | collective-permute-start | bytes 165896 | tf_op jit(solution)/shard_map/ppermute | solution.py:59
  8.6 1.3 %collective-permute-done.3.refs_1_ = bf16[24,1152]{1,0:T(8,128)(2,1)S(1)} collective-permute-done((bf16[24,1152]{1,0:T(8,128)(2,1)S(1)}, bf16[24,1152]{1,0:T(8,128)(2,1)S(1)}, u32[]{:S(2)}, u32[]{:S(2)}) %collective-permute-start.3) | collective-permute-done | bytes 55328 | tf_op jit(solution)/shard_map/ppermute | solution.py:59
  9.9 3.5 %shard_map.86 = (bf16[64,1152]{1,0:T(8,128)(2,1)S(1)}, bf16[128,64]{1,0:T(8,128)(2,1)S(1)}, bf16[3072,384]{1,0:T(8,128)(2,1)}) custom-call(s32[5]{0:T(128)S(1)} %stack.144.where_ref, s32[1,1536]{1,0:T(1,128)} %own_ids.3, s32[1,1536]{1,0:T(1,128)S(1)} %collective-permute-done.1.other_ids, bf16[24,1152]{1,0:T(8,128)(2,1)S(1)} %collective-permute-done.2.refs_0_, ...), custom_call_target="tpu_custom_call" | custom-call | flops 1024 | bytes 1024 | tf_op jit(solution)/shard_map/pallas_call | solution.py:245
  13.7 5.4 %collective-permute-start.7 = (bf16[64,1152]{1,0:T(8,128)(2,1)S(1)}, bf16[64,1152]{1,0:T(8,128)(2,1)S(1)}, u32[]{:S(2)}, u32[]{:S(2)}) collective-permute-start(bf16[64,1152]{1,0:T(8,128)(2,1)S(1)} %get-tuple-element.249.refs_0_), channel_id=1, source_target_pairs={{0,6},{1,7},{2,0},{3,1},{4,2},{5,3},{6,4},{7,5},{8,14},{9,15},{10,... | collective-permute-start | bytes 442376 | tf_op jit(solution)/shard_map/ppermute | solution.py:59
  20.0 2.4 %collective-permute-start.9 = (bf16[64,1152]{1,0:T(8,128)(2,1)S(1)}, bf16[64,1152]{1,0:T(8,128)(2,1)S(1)}, u32[]{:S(2)}, u32[]{:S(2)}) collective-permute-start(bf16[64,1152]{1,0:T(8,128)(2,1)S(1)} %get-tuple-element.249.refs_0_), channel_id=1, source_target_pairs={{0,2},{1,3},{2,4},{3,5},{4,6},{5,7},{6,0},{7,1},{8,10},{9,11},{10,... | collective-permute-start | bytes 442376 | tf_op jit(solution)/shard_map/ppermute | solution.py:59
  23.6 7.5 %collective-permute-done.8.refs_2_ = bf16[64,1152]{1,0:T(8,128)(2,1)S(1)} collective-permute-done((bf16[64,1152]{1,0:T(8,128)(2,1)S(1)}, bf16[64,1152]{1,0:T(8,128)(2,1)S(1)}, u32[]{:S(2)}, u32[]{:S(2)}) %collective-permute-start.8) | collective-permute-done | bytes 147488 | tf_op jit(solution)/shard_map/ppermute | solution.py:59
  31.4 1.9 %shard_map.87 = (bf16[224,640]{1,0:T(8,128)(2,1)S(1)}, bf16[224,640]{1,0:T(8,128)(2,1)S(1)}, bf16[224,640]{1,0:T(8,128)(2,1)}, bf16[224,640]{1,0:T(8,128)(2,1)}) custom-call(s32[2]{0:T(128)S(1)} %pad_add_fusion.5.where_ref, bf16[128,64]{1,0:T(8,128)(2,1)S(1)} %get-tuple-element.248.route, bf16[64,1152]{1,0:T(8,128)(2,1)S(1)} %get-tuple-element.249.refs_0_, ...), custom_call_target="tpu_custom_call" | custom-call | flops 1024 | bytes 1024 | tf_op jit(solution)/shard_map/pallas_call | solution.py:279
  34.0 1.4 %collective-permute-start.10 = (bf16[224,640]{1,0:T(8,128)(2,1)}, bf16[224,640]{1,0:T(8,128)(2,1)S(1)}, u32[]{:S(2)}, u32[]{:S(2)}) collective-permute-start(bf16[224,640]{1,0:T(8,128)(2,1)} %get-tuple-element.255), channel_id=1, source_target_pairs={{0,24},{1,97},{2,26},{3,99},{4,28},{5,101},{6,30},{7,103},{8,0},{9... | collective-permute-start | bytes 860168 | tf_op jit(solution)/shard_map/ppermute | solution.py:59
  35.3 1.3 %collective-permute-start.11 = (bf16[224,640]{1,0:T(8,128)(2,1)}, bf16[224,640]{1,0:T(8,128)(2,1)S(1)}, u32[]{:S(2)}, u32[]{:S(2)}) collective-permute-start(bf16[224,640]{1,0:T(8,128)(2,1)} %get-tuple-element.256), channel_id=1, source_target_pairs={{0,16},{1,65},{2,18},{3,67},{4,20},{5,69},{6,22},{7,71},{8,24},{9,... | collective-permute-start | bytes 860168 | tf_op jit(solution)/shard_map/ppermute | solution.py:59
  37.6 4.1 %collective-permute-done.6.refs_1_ = bf16[3072,384]{1,0:T(8,128)(2,1)S(1)} collective-permute-done((bf16[3072,384]{1,0:T(8,128)(2,1)}, bf16[3072,384]{1,0:T(8,128)(2,1)S(1)}, u32[]{:S(2)}, u32[]{:S(2)}) %collective-permute-start.6) | collective-permute-done | bytes 2359328 | tf_op jit(solution)/shard_map/ppermute | solution.py:59
  41.7 1.7 %copy-done = bf16[3072,384]{1,0:T(8,128)(2,1)S(1)} copy-done((bf16[3072,384]{1,0:T(8,128)(2,1)S(1)}, bf16[3072,384]{1,0:T(8,128)(2,1)}, u32[]{:S(2)}) %copy-start) | copy-done | bytes 2359320
  43.4 4.6 %shard_map.88 = (bf16[448,768]{1,0:T(8,128)(2,1)S(1)}, bf16[448,768]{1,0:T(8,128)(2,1)S(1)}, bf16[448,768]{1,0:T(8,128)(2,1)S(1)}, bf16[448,768]{1,0:T(8,128)(2,...) custom-call(s32[20]{0:T(128)S(1)} %stack.137.where_ref, ...), custom_call_target="tpu_custom_call" | custom-call | flops 1024 | bytes 1024 | tf_op jit(solution)/shard_map/pallas_call | solution.py:405
  49.5 1.3 %shard_map.91 = (bf16[448,640]{1,0:T(8,128)(2,1)}, bf16[448,640]{1,0:T(8,128)(2,1)S(1)}) custom-call(bf16[448,640]{1,0:T(8,128)(2,1)S(1)} %shard_map.90._.refs_1_, bf16[448,640]{1,0:T(8,128)(2,1)S(1)} %shard_map.89.refs_0_, bf16[448,640]{1,0:T(8,128)(2,1)S(1)} %shard_map.90._.refs_1_), custom_call_target="tpu_custom_call" | custom-call | flops 1024 | bytes 1024 | tf_op jit(solution)/shard_map/pallas_call | solution.py:318
  51.3 1.8 %collective-permute-start.14 = (bf16[448,640]{1,0:T(8,128)(2,1)S(1)}, bf16[448,640]{1,0:T(8,128)(2,1)}, u32[]{:S(2)}, u32[]{:S(2)}) collective-permute-start(bf16[448,640]{1,0:T(8,128)(2,1)S(1)} %shard_map.90._.refs_1_), channel_id=1, source_target_pairs={{0,96},{1,25},{2,98},{3,27},{4,100},{5,29},{6,102},{7,31},{8,104},... | collective-permute-start | bytes 1720328 | tf_op jit(solution)/shard_map/ppermute | solution.py:59
  54.2 1.3 %collective-permute-start.15 = (bf16[448,640]{1,0:T(8,128)(2,1)S(1)}, bf16[448,640]{1,0:T(8,128)(2,1)}, u32[]{:S(2)}, u32[]{:S(2)}) collective-permute-start(bf16[448,640]{1,0:T(8,128)(2,1)S(1)} %get-tuple-element.261), channel_id=1, source_target_pairs={{0,32},{1,9},{2,34},{3,11},{4,36},{5,13},{6,38},{7,15},{8,40},{9,1... | collective-permute-start | bytes 1720328 | tf_op jit(solution)/shard_map/ppermute | solution.py:59
  55.4 1.4 %conditional.1 = (f32[768,640]{1,0:T(8,128)}) conditional(s32[]{:T(128)} %convert_element_type.46, () %tuple.35, (s32[]{:T(128)}, bf16[24,1152]{1,0:T(8,128)(2,1)S(1)}, bf16[24,1152]{1,0:T(8,128)(2,1)S(1)}, bf16[24,1152]{1,0:T(8,128)(2,1)S(1)}, bf16[24,1152]{1,0:T(8,128)(2,1)S(1)}, /*index=5*/s32[1,1536]{1,0:T(1,128)S(1)}, s32[1,1536]{1,0:T(1,128)S(1)}, ...), branch_computations={%region_0.1_spmd, %region_1.4_spmd} | conditional | flops 48485392 | bytes 5246637 | solution.py:495
  55.4 1.4 %broadcast.28 = f32[768,640]{1,0:T(8,128)} broadcast(f32[]{:T(128)} %constant.84.clone), dimensions={} | broadcast | bytes 1966084 | tf_op jit(solution)/shard_map/broadcast.5
  60.3 2.7 %collective-permute-start.18 = (bf16[448,640]{1,0:T(8,128)(2,1)}, bf16[448,640]{1,0:T(8,128)(2,1)S(1)}, u32[]{:S(2)}, u32[]{:S(2)}) collective-permute-start(bf16[448,640]{1,0:T(8,128)(2,1)} %collective-permute-done.14), channel_id=1, source_target_pairs={{0,96},{1,25},{2,98},{3,27},{4,100},{5,29},{6,102},{7,31},{8,104},... | collective-permute-start | bytes 1720328 | tf_op jit(solution)/shard_map/ppermute | solution.py:59
  63.0 1.9 %fusion.12 = f32[768,640]{1,0:T(8,128)S(1)} fusion(bf16[448,768]{1,0:T(8,128)(2,1)S(1)} %copy-done.12, bf16[448,640]{1,0:T(8,128)(2,1)} %collective-permute-done.14), kind=kOutput, calls=%fused_computation.50 | convolution fusion | flops 440401920 | bytes 3227648 | tf_op jit(solution)/shard_map/dot_general | solution.py:425
  64.9 1.9 %fusion.11 = f32[768,640]{1,0:T(8,128)S(1)} fusion(bf16[448,768]{1,0:T(8,128)(2,1)S(1)} %copy-done.10, bf16[448,640]{1,0:T(8,128)(2,1)} %collective-permute-done.13), kind=kOutput, calls=%fused_computation.49 | convolution fusion | flops 440401920 | bytes 3227648 | tf_op jit(solution)/shard_map/dot_general | solution.py:425
  66.9 1.9 %fusion.14 = f32[768,640]{1,0:T(8,128)S(1)} fusion(bf16[448,768]{1,0:T(8,128)(2,1)S(1)} %copy-done.8, bf16[448,640]{1,0:T(8,128)(2,1)} %collective-permute-done.16), kind=kOutput, calls=%fused_computation.52 | convolution fusion | flops 440401920 | bytes 3227648 | tf_op jit(solution)/shard_map/dot_general | solution.py:425
  68.8 1.9 %fusion.13 = f32[768,640]{1,0:T(8,128)S(1)} fusion(bf16[448,768]{1,0:T(8,128)(2,1)S(1)} %copy-done.6, bf16[448,640]{1,0:T(8,128)(2,1)} %collective-permute-done.15), kind=kOutput, calls=%fused_computation.51 | convolution fusion | flops 440401920 | bytes 3227648 | tf_op jit(solution)/shard_map/dot_general | solution.py:425
  72.6 1.3 %add_add_fusion = f32[768,640]{1,0:T(8,128)S(1)} fusion(f32[768,640]{1,0:T(8,128)S(1)} %fusion.15, f32[768,640]{1,0:T(8,128)S(1)} %fusion.14, f32[768,640]{1,0:T(8,128)S(1)} %fusion.13, f32[768,640]{1,0:T(8,128)S(1)} %fusion.12, f32[768,640]{1,0:T(8,128)S(1)} %fusion.11, f32[768,640]{1,0:T(8,128)S(1)} %fusion.10, f32[768,640]{1,0:T(8,128)S(1)} %copy-done.21, ...), kind=kOutput, calls=%fused_computation.11 | convolution fusion | flops 444334080 | bytes 18956288 | tf_op jit(solution)/shard_map/dot_general | solution.py:425
  73.9 1.4 %multiply_convert_fusion = (f16[96,640]{1,0:T(8,128)(2,1)S(1)}, f16[96,640]{1,0:T(8,128)(2,1)S(1)}, f16[96,640]{1,0:T(8,128)(2,1)S(1)}, f16[96,640]{1,0:T(8,128)...) fusion(f32[768,640]{1,0:T(8,128)S(1)} %add_add_fusion, ...), kind=kLoop, calls=%fused_computation.13 | loop fusion | flops 737280 | bytes 2703396 | tf_op jit(solution)/shard_map/convert_element_type | solution.py:522
  75.3 1.1 %collective-permute-start.20 = (f16[96,640]{1,0:T(8,128)(2,1)S(1)}, f16[96,640]{1,0:T(8,128)(2,1)S(1)}, u32[]{:S(2)}, u32[]{:S(2)}) collective-permute-start(f16[96,640]{1,0:T(8,128)(2,1)S(1)} %get-tuple-element.321), channel_id=1, source_target_pairs={{0,8},{1,33},{2,10},{3,35},{4,12},{5,37},{6,14},{7,39},{8,0},{9,41... | collective-permute-start | bytes 368648 | tf_op jit(solution)/shard_map/ppermute | solution.py:59
  77.8 1.6 %collective-permute-start.23 = (f16[96,640]{1,0:T(8,128)(2,1)S(1)}, f16[96,640]{1,0:T(8,128)(2,1)S(1)}, u32[]{:S(2)}, u32[]{:S(2)}) collective-permute-start(f16[96,640]{1,0:T(8,128)(2,1)S(1)} %get-tuple-element.318), channel_id=1, source_target_pairs={{0,136},{1,161},{2,138},{3,163},{4,140},{5,165},{6,142},{7,167},{8... | collective-permute-start | bytes 368648 | tf_op jit(solution)/shard_map/ppermute | solution.py:59
  79.3 5.4 %collective-permute-start.22 = (f16[96,640]{1,0:T(8,128)(2,1)S(1)}, f16[96,640]{1,0:T(8,128)(2,1)S(1)}, u32[]{:S(2)}, u32[]{:S(2)}) collective-permute-start(f16[96,640]{1,0:T(8,128)(2,1)S(1)} %get-tuple-element.319), channel_id=1, source_target_pairs={{0,9},{1,32},{2,11},{3,34},{4,13},{5,36},{6,15},{7,38},{8,1},{9,40... | collective-permute-start | bytes 368648 | tf_op jit(solution)/shard_map/ppermute | solution.py:59
  84.7 2.5 %collective-permute-start.25 = (f16[96,640]{1,0:T(8,128)(2,1)S(1)}, f16[96,640]{1,0:T(8,128)(2,1)S(1)}, u32[]{:S(2)}, u32[]{:S(2)}) collective-permute-start(f16[96,640]{1,0:T(8,128)(2,1)S(1)} %get-tuple-element.316), channel_id=1, source_target_pairs={{0,137},{1,160},{2,139},{3,162},{4,141},{5,164},{6,143},{7,166},{8... | collective-permute-start | bytes 368648 | tf_op jit(solution)/shard_map/ppermute | solution.py:59
  87.9 1.7 %shard_map.92 = (f32[96,2304]{1,0:T(8,128)S(1)}, f32[96,2304]{1,0:T(8,128)S(1)}, f32[96,2304]{1,0:T(8,128)S(1)}) custom-call(s32[1]{0:T(128)} %bitcast.34.where_ref, f32[96,4608]{1,0:T(8,128)} %refs_4_.1, f32[96,4608]{1,0:T(8,128)} %refs_5_.1, f32[96,4608]{1,0:T(8,128)} %refs_6_.1, f32[96,640]{1,0:T(8,128)S(1)} %collective-permute-done.21.refs_3_), custom_call_target="tpu_custom_call" | custom-call | flops 1024 | bytes 1024 | tf_op jit(solution)/shard_map/pallas_call | solution.py:133
  89.6 3.8 %shard_map.93 = (f32[96,4608]{1,0:T(8,128)}, f32[96,4608]{1,0:T(8,128)}, f32[96,4608]{1,0:T(8,128)}, f32[1,1]{1,0:T(1,128)}) custom-call(s32[4]{0:T(128)S(1)} %pad_add_fusion.6.where_ref, f32[1]{0:T(128)} %bitcast.32.held_ref, f32[96,640]{1,0:T(8,128)S(1)} %get-tuple-element.332.refs_0_, f32[96,512]{1,0:T(8,128)S(1)} %dynamic-slice_select_fusion.1.refs_1_, ...), custom_call_target="tpu_custom_call" | custom-call | flops 1024 | bytes 1024 | tf_op jit(solution)/shard_map/pallas_call | solution.py:106
  95.7 2.7 %shard_map.94 = (f32[96,4608]{1,0:T(8,128)}, f32[96,4608]{1,0:T(8,128)}, f32[96,4608]{1,0:T(8,128)}, f32[1,1]{1,0:T(1,128)}) custom-call(s32[4]{0:T(128)S(1)} %pad_add_fusion.2.where_ref, f32[1]{0:T(128)S(6)} %div.10.held_ref, f32[96,640]{1,0:T(8,128)S(1)} %get-tuple-element.327.refs_0_, ...), custom_call_target="tpu_custom_call", output_to_operand_aliasing={{0}: (9, {}), {1}: (10, {}), {2}: (11, {})} | custom-call | flops 1024 | bytes 1024 | tf_op jit(solution)/shard_map/pallas_call | solution.py:106
  (115 shorter events, 18.3 us)
Async XLA Ops:
  0.6 41.1 %copy-start.28 = (s32[1,1536]{1,0:T(1,128)S(1)}, s32[1,1536]{1,0:T(1,128)}, u32[]{:S(2)}) copy-start(s32[1,1536]{1,0:T(1,128)} %own_ids.3) | copy-start | bytes 18436
  0.6 9.3 %collective-permute-start.5 = (bf16[1536,384]{1,0:T(8,128)(2,1)}, bf16[1536,384]{1,0:T(8,128)(2,1)S(1)}, u32[]{:S(2)}, u32[]{:S(2)}) collective-permute-start(bf16[1536,384]{1,0:T(8,128)(2,1)} %bitcast.54), channel_id=1, source_target_pairs={{0,1},{1,0},{2,3},{3,2},{4,5},{5,4},{6,7},{7,6},{8,9},{9,8},{10,11... | collective-permute-start | bytes 3538952 | tf_op jit(solution)/shard_map/ppermute | solution.py:59
  5.0 8.4 %copy-start.19 = (bf16[24,1152]{1,0:T(8,128)(2,1)}, bf16[24,1152]{1,0:T(8,128)(2,1)S(1)}, u32[]{:S(2)}) copy-start(bf16[24,1152]{1,0:T(8,128)(2,1)S(1)} %get-tuple-element.246.refs_3_) | copy-start | bytes 165892
  5.0 3.6 %collective-permute-start.2 = (bf16[24,1152]{1,0:T(8,128)(2,1)S(1)}, bf16[24,1152]{1,0:T(8,128)(2,1)S(1)}, u32[]{:S(2)}, u32[]{:S(2)}) collective-permute-start(bf16[24,1152]{1,0:T(8,128)(2,1)S(1)} %get-tuple-element.243), channel_id=1, source_target_pairs={{0,128},{1,129},{2,130},{3,131},{4,132},{5,133},{6,134},{7,135},{8... | collective-permute-start | bytes 165896 | tf_op jit(solution)/shard_map/ppermute | solution.py:59
  5.1 4.8 %collective-permute-start.3 = (bf16[24,1152]{1,0:T(8,128)(2,1)S(1)}, bf16[24,1152]{1,0:T(8,128)(2,1)S(1)}, u32[]{:S(2)}, u32[]{:S(2)}) collective-permute-start(bf16[24,1152]{1,0:T(8,128)(2,1)S(1)} %get-tuple-element.244), channel_id=1, source_target_pairs={{0,129},{1,128},{2,131},{3,130},{4,133},{5,132},{6,135},{7,134},{8... | collective-permute-start | bytes 165896 | tf_op jit(solution)/shard_map/ppermute | solution.py:59
  6.8 3.1 %collective-permute-start.4 = (bf16[24,1152]{1,0:T(8,128)(2,1)S(1)}, bf16[24,1152]{1,0:T(8,128)(2,1)S(1)}, u32[]{:S(2)}, u32[]{:S(2)}) collective-permute-start(bf16[24,1152]{1,0:T(8,128)(2,1)S(1)} %get-tuple-element.245), channel_id=1, source_target_pairs={{0,1},{1,0},{2,3},{3,2},{4,5},{5,4},{6,7},{7,6},{8,9},{9,8},{10,11... | collective-permute-start | bytes 165896 | tf_op jit(solution)/shard_map/ppermute | solution.py:59
  7.0 1.2 %collective-permute-start.1 = (s32[1,1536]{1,0:T(1,128)S(1)}, s32[1,1536]{1,0:T(1,128)S(1)}, u32[]{:S(2)}, u32[]{:S(2)}) collective-permute-start(s32[1,1536]{1,0:T(1,128)S(1)} %get-tuple-element.242), channel_id=1, source_target_pairs={{0,1},{1,0},{2,3},{3,2},{4,5},{5,4},{6,7},{7,6},{8,9},{9,8},{10,11... | collective-permute-start | bytes 18440 | tf_op jit(solution)/shard_map/ppermute | solution.py:59
  13.4 28.3 %collective-permute-start.6 = (bf16[3072,384]{1,0:T(8,128)(2,1)}, bf16[3072,384]{1,0:T(8,128)(2,1)S(1)}, u32[]{:S(2)}, u32[]{:S(2)}) collective-permute-start(bf16[3072,384]{1,0:T(8,128)(2,1)} %get-tuple-element.247.refs_0_), channel_id=1, source_target_pairs={{0,8},{1,33},{2,10},{3,35},{4,12},{5,37},{6,14},{7,39},{8,0},{9,41... | collective-permute-start | bytes 7077896 | tf_op jit(solution)/shard_map/ppermute | solution.py:59
  13.7 9.8 %collective-permute-start.7 = (bf16[64,1152]{1,0:T(8,128)(2,1)S(1)}, bf16[64,1152]{1,0:T(8,128)(2,1)S(1)}, u32[]{:S(2)}, u32[]{:S(2)}) collective-permute-start(bf16[64,1152]{1,0:T(8,128)(2,1)S(1)} %get-tuple-element.249.refs_0_), channel_id=1, source_target_pairs={{0,6},{1,7},{2,0},{3,1},{4,2},{5,3},{6,4},{7,5},{8,14},{9,15},{10,... | collective-permute-start | bytes 442376 | tf_op jit(solution)/shard_map/ppermute | solution.py:59
  19.1 11.9 %collective-permute-start.8 = (bf16[64,1152]{1,0:T(8,128)(2,1)S(1)}, bf16[64,1152]{1,0:T(8,128)(2,1)S(1)}, u32[]{:S(2)}, u32[]{:S(2)}) collective-permute-start(bf16[64,1152]{1,0:T(8,128)(2,1)S(1)} %get-tuple-element.249.refs_0_), channel_id=1, source_target_pairs={{0,4},{1,5},{2,6},{3,7},{4,0},{5,1},{6,2},{7,3},{8,12},{9,13},{10,... | collective-permute-start | bytes 442376 | tf_op jit(solution)/shard_map/ppermute | solution.py:59
  20.0 11.3 %collective-permute-start.9 = (bf16[64,1152]{1,0:T(8,128)(2,1)S(1)}, bf16[64,1152]{1,0:T(8,128)(2,1)S(1)}, u32[]{:S(2)}, u32[]{:S(2)}) collective-permute-start(bf16[64,1152]{1,0:T(8,128)(2,1)S(1)} %get-tuple-element.249.refs_0_), channel_id=1, source_target_pairs={{0,2},{1,3},{2,4},{3,5},{4,6},{5,7},{6,0},{7,1},{8,10},{9,11},{10,... | collective-permute-start | bytes 442376 | tf_op jit(solution)/shard_map/ppermute | solution.py:59
  34.0 15.0 %collective-permute-start.10 = (bf16[224,640]{1,0:T(8,128)(2,1)}, bf16[224,640]{1,0:T(8,128)(2,1)S(1)}, u32[]{:S(2)}, u32[]{:S(2)}) collective-permute-start(bf16[224,640]{1,0:T(8,128)(2,1)} %get-tuple-element.255), channel_id=1, source_target_pairs={{0,24},{1,97},{2,26},{3,99},{4,28},{5,101},{6,30},{7,103},{8,0},{9... | collective-permute-start | bytes 860168 | tf_op jit(solution)/shard_map/ppermute | solution.py:59
  35.3 13.6 %collective-permute-start.11 = (bf16[224,640]{1,0:T(8,128)(2,1)}, bf16[224,640]{1,0:T(8,128)(2,1)S(1)}, u32[]{:S(2)}, u32[]{:S(2)}) collective-permute-start(bf16[224,640]{1,0:T(8,128)(2,1)} %get-tuple-element.256), channel_id=1, source_target_pairs={{0,16},{1,65},{2,18},{3,67},{4,20},{5,69},{6,22},{7,71},{8,24},{9,... | collective-permute-start | bytes 860168 | tf_op jit(solution)/shard_map/ppermute | solution.py:59
  36.6 12.4 %collective-permute-start.12 = (bf16[224,640]{1,0:T(8,128)(2,1)S(1)}, bf16[224,640]{1,0:T(8,128)(2,1)S(1)}, u32[]{:S(2)}, u32[]{:S(2)}) collective-permute-start(bf16[224,640]{1,0:T(8,128)(2,1)S(1)} %get-tuple-element.250.refs_2_), channel_id=1, source_target_pairs={{0,8},{1,33},{2,10},{3,35},{4,12},{5,37},{6,14},{7,39},{8,16},{9,4... | collective-permute-start | bytes 860168 | tf_op jit(solution)/shard_map/ppermute | solution.py:59
  43.4 5.7 %copy-start.18 = (bf16[224,640]{1,0:T(8,128)(2,1)S(1)}, bf16[224,640]{1,0:T(8,128)(2,1)}, u32[]{:S(2)}) copy-start(bf16[224,640]{1,0:T(8,128)(2,1)} %copy-done.17) | copy-start | bytes 860164
  49.0 5.1 %copy-start.20 = (bf16[24,1152]{1,0:T(8,128)(2,1)S(1)}, bf16[24,1152]{1,0:T(8,128)(2,1)}, u32[]{:S(2)}) copy-start(bf16[24,1152]{1,0:T(8,128)(2,1)} %copy-done.19) | copy-start | bytes 165892
  49.0 5.1 %copy-start.23 = (bf16[24,1152]{1,0:T(8,128)(2,1)S(1)}, bf16[24,1152]{1,0:T(8,128)(2,1)}, u32[]{:S(2)}) copy-start(bf16[24,1152]{1,0:T(8,128)(2,1)} %copy-done.22) | copy-start | bytes 165892
  49.1 10.4 %collective-permute-start.13 = (bf16[448,640]{1,0:T(8,128)(2,1)S(1)}, bf16[448,640]{1,0:T(8,128)(2,1)}, u32[]{:S(2)}, u32[]{:S(2)}) collective-permute-start(bf16[448,640]{1,0:T(8,128)(2,1)S(1)} %shard_map.89.refs_0_), channel_id=1, source_target_pairs={{0,32},{1,9},{2,34},{3,11},{4,36},{5,13},{6,38},{7,15},{8,40},{9,1... | collective-permute-start | bytes 1720328 | tf_op jit(solution)/shard_map/ppermute | solution.py:59
  51.3 9.0 %collective-permute-start.14 = (bf16[448,640]{1,0:T(8,128)(2,1)S(1)}, bf16[448,640]{1,0:T(8,128)(2,1)}, u32[]{:S(2)}, u32[]{:S(2)}) collective-permute-start(bf16[448,640]{1,0:T(8,128)(2,1)S(1)} %shard_map.90._.refs_1_), channel_id=1, source_target_pairs={{0,96},{1,25},{2,98},{3,27},{4,100},{5,29},{6,102},{7,31},{8,104},... | collective-permute-start | bytes 1720328 | tf_op jit(solution)/shard_map/ppermute | solution.py:59
  53.9 13.0 %collective-permute-start.16 = (bf16[448,640]{1,0:T(8,128)(2,1)}, bf16[448,640]{1,0:T(8,128)(2,1)}, u32[]{:S(2)}, u32[]{:S(2)}) collective-permute-start(bf16[448,640]{1,0:T(8,128)(2,1)} %get-tuple-element.263), channel_id=1, source_target_pairs={{0,96},{1,25},{2,98},{3,27},{4,100},{5,29},{6,102},{7,31},{8,104},... | collective-permute-start | bytes 1720328 | tf_op jit(solution)/shard_map/ppermute | solution.py:59
  54.2 14.6 %collective-permute-start.15 = (bf16[448,640]{1,0:T(8,128)(2,1)S(1)}, bf16[448,640]{1,0:T(8,128)(2,1)}, u32[]{:S(2)}, u32[]{:S(2)}) collective-permute-start(bf16[448,640]{1,0:T(8,128)(2,1)S(1)} %get-tuple-element.261), channel_id=1, source_target_pairs={{0,32},{1,9},{2,34},{3,11},{4,36},{5,13},{6,38},{7,15},{8,40},{9,1... | collective-permute-start | bytes 1720328 | tf_op jit(solution)/shard_map/ppermute | solution.py:59
  57.7 5.3 %copy-start.12 = (bf16[448,768]{1,0:T(8,128)(2,1)S(1)}, bf16[448,768]{1,0:T(8,128)(2,1)}, u32[]{:S(2)}) copy-start(bf16[448,768]{1,0:T(8,128)(2,1)} %copy-done.11) | copy-start | bytes 2064388
  58.8 6.1 %copy-start.10 = (bf16[448,768]{1,0:T(8,128)(2,1)S(1)}, bf16[448,768]{1,0:T(8,128)(2,1)}, u32[]{:S(2)}) copy-start(bf16[448,768]{1,0:T(8,128)(2,1)} %copy-done.9) | copy-start | bytes 2064388
  59.6 12.2 %collective-permute-start.17 = (bf16[448,640]{1,0:T(8,128)(2,1)}, bf16[448,640]{1,0:T(8,128)(2,1)S(1)}, u32[]{:S(2)}, u32[]{:S(2)}) collective-permute-start(bf16[448,640]{1,0:T(8,128)(2,1)} %collective-permute-done.13), channel_id=1, source_target_pairs={{0,32},{1,9},{2,34},{3,11},{4,36},{5,13},{6,38},{7,15},{8,40},{9,1... | collective-permute-start | bytes 1720328 | tf_op jit(solution)/shard_map/ppermute | solution.py:59
  60.3 12.3 %collective-permute-start.18 = (bf16[448,640]{1,0:T(8,128)(2,1)}, bf16[448,640]{1,0:T(8,128)(2,1)S(1)}, u32[]{:S(2)}, u32[]{:S(2)}) collective-permute-start(bf16[448,640]{1,0:T(8,128)(2,1)} %collective-permute-done.14), channel_id=1, source_target_pairs={{0,96},{1,25},{2,98},{3,27},{4,100},{5,29},{6,102},{7,31},{8,104},... | collective-permute-start | bytes 1720328 | tf_op jit(solution)/shard_map/ppermute | solution.py:59
  75.3 9.4 %collective-permute-start.20 = (f16[96,640]{1,0:T(8,128)(2,1)S(1)}, f16[96,640]{1,0:T(8,128)(2,1)S(1)}, u32[]{:S(2)}, u32[]{:S(2)}) collective-permute-start(f16[96,640]{1,0:T(8,128)(2,1)S(1)} %get-tuple-element.321), channel_id=1, source_target_pairs={{0,8},{1,33},{2,10},{3,35},{4,12},{5,37},{6,14},{7,39},{8,0},{9,41... | collective-permute-start | bytes 368648 | tf_op jit(solution)/shard_map/ppermute | solution.py:59
  77.8 15.7 %collective-permute-start.23 = (f16[96,640]{1,0:T(8,128)(2,1)S(1)}, f16[96,640]{1,0:T(8,128)(2,1)S(1)}, u32[]{:S(2)}, u32[]{:S(2)}) collective-permute-start(f16[96,640]{1,0:T(8,128)(2,1)S(1)} %get-tuple-element.318), channel_id=1, source_target_pairs={{0,136},{1,161},{2,138},{3,163},{4,140},{5,165},{6,142},{7,167},{8... | collective-permute-start | bytes 368648 | tf_op jit(solution)/shard_map/ppermute | solution.py:59
  79.3 8.5 %collective-permute-start.22 = (f16[96,640]{1,0:T(8,128)(2,1)S(1)}, f16[96,640]{1,0:T(8,128)(2,1)S(1)}, u32[]{:S(2)}, u32[]{:S(2)}) collective-permute-start(f16[96,640]{1,0:T(8,128)(2,1)S(1)} %get-tuple-element.319), channel_id=1, source_target_pairs={{0,9},{1,32},{2,11},{3,34},{4,13},{5,36},{6,15},{7,38},{8,1},{9,40... | collective-permute-start | bytes 368648 | tf_op jit(solution)/shard_map/ppermute | solution.py:59
  84.7 3.1 %collective-permute-start.21 = (f32[96,640]{1,0:T(8,128)S(1)}, f32[96,640]{1,0:T(8,128)S(1)}, u32[]{:S(2)}, u32[]{:S(2)}) collective-permute-start(f32[96,640]{1,0:T(8,128)S(1)} %get-tuple-element.320), channel_id=1, source_target_pairs={{0,1},{1,0},{2,3},{3,2},{4,5},{5,4},{6,7},{7,6},{8,9},{9,8},{10,11... | collective-permute-start | bytes 737288 | tf_op jit(solution)/shard_map/ppermute | solution.py:59
  84.7 8.7 %collective-permute-start.19 = (f16[96,640]{1,0:T(8,128)(2,1)S(1)}, f16[96,640]{1,0:T(8,128)(2,1)S(1)}, u32[]{:S(2)}, u32[]{:S(2)}) collective-permute-start(f16[96,640]{1,0:T(8,128)(2,1)S(1)} %get-tuple-element.322), channel_id=1, source_target_pairs={{0,128},{1,129},{2,130},{3,131},{4,132},{5,133},{6,134},{7,135},{8... | collective-permute-start | bytes 368648 | tf_op jit(solution)/shard_map/ppermute | solution.py:59
  84.7 9.5 %collective-permute-start.25 = (f16[96,640]{1,0:T(8,128)(2,1)S(1)}, f16[96,640]{1,0:T(8,128)(2,1)S(1)}, u32[]{:S(2)}, u32[]{:S(2)}) collective-permute-start(f16[96,640]{1,0:T(8,128)(2,1)S(1)} %get-tuple-element.316), channel_id=1, source_target_pairs={{0,137},{1,160},{2,139},{3,162},{4,141},{5,164},{6,143},{7,166},{8... | collective-permute-start | bytes 368648 | tf_op jit(solution)/shard_map/ppermute | solution.py:59
  87.8 7.2 %collective-permute-start.24 = (f16[96,640]{1,0:T(8,128)(2,1)S(1)}, f16[96,640]{1,0:T(8,128)(2,1)S(1)}, u32[]{:S(2)}, u32[]{:S(2)}) collective-permute-start(f16[96,640]{1,0:T(8,128)(2,1)S(1)} %get-tuple-element.317), channel_id=1, source_target_pairs={{0,129},{1,128},{2,131},{3,130},{4,133},{5,132},{6,135},{7,134},{8... | collective-permute-start | bytes 368648 | tf_op jit(solution)/shard_map/ppermute | solution.py:59
  (22 other events, 53.9 us)

commit v5 on v4

--- a/solution.py
+++ b/solution.py
@@ -333,11 +333,9 @@
     tokens = group // 4
     rows = 2 * group + CAP_ROUTE
 
-    def load(shard):
-        pair = [logits[shard].at[pl.ds(k * tall, tall)] for k in range(2)]
-        return [pltpu.make_async_copy(a, b, sems.at[k]) for k, (a, b) in enumerate(zip(pair, (own, other)))]
-
-    for copy in load(0):
+    halves = [[array.at[pl.ds(k * tall, tall)] for k in range(2)] for array in logits]
+    copies = [pltpu.make_async_copy(a, b, sems.at[k]) for k, (a, b) in enumerate(zip(halves[0], (own, other)))]
+    for copy in copies:
         copy.start()
     ids = by_column(own_ids, other_ids, group)
     spots = ids.shape[1]
@@ -369,15 +367,17 @@
         slots.append(jnp.sum(jnp.where(chosen, ids[c : c + 1, :] + 1, 0), 1, keepdims=True) - 1)
     slots = jnp.concatenate(slots, 0)
     for shard in range(2):
-        for copy in load(shard):
-            copy.wait()
+        sides = (own, other) if shard == 0 else halves[1]
+        if shard == 0:
+            for copy in copies:
+                copy.wait()
         wide = slice(shard * voc, (shard + 1) * voc)
         columns = lax.broadcasted_iota(jnp.int32, (CAP_ROUTE, voc), 1) + where_ref[17 + shard]
         top = jnp.zeros((8, voc), jnp.float32)
         for n in range(16):
             out, low = weights[n // 2], n % 2 * rows
             at = pl.multiple_of(where_ref[n] * group, 16)
-            first, second = own[pl.ds(at, group), :], other[pl.ds(at, group), :]
+            first, second = [side[pl.ds(at, group), :] for side in sides]
             for z in range(4):
                 both = [array[z * tokens : (z + 1) * tokens, :] for array in (first, second)]
                 out[low + 2 * z * tokens : low + 2 * (z + 1) * tokens, wide] = jnp.concatenate(both, 0)
@@ -389,9 +389,6 @@
                 picked = jnp.where(where_ref[n] == c, slots[c * CAP_ROUTE : (c + 1) * CAP_ROUTE, :], picked)
             out[low + 2 * group : low + rows, wide] = jnp.where(picked == columns, 1.0, 0.0).astype(jnp.bfloat16)
         largest[shard] = jnp.max(top)
-        if shard == 0:
-            for copy in load(1):
-                copy.start()
 
 
 def prepare(where, own_ids, other_ids, logits, order, group):
@@ -404,7 +401,7 @@
 
     return pl.pallas_call(
         kernel,
-        in_specs=[smem, vmem, vmem] + [pl.BlockSpec(memory_space=pl.ANY)] * 3,
+        in_specs=[smem, vmem, vmem, pl.BlockSpec(memory_space=pl.ANY), vmem, pl.BlockSpec(memory_space=pl.ANY)],
         out_specs=[vmem] * 8 + [smem, smem],
         out_shape=[pltpu.VMEM((rows, 2 * voc), jnp.bfloat16)] * 8
         + [jax.ShapeDtypeStruct((3,), jnp.int32), jax.ShapeDtypeStruct((2,), jnp.float32)],
@@ -412,7 +409,7 @@
         + [pltpu.SemaphoreType.DMA((2,))],
         cost_estimate=SMALL,
         compiler_params=pltpu.CompilerParams(vmem_limit_bytes=8 * 1024 * 1024),
-    )(where, own_ids, other_ids, *logits, order)
+    )(where, own_ids, other_ids, in_hbm(logits[0]), logits[1], order)
 
 
 def add_products(total, products):

time: 98.9 us -> 99.1 us (level)
  local copies, waits for them, and re-layouts: 6.3 us -> 4.48 us
  starting transfers between devices: 35.1 us -> 36.8 us
    unnamed x58 -> x56, local copies, waits for them, and re-layouts: 4.03 us -> 2.27 us
    ppermute x25, starting transfers between devices: 35.1 us -> 36.8 us  [send(): return lax.ppermute(array, AXES, table)]
  transfers between devices with their start and end apart: 25 -> 25, of which waited for: 12 -> 13; matrix products, arithmetic and copies ran while one was open for 14% -> 14% of each run, Pallas kernels for 15% -> 15%
where the time goes in v5:
time: 99.1 us; the launch traced here: 98.6 us
  starting transfers between devices  36.8 us (37%)
  Pallas kernels  20.9 us (21%)
  waiting for transfers between devices  19.3 us (19%)
  matrix products  11.4 us (12%)
  local copies, waits for them, and re-layouts  4.48 us (5%)
  other arithmetic  3.27 us (3%)
  between operations  2.53 us (3%)
    ppermute x25, starting transfers between devices, send(): return lax.ppermute(array, AXES, table)  36.8 us
    ppermute x25, waiting for transfers between devices, send(): return lax.ppermute(array, AXES, table)  19.3 us
    dot_general x8, matrix products, dot_rows(): lax.dot_general(weights, rows, (((0,), (0,)), ((), ())), preferred_elemen...  11.4 us
    pallas_call x2, Pallas kernels, adamw_pair(): pl.pallas_call(adamw_kernel, grid_spec=pltpu.PrefetchScalarGridSpec(num_s...  6.53 us
    pallas_call x1, Pallas kernels, prepare(): pl.pallas_call(kernel, in_specs=[smem, vmem, vmem, pl.BlockSpec(memory_sp...  4.81 us
    pallas_call x1, Pallas kernels, build_chunk(): pl.pallas_call(chunk_kernel, in_specs=[pl.BlockSpec(memory_space=pltpu.SM...  3.46 us
    unnamed x56, local copies, waits for them, and re-layouts  2.27 us
  transfers between devices with their start and end apart: 25, of which 13 were waited for; matrix products, arithmetic and copies ran while one was open for 14% of the time, Pallas kernels for 15%

profile of v5, /device:TPU:1, one launch (start us, length us, event | category | flops | bytes accessed | tf_op | source)
XLA Modules:
  0.0 98.6 jit_solution(16520684568402998964)
XLA Ops:
  0.6 3.3 %collective-permute-start.5 = (bf16[1536,384]{1,0:T(8,128)(2,1)}, bf16[1536,384]{1,0:T(8,128)(2,1)S(1)}, u32[]{:S(2)}, u32[]{:S(2)}) collective-permute-start(bf16[1536,384]{1,0:T(8,128)(2,1)} %bitcast.54), channel_id=1, source_target_pairs={{0,1},{1,0},{2,3},{3,2},{4,5},{5,4},{6,7},{7,6},{8,9},{9,8},{10,11... | collective-permute-start | bytes 3538952 | tf_op jit(solution)/shard_map/ppermute | solution.py:59
  5.1 1.7 %collective-permute-start.3 = (bf16[24,1152]{1,0:T(8,128)(2,1)S(1)}, bf16[24,1152]{1,0:T(8,128)(2,1)S(1)}, u32[]{:S(2)}, u32[]{:S(2)}) collective-permute-start(bf16[24,1152]{1,0:T(8,128)(2,1)S(1)} %get-tuple-element.244), channel_id=1, source_target_pairs={{0,129},{1,128},{2,131},{3,130},{4,133},{5,132},{6,135},{7,134},{8... | collective-permute-start | bytes 165896 | tf_op jit(solution)/shard_map/ppermute | solution.py:59
  8.6 1.3 %collective-permute-done.3.refs_1_ = bf16[24,1152]{1,0:T(8,128)(2,1)S(1)} collective-permute-done((bf16[24,1152]{1,0:T(8,128)(2,1)S(1)}, bf16[24,1152]{1,0:T(8,128)(2,1)S(1)}, u32[]{:S(2)}, u32[]{:S(2)}) %collective-permute-start.3) | collective-permute-done | bytes 55328 | tf_op jit(solution)/shard_map/ppermute | solution.py:59
  9.9 3.5 %shard_map.86 = (bf16[64,1152]{1,0:T(8,128)(2,1)S(1)}, bf16[128,64]{1,0:T(8,128)(2,1)S(1)}, bf16[3072,384]{1,0:T(8,128)(2,1)}) custom-call(s32[5]{0:T(128)S(1)} %stack.144.where_ref, s32[1,1536]{1,0:T(1,128)} %own_ids.3, s32[1,1536]{1,0:T(1,128)S(1)} %collective-permute-done.1.other_ids, bf16[24,1152]{1,0:T(8,128)(2,1)S(1)} %collective-permute-done.2.refs_0_, ...), custom_call_target="tpu_custom_call" | custom-call | flops 1024 | bytes 1024 | tf_op jit(solution)/shard_map/pallas_call | solution.py:245
  13.7 5.4 %collective-permute-start.7 = (bf16[64,1152]{1,0:T(8,128)(2,1)S(1)}, bf16[64,1152]{1,0:T(8,128)(2,1)S(1)}, u32[]{:S(2)}, u32[]{:S(2)}) collective-permute-start(bf16[64,1152]{1,0:T(8,128)(2,1)S(1)} %get-tuple-element.249.refs_0_), channel_id=1, source_target_pairs={{0,6},{1,7},{2,0},{3,1},{4,2},{5,3},{6,4},{7,5},{8,14},{9,15},{10,... | collective-permute-start | bytes 442376 | tf_op jit(solution)/shard_map/ppermute | solution.py:59
  20.0 2.4 %collective-permute-start.9 = (bf16[64,1152]{1,0:T(8,128)(2,1)S(1)}, bf16[64,1152]{1,0:T(8,128)(2,1)S(1)}, u32[]{:S(2)}, u32[]{:S(2)}) collective-permute-start(bf16[64,1152]{1,0:T(8,128)(2,1)S(1)} %get-tuple-element.249.refs_0_), channel_id=1, source_target_pairs={{0,2},{1,3},{2,4},{3,5},{4,6},{5,7},{6,0},{7,1},{8,10},{9,11},{10,... | collective-permute-start | bytes 442376 | tf_op jit(solution)/shard_map/ppermute | solution.py:59
  22.5 1.1 %collective-permute-done.7.refs_1_ = bf16[64,1152]{1,0:T(8,128)(2,1)S(1)} collective-permute-done((bf16[64,1152]{1,0:T(8,128)(2,1)S(1)}, bf16[64,1152]{1,0:T(8,128)(2,1)S(1)}, u32[]{:S(2)}, u32[]{:S(2)}) %collective-permute-start.7) | collective-permute-done | bytes 147488 | tf_op jit(solution)/shard_map/ppermute | solution.py:59
  23.6 7.5 %collective-permute-done.8.refs_2_ = bf16[64,1152]{1,0:T(8,128)(2,1)S(1)} collective-permute-done((bf16[64,1152]{1,0:T(8,128)(2,1)S(1)}, bf16[64,1152]{1,0:T(8,128)(2,1)S(1)}, u32[]{:S(2)}, u32[]{:S(2)}) %collective-permute-start.8) | collective-permute-done | bytes 147488 | tf_op jit(solution)/shard_map/ppermute | solution.py:59
  31.4 1.9 %shard_map.87 = (bf16[224,640]{1,0:T(8,128)(2,1)S(1)}, bf16[224,640]{1,0:T(8,128)(2,1)S(1)}, bf16[224,640]{1,0:T(8,128)(2,1)}, bf16[224,640]{1,0:T(8,128)(2,1)}) custom-call(s32[2]{0:T(128)S(1)} %pad_add_fusion.5.where_ref, bf16[128,64]{1,0:T(8,128)(2,1)S(1)} %get-tuple-element.248.route, bf16[64,1152]{1,0:T(8,128)(2,1)S(1)} %get-tuple-element.249.refs_0_, ...), custom_call_target="tpu_custom_call" | custom-call | flops 1024 | bytes 1024 | tf_op jit(solution)/shard_map/pallas_call | solution.py:279
  34.0 1.4 %collective-permute-start.10 = (bf16[224,640]{1,0:T(8,128)(2,1)}, bf16[224,640]{1,0:T(8,128)(2,1)S(1)}, u32[]{:S(2)}, u32[]{:S(2)}) collective-permute-start(bf16[224,640]{1,0:T(8,128)(2,1)} %get-tuple-element.255), channel_id=1, source_target_pairs={{0,24},{1,97},{2,26},{3,99},{4,28},{5,101},{6,30},{7,103},{8,0},{9... | collective-permute-start | bytes 860168 | tf_op jit(solution)/shard_map/ppermute | solution.py:59
  35.4 1.3 %collective-permute-start.11 = (bf16[224,640]{1,0:T(8,128)(2,1)}, bf16[224,640]{1,0:T(8,128)(2,1)S(1)}, u32[]{:S(2)}, u32[]{:S(2)}) collective-permute-start(bf16[224,640]{1,0:T(8,128)(2,1)} %get-tuple-element.256), channel_id=1, source_target_pairs={{0,16},{1,65},{2,18},{3,67},{4,20},{5,69},{6,22},{7,71},{8,24},{9,... | collective-permute-start | bytes 860168 | tf_op jit(solution)/shard_map/ppermute | solution.py:59
  37.6 4.1 %collective-permute-done.6.refs_1_ = bf16[3072,384]{1,0:T(8,128)(2,1)S(1)} collective-permute-done((bf16[3072,384]{1,0:T(8,128)(2,1)}, bf16[3072,384]{1,0:T(8,128)(2,1)S(1)}, u32[]{:S(2)}, u32[]{:S(2)}) %collective-permute-start.6) | collective-permute-done | bytes 2359328 | tf_op jit(solution)/shard_map/ppermute | solution.py:59
  41.7 4.8 %shard_map.88 = (bf16[448,768]{1,0:T(8,128)(2,1)S(1)}, bf16[448,768]{1,0:T(8,128)(2,1)S(1)}, bf16[448,768]{1,0:T(8,128)(2,1)S(1)}, bf16[448,768]{1,0:T(8,128)(2,...) custom-call(s32[20]{0:T(128)S(1)} %stack.137.where_ref, ...), custom_call_target="tpu_custom_call" | custom-call | flops 1024 | bytes 1024 | tf_op jit(solution)/shard_map/pallas_call | solution.py:402
  48.3 1.4 %shard_map.91 = (bf16[448,640]{1,0:T(8,128)(2,1)}, bf16[448,640]{1,0:T(8,128)(2,1)S(1)}) custom-call(bf16[448,640]{1,0:T(8,128)(2,1)S(1)} %shard_map.90._.refs_1_, bf16[448,640]{1,0:T(8,128)(2,1)S(1)} %shard_map.89.refs_0_, bf16[448,640]{1,0:T(8,128)(2,1)S(1)} %shard_map.90._.refs_1_), custom_call_target="tpu_custom_call" | custom-call | flops 1024 | bytes 1024 | tf_op jit(solution)/shard_map/pallas_call | solution.py:318
  49.8 1.8 %collective-permute-start.14 = (bf16[448,640]{1,0:T(8,128)(2,1)S(1)}, bf16[448,640]{1,0:T(8,128)(2,1)}, u32[]{:S(2)}, u32[]{:S(2)}) collective-permute-start(bf16[448,640]{1,0:T(8,128)(2,1)S(1)} %shard_map.90._.refs_1_), channel_id=1, source_target_pairs={{0,96},{1,25},{2,98},{3,27},{4,100},{5,29},{6,102},{7,31},{8,104},... | collective-permute-start | bytes 1720328 | tf_op jit(solution)/shard_map/ppermute | solution.py:59
  52.8 1.1 %collective-permute-start.15 = (bf16[448,640]{1,0:T(8,128)(2,1)S(1)}, bf16[448,640]{1,0:T(8,128)(2,1)}, u32[]{:S(2)}, u32[]{:S(2)}) collective-permute-start(bf16[448,640]{1,0:T(8,128)(2,1)S(1)} %get-tuple-element.261), channel_id=1, source_target_pairs={{0,32},{1,9},{2,34},{3,11},{4,36},{5,13},{6,38},{7,15},{8,40},{9,1... | collective-permute-start | bytes 1720328 | tf_op jit(solution)/shard_map/ppermute | solution.py:59
  53.9 1.4 %conditional.1 = (f32[768,640]{1,0:T(8,128)}) conditional(s32[]{:T(128)} %convert_element_type.46, () %tuple.35, (s32[]{:T(128)}, bf16[24,1152]{1,0:T(8,128)(2,1)S(1)}, bf16[24,1152]{1,0:T(8,128)(2,1)S(1)}, bf16[24,1152]{1,0:T(8,128)(2,1)S(1)}, bf16[24,1152]{1,0:T(8,128)(2,1)S(1)}, /*index=5*/s32[1,1536]{1,0:T(1,128)S(1)}, s32[1,1536]{1,0:T(1,128)S(1)}, ...), branch_computations={%region_0.1_spmd, %region_1.4_spmd} | conditional | flops 48485392 | bytes 5246637 | solution.py:492
  53.9 1.4 %broadcast.28 = f32[768,640]{1,0:T(8,128)} broadcast(f32[]{:T(128)} %constant.84.clone), dimensions={} | broadcast | bytes 1966084 | tf_op jit(solution)/shard_map/broadcast.5
  58.9 2.8 %collective-permute-start.18 = (bf16[448,640]{1,0:T(8,128)(2,1)}, bf16[448,640]{1,0:T(8,128)(2,1)S(1)}, u32[]{:S(2)}, u32[]{:S(2)}) collective-permute-start(bf16[448,640]{1,0:T(8,128)(2,1)} %collective-permute-done.14), channel_id=1, source_target_pairs={{0,96},{1,25},{2,98},{3,27},{4,100},{5,29},{6,102},{7,31},{8,104},... | collective-permute-start | bytes 1720328 | tf_op jit(solution)/shard_map/ppermute | solution.py:59
  61.8 1.9 %fusion.12 = f32[768,640]{1,0:T(8,128)S(1)} fusion(bf16[448,768]{1,0:T(8,128)(2,1)S(1)} %copy-done.11, bf16[448,640]{1,0:T(8,128)(2,1)} %collective-permute-done.14), kind=kOutput, calls=%fused_computation.50 | convolution fusion | flops 440401920 | bytes 3227648 | tf_op jit(solution)/shard_map/dot_general | solution.py:422
  63.7 1.9 %fusion.11 = f32[768,640]{1,0:T(8,128)S(1)} fusion(bf16[448,768]{1,0:T(8,128)(2,1)S(1)} %copy-done.9, bf16[448,640]{1,0:T(8,128)(2,1)} %collective-permute-done.13), kind=kOutput, calls=%fused_computation.49 | convolution fusion | flops 440401920 | bytes 3227648 | tf_op jit(solution)/shard_map/dot_general | solution.py:422
  65.6 1.9 %fusion.14 = f32[768,640]{1,0:T(8,128)S(1)} fusion(bf16[448,768]{1,0:T(8,128)(2,1)S(1)} %copy-done.7, bf16[448,640]{1,0:T(8,128)(2,1)} %collective-permute-done.16), kind=kOutput, calls=%fused_computation.52 | convolution fusion | flops 440401920 | bytes 3227648 | tf_op jit(solution)/shard_map/dot_general | solution.py:422
  67.6 1.9 %fusion.13 = f32[768,640]{1,0:T(8,128)S(1)} fusion(bf16[448,768]{1,0:T(8,128)(2,1)S(1)} %copy-done.5, bf16[448,640]{1,0:T(8,128)(2,1)} %collective-permute-done.15), kind=kOutput, calls=%fused_computation.51 | convolution fusion | flops 440401920 | bytes 3227648 | tf_op jit(solution)/shard_map/dot_general | solution.py:422
  71.3 1.3 %add_add_fusion = f32[768,640]{1,0:T(8,128)S(1)} fusion(f32[768,640]{1,0:T(8,128)S(1)} %fusion.15, f32[768,640]{1,0:T(8,128)S(1)} %fusion.14, f32[768,640]{1,0:T(8,128)S(1)} %fusion.13, f32[768,640]{1,0:T(8,128)S(1)} %fusion.12, f32[768,640]{1,0:T(8,128)S(1)} %fusion.11, f32[768,640]{1,0:T(8,128)S(1)} %fusion.10, f32[768,640]{1,0:T(8,128)S(1)} %copy-done.20, ...), kind=kOutput, calls=%fused_computation.11 | convolution fusion | flops 444334080 | bytes 18956288 | tf_op jit(solution)/shard_map/dot_general | solution.py:422
  72.6 1.3 %multiply_convert_fusion = (f16[96,640]{1,0:T(8,128)(2,1)S(1)}, f16[96,640]{1,0:T(8,128)(2,1)S(1)}, f16[96,640]{1,0:T(8,128)(2,1)S(1)}, f16[96,640]{1,0:T(8,128)...) fusion(f32[768,640]{1,0:T(8,128)S(1)} %add_add_fusion, ...), kind=kLoop, calls=%fused_computation.13 | loop fusion | flops 737280 | bytes 2703396 | tf_op jit(solution)/shard_map/convert_element_type | solution.py:519
  73.9 1.7 %collective-permute-start.20 = (f16[96,640]{1,0:T(8,128)(2,1)S(1)}, f16[96,640]{1,0:T(8,128)(2,1)S(1)}, u32[]{:S(2)}, u32[]{:S(2)}) collective-permute-start(f16[96,640]{1,0:T(8,128)(2,1)S(1)} %get-tuple-element.321), channel_id=1, source_target_pairs={{0,8},{1,33},{2,10},{3,35},{4,12},{5,37},{6,14},{7,39},{8,0},{9,41... | collective-permute-start | bytes 368648 | tf_op jit(solution)/shard_map/ppermute | solution.py:59
  77.1 2.5 %collective-permute-start.23 = (f16[96,640]{1,0:T(8,128)(2,1)S(1)}, f16[96,640]{1,0:T(8,128)(2,1)S(1)}, u32[]{:S(2)}, u32[]{:S(2)}) collective-permute-start(f16[96,640]{1,0:T(8,128)(2,1)S(1)} %get-tuple-element.318), channel_id=1, source_target_pairs={{0,136},{1,161},{2,138},{3,163},{4,140},{5,165},{6,142},{7,167},{8... | collective-permute-start | bytes 368648 | tf_op jit(solution)/shard_map/ppermute | solution.py:59
  79.6 5.3 %collective-permute-start.22 = (f16[96,640]{1,0:T(8,128)(2,1)S(1)}, f16[96,640]{1,0:T(8,128)(2,1)S(1)}, u32[]{:S(2)}, u32[]{:S(2)}) collective-permute-start(f16[96,640]{1,0:T(8,128)(2,1)S(1)} %get-tuple-element.319), channel_id=1, source_target_pairs={{0,9},{1,32},{2,11},{3,34},{4,13},{5,36},{6,15},{7,38},{8,1},{9,40... | collective-permute-start | bytes 368648 | tf_op jit(solution)/shard_map/ppermute | solution.py:59
  84.8 2.5 %collective-permute-start.25 = (f16[96,640]{1,0:T(8,128)(2,1)S(1)}, f16[96,640]{1,0:T(8,128)(2,1)S(1)}, u32[]{:S(2)}, u32[]{:S(2)}) collective-permute-start(f16[96,640]{1,0:T(8,128)(2,1)S(1)} %get-tuple-element.316), channel_id=1, source_target_pairs={{0,137},{1,160},{2,139},{3,162},{4,141},{5,164},{6,143},{7,166},{8... | collective-permute-start | bytes 368648 | tf_op jit(solution)/shard_map/ppermute | solution.py:59
  88.0 1.7 %shard_map.92 = (f32[96,2304]{1,0:T(8,128)S(1)}, f32[96,2304]{1,0:T(8,128)S(1)}, f32[96,2304]{1,0:T(8,128)S(1)}) custom-call(s32[1]{0:T(128)} %bitcast.34.where_ref, f32[96,4608]{1,0:T(8,128)} %refs_4_.1, f32[96,4608]{1,0:T(8,128)} %refs_5_.1, f32[96,4608]{1,0:T(8,128)} %refs_6_.1, f32[96,640]{1,0:T(8,128)S(1)} %collective-permute-done.21.refs_3_), custom_call_target="tpu_custom_call" | custom-call | flops 1024 | bytes 1024 | tf_op jit(solution)/shard_map/pallas_call | solution.py:133
  89.7 3.8 %shard_map.93 = (f32[96,4608]{1,0:T(8,128)}, f32[96,4608]{1,0:T(8,128)}, f32[96,4608]{1,0:T(8,128)}, f32[1,1]{1,0:T(1,128)}) custom-call(s32[4]{0:T(128)S(1)} %pad_add_fusion.6.where_ref, f32[1]{0:T(128)} %bitcast.32.held_ref, f32[96,640]{1,0:T(8,128)S(1)} %get-tuple-element.332.refs_0_, f32[96,512]{1,0:T(8,128)S(1)} %dynamic-slice_select_fusion.1.refs_1_, ...), custom_call_target="tpu_custom_call" | custom-call | flops 1024 | bytes 1024 | tf_op jit(solution)/shard_map/pallas_call | solution.py:106
  95.9 2.7 %shard_map.94 = (f32[96,4608]{1,0:T(8,128)}, f32[96,4608]{1,0:T(8,128)}, f32[96,4608]{1,0:T(8,128)}, f32[1,1]{1,0:T(1,128)}) custom-call(s32[4]{0:T(128)S(1)} %pad_add_fusion.2.where_ref, f32[1]{0:T(128)S(6)} %div.10.held_ref, f32[96,640]{1,0:T(8,128)S(1)} %get-tuple-element.327.refs_0_, ...), custom_call_target="tpu_custom_call", output_to_operand_aliasing={{0}: (9, {}), {1}: (10, {}), {2}: (11, {})} | custom-call | flops 1024 | bytes 1024 | tf_op jit(solution)/shard_map/pallas_call | solution.py:106
  (113 shorter events, 17.5 us)
Async XLA Ops:
  0.6 41.1 %copy-start.27 = (s32[1,1536]{1,0:T(1,128)S(1)}, s32[1,1536]{1,0:T(1,128)}, u32[]{:S(2)}) copy-start(s32[1,1536]{1,0:T(1,128)} %own_ids.3) | copy-start | bytes 18436
  0.6 9.3 %collective-permute-start.5 = (bf16[1536,384]{1,0:T(8,128)(2,1)}, bf16[1536,384]{1,0:T(8,128)(2,1)S(1)}, u32[]{:S(2)}, u32[]{:S(2)}) collective-permute-start(bf16[1536,384]{1,0:T(8,128)(2,1)} %bitcast.54), channel_id=1, source_target_pairs={{0,1},{1,0},{2,3},{3,2},{4,5},{5,4},{6,7},{7,6},{8,9},{9,8},{10,11... | collective-permute-start | bytes 3538952 | tf_op jit(solution)/shard_map/ppermute | solution.py:59
  5.0 8.4 %copy-start.18 = (bf16[24,1152]{1,0:T(8,128)(2,1)}, bf16[24,1152]{1,0:T(8,128)(2,1)S(1)}, u32[]{:S(2)}) copy-start(bf16[24,1152]{1,0:T(8,128)(2,1)S(1)} %get-tuple-element.246.refs_3_) | copy-start | bytes 165892
  5.0 3.6 %collective-permute-start.2 = (bf16[24,1152]{1,0:T(8,128)(2,1)S(1)}, bf16[24,1152]{1,0:T(8,128)(2,1)S(1)}, u32[]{:S(2)}, u32[]{:S(2)}) collective-permute-start(bf16[24,1152]{1,0:T(8,128)(2,1)S(1)} %get-tuple-element.243), channel_id=1, source_target_pairs={{0,128},{1,129},{2,130},{3,131},{4,132},{5,133},{6,134},{7,135},{8... | collective-permute-start | bytes 165896 | tf_op jit(solution)/shard_map/ppermute | solution.py:59
  5.1 4.8 %collective-permute-start.3 = (bf16[24,1152]{1,0:T(8,128)(2,1)S(1)}, bf16[24,1152]{1,0:T(8,128)(2,1)S(1)}, u32[]{:S(2)}, u32[]{:S(2)}) collective-permute-start(bf16[24,1152]{1,0:T(8,128)(2,1)S(1)} %get-tuple-element.244), channel_id=1, source_target_pairs={{0,129},{1,128},{2,131},{3,130},{4,133},{5,132},{6,135},{7,134},{8... | collective-permute-start | bytes 165896 | tf_op jit(solution)/shard_map/ppermute | solution.py:59
  6.8 3.1 %collective-permute-start.4 = (bf16[24,1152]{1,0:T(8,128)(2,1)S(1)}, bf16[24,1152]{1,0:T(8,128)(2,1)S(1)}, u32[]{:S(2)}, u32[]{:S(2)}) collective-permute-start(bf16[24,1152]{1,0:T(8,128)(2,1)S(1)} %get-tuple-element.245), channel_id=1, source_target_pairs={{0,1},{1,0},{2,3},{3,2},{4,5},{5,4},{6,7},{7,6},{8,9},{9,8},{10,11... | collective-permute-start | bytes 165896 | tf_op jit(solution)/shard_map/ppermute | solution.py:59
  7.0 1.2 %collective-permute-start.1 = (s32[1,1536]{1,0:T(1,128)S(1)}, s32[1,1536]{1,0:T(1,128)S(1)}, u32[]{:S(2)}, u32[]{:S(2)}) collective-permute-start(s32[1,1536]{1,0:T(1,128)S(1)} %get-tuple-element.242), channel_id=1, source_target_pairs={{0,1},{1,0},{2,3},{3,2},{4,5},{5,4},{6,7},{7,6},{8,9},{9,8},{10,11... | collective-permute-start | bytes 18440 | tf_op jit(solution)/shard_map/ppermute | solution.py:59
  13.4 28.3 %collective-permute-start.6 = (bf16[3072,384]{1,0:T(8,128)(2,1)}, bf16[3072,384]{1,0:T(8,128)(2,1)S(1)}, u32[]{:S(2)}, u32[]{:S(2)}) collective-permute-start(bf16[3072,384]{1,0:T(8,128)(2,1)} %get-tuple-element.247.refs_0_), channel_id=1, source_target_pairs={{0,8},{1,33},{2,10},{3,35},{4,12},{5,37},{6,14},{7,39},{8,0},{9,41... | collective-permute-start | bytes 7077896 | tf_op jit(solution)/shard_map/ppermute | solution.py:59
  13.7 9.8 %collective-permute-start.7 = (bf16[64,1152]{1,0:T(8,128)(2,1)S(1)}, bf16[64,1152]{1,0:T(8,128)(2,1)S(1)}, u32[]{:S(2)}, u32[]{:S(2)}) collective-permute-start(bf16[64,1152]{1,0:T(8,128)(2,1)S(1)} %get-tuple-element.249.refs_0_), channel_id=1, source_target_pairs={{0,6},{1,7},{2,0},{3,1},{4,2},{5,3},{6,4},{7,5},{8,14},{9,15},{10,... | collective-permute-start | bytes 442376 | tf_op jit(solution)/shard_map/ppermute | solution.py:59
  19.2 11.9 %collective-permute-start.8 = (bf16[64,1152]{1,0:T(8,128)(2,1)S(1)}, bf16[64,1152]{1,0:T(8,128)(2,1)S(1)}, u32[]{:S(2)}, u32[]{:S(2)}) collective-permute-start(bf16[64,1152]{1,0:T(8,128)(2,1)S(1)} %get-tuple-element.249.refs_0_), channel_id=1, source_target_pairs={{0,4},{1,5},{2,6},{3,7},{4,0},{5,1},{6,2},{7,3},{8,12},{9,13},{10,... | collective-permute-start | bytes 442376 | tf_op jit(solution)/shard_map/ppermute | solution.py:59
  20.0 11.3 %collective-permute-start.9 = (bf16[64,1152]{1,0:T(8,128)(2,1)S(1)}, bf16[64,1152]{1,0:T(8,128)(2,1)S(1)}, u32[]{:S(2)}, u32[]{:S(2)}) collective-permute-start(bf16[64,1152]{1,0:T(8,128)(2,1)S(1)} %get-tuple-element.249.refs_0_), channel_id=1, source_target_pairs={{0,2},{1,3},{2,4},{3,5},{4,6},{5,7},{6,0},{7,1},{8,10},{9,11},{10,... | collective-permute-start | bytes 442376 | tf_op jit(solution)/shard_map/ppermute | solution.py:59
  34.0 13.5 %collective-permute-start.10 = (bf16[224,640]{1,0:T(8,128)(2,1)}, bf16[224,640]{1,0:T(8,128)(2,1)S(1)}, u32[]{:S(2)}, u32[]{:S(2)}) collective-permute-start(bf16[224,640]{1,0:T(8,128)(2,1)} %get-tuple-element.255), channel_id=1, source_target_pairs={{0,24},{1,97},{2,26},{3,99},{4,28},{5,101},{6,30},{7,103},{8,0},{9... | collective-permute-start | bytes 860168 | tf_op jit(solution)/shard_map/ppermute | solution.py:59
  35.4 12.1 %collective-permute-start.11 = (bf16[224,640]{1,0:T(8,128)(2,1)}, bf16[224,640]{1,0:T(8,128)(2,1)S(1)}, u32[]{:S(2)}, u32[]{:S(2)}) collective-permute-start(bf16[224,640]{1,0:T(8,128)(2,1)} %get-tuple-element.256), channel_id=1, source_target_pairs={{0,16},{1,65},{2,18},{3,67},{4,20},{5,69},{6,22},{7,71},{8,24},{9,... | collective-permute-start | bytes 860168 | tf_op jit(solution)/shard_map/ppermute | solution.py:59
  36.6 10.8 %collective-permute-start.12 = (bf16[224,640]{1,0:T(8,128)(2,1)S(1)}, bf16[224,640]{1,0:T(8,128)(2,1)S(1)}, u32[]{:S(2)}, u32[]{:S(2)}) collective-permute-start(bf16[224,640]{1,0:T(8,128)(2,1)S(1)} %get-tuple-element.250.refs_2_), channel_id=1, source_target_pairs={{0,8},{1,33},{2,10},{3,35},{4,12},{5,37},{6,14},{7,39},{8,16},{9,4... | collective-permute-start | bytes 860168 | tf_op jit(solution)/shard_map/ppermute | solution.py:59
  37.6 10.0 %copy-start.17 = (bf16[224,640]{1,0:T(8,128)(2,1)S(1)}, bf16[224,640]{1,0:T(8,128)(2,1)}, u32[]{:S(2)}) copy-start(bf16[224,640]{1,0:T(8,128)(2,1)} %copy-done.16) | copy-start | bytes 860164
  47.5 5.2 %copy-start.19 = (bf16[24,1152]{1,0:T(8,128)(2,1)S(1)}, bf16[24,1152]{1,0:T(8,128)(2,1)}, u32[]{:S(2)}) copy-start(bf16[24,1152]{1,0:T(8,128)(2,1)} %copy-done.18) | copy-start | bytes 165892
  47.5 5.2 %copy-start.22 = (bf16[24,1152]{1,0:T(8,128)(2,1)S(1)}, bf16[24,1152]{1,0:T(8,128)(2,1)}, u32[]{:S(2)}) copy-start(bf16[24,1152]{1,0:T(8,128)(2,1)} %copy-done.21) | copy-start | bytes 165892
  47.6 10.2 %collective-permute-start.13 = (bf16[448,640]{1,0:T(8,128)(2,1)S(1)}, bf16[448,640]{1,0:T(8,128)(2,1)}, u32[]{:S(2)}, u32[]{:S(2)}) collective-permute-start(bf16[448,640]{1,0:T(8,128)(2,1)S(1)} %shard_map.89.refs_0_), channel_id=1, source_target_pairs={{0,32},{1,9},{2,34},{3,11},{4,36},{5,13},{6,38},{7,15},{8,40},{9,1... | collective-permute-start | bytes 1720328 | tf_op jit(solution)/shard_map/ppermute | solution.py:59
  49.8 9.1 %collective-permute-start.14 = (bf16[448,640]{1,0:T(8,128)(2,1)S(1)}, bf16[448,640]{1,0:T(8,128)(2,1)}, u32[]{:S(2)}, u32[]{:S(2)}) collective-permute-start(bf16[448,640]{1,0:T(8,128)(2,1)S(1)} %shard_map.90._.refs_1_), channel_id=1, source_target_pairs={{0,96},{1,25},{2,98},{3,27},{4,100},{5,29},{6,102},{7,31},{8,104},... | collective-permute-start | bytes 1720328 | tf_op jit(solution)/shard_map/ppermute | solution.py:59
  52.3 13.3 %collective-permute-start.16 = (bf16[448,640]{1,0:T(8,128)(2,1)}, bf16[448,640]{1,0:T(8,128)(2,1)}, u32[]{:S(2)}, u32[]{:S(2)}) collective-permute-start(bf16[448,640]{1,0:T(8,128)(2,1)} %get-tuple-element.263), channel_id=1, source_target_pairs={{0,96},{1,25},{2,98},{3,27},{4,100},{5,29},{6,102},{7,31},{8,104},... | collective-permute-start | bytes 1720328 | tf_op jit(solution)/shard_map/ppermute | solution.py:59
  52.8 14.8 %collective-permute-start.15 = (bf16[448,640]{1,0:T(8,128)(2,1)S(1)}, bf16[448,640]{1,0:T(8,128)(2,1)}, u32[]{:S(2)}, u32[]{:S(2)}) collective-permute-start(bf16[448,640]{1,0:T(8,128)(2,1)S(1)} %get-tuple-element.261), channel_id=1, source_target_pairs={{0,32},{1,9},{2,34},{3,11},{4,36},{5,13},{6,38},{7,15},{8,40},{9,1... | collective-permute-start | bytes 1720328 | tf_op jit(solution)/shard_map/ppermute | solution.py:59
  56.1 5.6 %copy-start.11 = (bf16[448,768]{1,0:T(8,128)(2,1)S(1)}, bf16[448,768]{1,0:T(8,128)(2,1)}, u32[]{:S(2)}) copy-start(bf16[448,768]{1,0:T(8,128)(2,1)} %copy-done.10) | copy-start | bytes 2064388
  57.2 6.5 %copy-start.9 = (bf16[448,768]{1,0:T(8,128)(2,1)S(1)}, bf16[448,768]{1,0:T(8,128)(2,1)}, u32[]{:S(2)}) copy-start(bf16[448,768]{1,0:T(8,128)(2,1)} %copy-done.8) | copy-start | bytes 2064388
  57.9 12.2 %collective-permute-start.17 = (bf16[448,640]{1,0:T(8,128)(2,1)}, bf16[448,640]{1,0:T(8,128)(2,1)S(1)}, u32[]{:S(2)}, u32[]{:S(2)}) collective-permute-start(bf16[448,640]{1,0:T(8,128)(2,1)} %collective-permute-done.13), channel_id=1, source_target_pairs={{0,32},{1,9},{2,34},{3,11},{4,36},{5,13},{6,38},{7,15},{8,40},{9,1... | collective-permute-start | bytes 1720328 | tf_op jit(solution)/shard_map/ppermute | solution.py:59
  58.9 12.2 %collective-permute-start.18 = (bf16[448,640]{1,0:T(8,128)(2,1)}, bf16[448,640]{1,0:T(8,128)(2,1)S(1)}, u32[]{:S(2)}, u32[]{:S(2)}) collective-permute-start(bf16[448,640]{1,0:T(8,128)(2,1)} %collective-permute-done.14), channel_id=1, source_target_pairs={{0,96},{1,25},{2,98},{3,27},{4,100},{5,29},{6,102},{7,31},{8,104},... | collective-permute-start | bytes 1720328 | tf_op jit(solution)/shard_map/ppermute | solution.py:59
  73.9 10.9 %collective-permute-start.20 = (f16[96,640]{1,0:T(8,128)(2,1)S(1)}, f16[96,640]{1,0:T(8,128)(2,1)S(1)}, u32[]{:S(2)}, u32[]{:S(2)}) collective-permute-start(f16[96,640]{1,0:T(8,128)(2,1)S(1)} %get-tuple-element.321), channel_id=1, source_target_pairs={{0,8},{1,33},{2,10},{3,35},{4,12},{5,37},{6,14},{7,39},{8,0},{9,41... | collective-permute-start | bytes 368648 | tf_op jit(solution)/shard_map/ppermute | solution.py:59
  77.1 16.4 %collective-permute-start.23 = (f16[96,640]{1,0:T(8,128)(2,1)S(1)}, f16[96,640]{1,0:T(8,128)(2,1)S(1)}, u32[]{:S(2)}, u32[]{:S(2)}) collective-permute-start(f16[96,640]{1,0:T(8,128)(2,1)S(1)} %get-tuple-element.318), channel_id=1, source_target_pairs={{0,136},{1,161},{2,138},{3,163},{4,140},{5,165},{6,142},{7,167},{8... | collective-permute-start | bytes 368648 | tf_op jit(solution)/shard_map/ppermute | solution.py:59
  79.6 8.4 %collective-permute-start.22 = (f16[96,640]{1,0:T(8,128)(2,1)S(1)}, f16[96,640]{1,0:T(8,128)(2,1)S(1)}, u32[]{:S(2)}, u32[]{:S(2)}) collective-permute-start(f16[96,640]{1,0:T(8,128)(2,1)S(1)} %get-tuple-element.319), channel_id=1, source_target_pairs={{0,9},{1,32},{2,11},{3,34},{4,13},{5,36},{6,15},{7,38},{8,1},{9,40... | collective-permute-start | bytes 368648 | tf_op jit(solution)/shard_map/ppermute | solution.py:59
  84.8 3.1 %collective-permute-start.21 = (f32[96,640]{1,0:T(8,128)S(1)}, f32[96,640]{1,0:T(8,128)S(1)}, u32[]{:S(2)}, u32[]{:S(2)}) collective-permute-start(f32[96,640]{1,0:T(8,128)S(1)} %get-tuple-element.320), channel_id=1, source_target_pairs={{0,1},{1,0},{2,3},{3,2},{4,5},{5,4},{6,7},{7,6},{8,9},{9,8},{10,11... | collective-permute-start | bytes 737288 | tf_op jit(solution)/shard_map/ppermute | solution.py:59
  84.8 8.7 %collective-permute-start.19 = (f16[96,640]{1,0:T(8,128)(2,1)S(1)}, f16[96,640]{1,0:T(8,128)(2,1)S(1)}, u32[]{:S(2)}, u32[]{:S(2)}) collective-permute-start(f16[96,640]{1,0:T(8,128)(2,1)S(1)} %get-tuple-element.322), channel_id=1, source_target_pairs={{0,128},{1,129},{2,130},{3,131},{4,132},{5,133},{6,134},{7,135},{8... | collective-permute-start | bytes 368648 | tf_op jit(solution)/shard_map/ppermute | solution.py:59
  84.8 9.5 %collective-permute-start.25 = (f16[96,640]{1,0:T(8,128)(2,1)S(1)}, f16[96,640]{1,0:T(8,128)(2,1)S(1)}, u32[]{:S(2)}, u32[]{:S(2)}) collective-permute-start(f16[96,640]{1,0:T(8,128)(2,1)S(1)} %get-tuple-element.316), channel_id=1, source_target_pairs={{0,137},{1,160},{2,139},{3,162},{4,141},{5,164},{6,143},{7,166},{8... | collective-permute-start | bytes 368648 | tf_op jit(solution)/shard_map/ppermute | solution.py:59
  87.9 7.2 %collective-permute-start.24 = (f16[96,640]{1,0:T(8,128)(2,1)S(1)}, f16[96,640]{1,0:T(8,128)(2,1)S(1)}, u32[]{:S(2)}, u32[]{:S(2)}) collective-permute-start(f16[96,640]{1,0:T(8,128)(2,1)S(1)} %get-tuple-element.317), channel_id=1, source_target_pairs={{0,129},{1,128},{2,131},{3,130},{4,133},{5,132},{6,135},{7,134},{8... | collective-permute-start | bytes 368648 | tf_op jit(solution)/shard_map/ppermute | solution.py:59
  (21 other events, 53.2 us)
